TPU v7x, 128 devices: a whole 4x4x4 slice. The times are simulated.
128 devices in a mesh: seq: 32 (over y, z, core), ch: 4 (over x).
Axes of the slice: x: 4, y: 4, z: 4, core: 2. Of those that a mesh axis runs over, the one named last changes fastest.
Arguments:
- query_gate: bfloat16 [16384, 8192], P('seq', 'ch'), may hold values from -100 to 100
- key_branch: bfloat16 [16384, 8192], P('seq', 'ch'), may hold values from -6 to 6
- value_branch: bfloat16 [16384, 8192], P('seq', 'ch'), may hold values from -6 to 6
- norm_gain: float32 [8192], P('ch'), may hold values from 0.5 to 1.5
- residues: float32 [512, 16], P('ch'), may hold values from -4 to 4
- decay_rate: float32 [512, 16], P('ch'), may hold values from 3.0517578e-06 to 0.0333333333
- doc_lengths: int32 [16], replicated, may hold values from 1 to 4096, 16384 in all
- cotangent: bfloat16 [16384, 8192], P('seq', 'ch'), may hold values from -6 to 6
Outputs:
- layer_out: bfloat16 [16384, 8192], P('seq', 'ch')
- grad_query: bfloat16 [16384, 8192], P('seq', 'ch')
- grad_key: bfloat16 [16384, 8192], P('seq', 'ch')
- grad_value: bfloat16 [16384, 8192], P('seq', 'ch')
All inputs are finite; a program needn't handle non-finite values.
Results may differ from a plain program's by a relative error of at most 0.005.
Values may be sent and summed in bfloat16 or wider, within the bound.
No kernel may reach another device: no remote copies, remote signals or barrier semaphores. Data moves between devices by JAX's collectives and lax.ppermute only.
A program may use at most 192 MiB of HBM per device.

v0:
```python
import jax
import jax.numpy as jnp
from jax import lax
from jax.experimental import pallas as pl
from jax.experimental.pallas import tpu as pltpu
from jax.sharding import PartitionSpec as P

C = 64
W = 128
LB = 256
G = 16
R = 16
NG = W // G
REACH = 4096
EPS = 1e-6
f32, bf16 = jnp.float32, jnp.bfloat16
VLIM = 48 * 1024 * 1024


def doc_index(places, doc_lengths):
    doc_ends = jnp.cumsum(doc_lengths)
    doc_starts = doc_ends - doc_lengths
    before_here = (doc_starts[None, :] <= places[:, None]).astype(jnp.int32)
    return jnp.sum(before_here, axis=1) - 1


def dot(a, b):
    return jnp.dot(a, b, preferred_element_type=f32)


def lane_group(rows):
    return lax.broadcasted_iota(jnp.int32, (rows, W), 1) // G


def swap_blocks(parts):
    parts = list(parts)
    blk = lane_group(parts[0].shape[0])
    bit = 1
    while bit < NG:
        low = (blk & bit) == 0
        for m in range(NG):
            if not m & bit:
                a, b = parts[m], parts[m | bit]
                parts[m] = jnp.where(low, a, pltpu.roll(b, G * bit, 1))
                parts[m | bit] = jnp.where(low, pltpu.roll(a, W - G * bit, 1), b)
        bit *= 2
    return parts


def chunk_states(x, mask, et, decay, join_ref, order, emit):
    blk = lane_group(R)
    xm = x * mask
    state = jnp.zeros((R, W), f32)
    for m in order:
        emit(m, state)
        rows = xm[m * C : (m + 1) * C]
        full = dot(et, jnp.concatenate([rows, rows], axis=0))
        own = full[0:R]
        for g in range(1, NG):
            own = jnp.where(blk == g, full[g * R : (g + 1) * R], own)
        state = own + join_ref[0, m] * (decay * state)
    return state


def carried(entries, lag):
    rows = NG * R
    diag = (lax.broadcasted_iota(jnp.int32, (rows, W), 0) // R) == lane_group(rows)
    lag2 = jnp.concatenate([lag, lag], axis=1)
    out = []
    for e in entries:
        spread = jnp.where(diag, jnp.concatenate([e] * NG, axis=0), 0.0)
        hi = spread.astype(bf16)
        lo = (spread - hi.astype(f32)).astype(bf16)
        out.append(dot(lag2, jnp.concatenate([hi, lo], axis=0)))
    return out


def first_kernel(join_ref, k_ref, v_ref, mask_ref, et_ref, dc_ref, prod_ref, ent_ref, own_ref):
    chunks = k_ref.shape[0] // C
    for s in range(LB // W):
        at = slice(s * W, (s + 1) * W)
        x = (k_ref[:, at].astype(f32) * v_ref[:, at].astype(f32)).astype(bf16)
        prod_ref[:, at] = x

        def emit(m, state):
            ent_ref[m, :, at] = state

        end = chunk_states(x, mask_ref[...], et_ref[s * W : (s + 1) * W, :], dc_ref[:, at], join_ref, range(chunks), emit)
        own_ref[:, at] = end.astype(bf16)


def toeplitz_kernel(top_ref, x_ref, seg_ref, tap_ref, y_ref, z_ref, o_ref):
    seg = seg_ref[...]
    for s in range(LB // W):
        at = slice(s * W, (s + 1) * W)
        z = swap_blocks([x_ref[m * C : (m + 1) * C, at].astype(f32) for m in range(NG)])

        def matrix(g):
            taps = jnp.broadcast_to(tap_ref[s * NG + g : s * NG + g + 1, :], (C, W))
            return pltpu.roll(taps, 0, 1, stride=1, stride_axis=0)[:, :C].astype(bf16)

        for g in range(NG):
            z0 = jnp.where(seg == 0, z[g], 0.0).astype(bf16)
            z1 = jnp.where(seg == 1, z[g], 0.0).astype(bf16)
            y2 = dot(matrix(g), jnp.concatenate([z0, z1], axis=1))
            z_ref[g] = z[g]
            o_ref[g] = jnp.where(seg == 0, y2[:, :W], y2[:, W:])

        @pl.when(top_ref[0, 0] > 1)
        def _():
            def again(p, carry):
                for g in range(NG):
                    zp = jnp.where(seg == p, z_ref[g], 0.0).astype(bf16)
                    o_ref[g] = jnp.where(seg == p, dot(matrix(g), zp), o_ref[g])
                return carry

            lax.fori_loop(2, top_ref[0, 0] + 1, again, 0)

        y = swap_blocks([o_ref[g] for g in range(NG)])
        for m in range(NG):
            y_ref[m * C : (m + 1) * C, at] = y[m]


def entry_states(got, keep_ref, far, decay, join_ref, ent_ref, at, order):
    total = jnp.zeros((R, W), f32)
    for n in reversed(range(len(got))):
        total = keep_ref[0, n] * got[n][:, at].astype(f32) + far * total
    entries = []
    for m in order:
        entries.append(ent_ref[m, :, at] + total)
        total = join_ref[0, m] * (decay * total)
    return entries


def gate_kernel(join_ref, keep_ref, *refs):
    got, refs = refs[:8], refs[8:]
    y_ref, ent_ref, q_ref, c_ref, gain_ref, lag_ref, dc_ref, far_ref, same_ref, conv_ref, stat_ref, acc_ref = refs
    chunks = y_ref.shape[0] // C
    step = pl.program_id(0)

    @pl.when(step == 0)
    def _():
        acc_ref[...] = jnp.zeros_like(acc_ref)

    for s in range(LB // W):
        at = slice(s * W, (s + 1) * W)
        entries = entry_states(got, keep_ref, far_ref[:, at], dc_ref[:, at], join_ref, ent_ref, at, range(chunks))
        parts = carried(entries, lag_ref[:, at])
        for m in range(chunks):
            rows = slice(m * C, (m + 1) * C)
            conv = y_ref[rows, at] + same_ref[rows, :] * parts[m]
            conv_ref[rows, at] = conv
            gated = q_ref[rows, at].astype(f32) * conv
            acc_ref[rows, :W] += gated * gated
            acc_ref[rows, W:] += c_ref[rows, at].astype(f32) * gain_ref[:, at] * gated

    @pl.when(step == pl.num_programs(0) - 1)
    def _():
        row = lax.broadcasted_iota(jnp.int32, (8, 2 * W), 0)
        lane = lax.broadcasted_iota(jnp.int32, (8, 2 * W), 1)
        pick = (row == lane // W).astype(f32)
        stat_ref[...] = lax.dot_general(
            pick, acc_ref[...], (((1,), (1,)), ((), ())), precision=lax.Precision.HIGHEST, preferred_element_type=f32
        )


def grad_kernel(
    join_ref, conv_ref, q_ref, c_ref, gain_ref, inv_ref, mean_ref, mask_ref, et_ref, dc_ref,
    out_ref, gq_ref, gc_ref, ent_ref, own_ref,
):
    chunks = conv_ref.shape[0] // C
    inv, mean = inv_ref[...], mean_ref[...]
    for s in range(LB // W):
        at = slice(s * W, (s + 1) * W)
        conv = conv_ref[:, at]
        q = q_ref[:, at].astype(f32)
        gain = gain_ref[:, at]
        normed = q * conv * inv
        out_ref[:, at] = (normed * gain).astype(bf16)
        grad_gated = inv * (c_ref[:, at].astype(f32) * gain - normed * mean)
        gq_ref[:, at] = (grad_gated * conv).astype(bf16)
        x = (grad_gated * q).astype(bf16)
        gc_ref[:, at] = x

        def emit(m, state):
            ent_ref[m, :, at] = state

        order = list(reversed(range(chunks)))
        end = chunk_states(x, mask_ref[...], et_ref[s * W : (s + 1) * W, :], dc_ref[:, at], join_ref, order, emit)
        own_ref[:, at] = end.astype(bf16)


def last_kernel(join_ref, keep_ref, *refs):
    got, refs = refs[:8], refs[8:]
    y_ref, ent_ref, k_ref, v_ref, lag_ref, dc_ref, far_ref, same_ref, gk_ref, gv_ref = refs
    chunks = y_ref.shape[0] // C
    for s in range(LB // W):
        at = slice(s * W, (s + 1) * W)
        order = list(reversed(range(chunks)))
        entries = entry_states(got, keep_ref, far_ref[:, at], dc_ref[:, at], join_ref, ent_ref, at, order)
        parts = carried(entries, lag_ref[:, at])
        for n, m in enumerate(order):
            rows = slice(m * C, (m + 1) * C)
            grad = y_ref[rows, at] + same_ref[rows, :] * parts[n]
            gk_ref[rows, at] = (grad * v_ref[rows, at].astype(f32)).astype(bf16)
            gv_ref[rows, at] = (grad * k_ref[rows, at].astype(f32)).astype(bf16)


def split_hi_lo(x):
    hi = x.astype(bf16)
    return hi, (x - hi.astype(f32)).astype(bf16)


def local(query_gate, key_branch, value_branch, norm_gain, residues, decay_rate, doc_lengths, cotangent):
    rows, width = query_gate.shape
    chunks = rows // C
    groups = residues.shape[0]
    devices = lax.axis_size("seq")
    here = lax.axis_index("seq")
    total_width = width * lax.axis_size("ch")
    shifts = range(1, REACH // rows + 1)

    start = here * rows
    docs = doc_index(start - 1 + jnp.arange(rows + 2, dtype=jnp.int32), doc_lengths)
    inner = docs[1:-1].reshape(chunks, C)
    first, last = inner[:, 0], inner[:, -1]
    prior, after = docs[0 : rows : C], docs[C + 1 :: C]
    seg = inner - first[:, None]
    top = jnp.max(seg).reshape(1, 1)
    seg_lanes = jnp.repeat(seg.T, G, axis=1)

    def spread(flags, dtype):
        return jnp.broadcast_to(flags.reshape(rows, 1).astype(dtype), (rows, W))

    last_mask = spread(inner == last[:, None], bf16)
    first_mask = spread(inner == first[:, None], bf16)
    same_prior = spread(inner == prior[:, None], f32)
    same_after = spread(inner == after[:, None], f32)
    join_f = (last == prior).astype(f32).reshape(1, chunks)
    join_b = (first == after).astype(f32).reshape(1, chunks)
    step = jnp.arange(len(shifts), dtype=jnp.int32) + 1
    end_docs = doc_index((here - step + 1) * rows - 1, doc_lengths)
    keep_f = ((end_docs == docs[0]) & (here >= step)).astype(f32).reshape(1, -1)
    begin_docs = doc_index((here + step) * rows, doc_lengths)
    keep_b = ((begin_docs == docs[-1]) & (here + step < devices)).astype(f32).reshape(1, -1)

    flat_rate = decay_rate.reshape(groups * R)
    flat_res = residues.reshape(groups * R)
    place = jnp.arange(C, dtype=f32)
    et_b = jnp.exp(-flat_rate[:, None] * place[None, :])
    et_f = jnp.exp(-flat_rate[:, None] * (C - 1 - place)[None, :])
    et_f = jnp.concatenate(split_hi_lo(et_f), axis=1)
    et_b = jnp.concatenate(split_hi_lo(et_b), axis=1)
    lag_f = (flat_res[None, :] * jnp.exp(-flat_rate[None, :] * (place + 1.0)[:, None])).astype(bf16)
    lag_b = (flat_res[None, :] * jnp.exp(-flat_rate[None, :] * (C - place)[:, None])).astype(bf16)
    lane = jnp.arange(W)
    back = (W - lane) % W

    def taps(lags):
        h = jnp.sum(residues[:, :, None] * jnp.exp(-decay_rate[:, :, None] * lags.astype(f32)), axis=1)
        return jnp.where(lags < C, h, 0.0)

    tap_f, tap_b = taps(back), taps(lane)
    rate_lanes = jnp.repeat(decay_rate.T, G, axis=1)
    decay = jnp.exp(-rate_lanes * C)
    far = jnp.exp(-rate_lanes * rows)
    gain = norm_gain.reshape(1, width)

    grid = (width // LB,)
    wide = pl.BlockSpec((rows, LB), lambda i: (0, i))
    modes = pl.BlockSpec((R, LB), lambda i: (0, i))
    lagged = pl.BlockSpec((C, LB), lambda i: (0, i))
    table = pl.BlockSpec((LB // G * R, 2 * C), lambda i: (i, 0))
    tapped = pl.BlockSpec((LB // G, W), lambda i: (i, 0))
    entry = pl.BlockSpec((chunks, R, LB), lambda i: (0, 0, i))
    row1 = pl.BlockSpec((1, LB), lambda i: (0, i))
    whole = pl.BlockSpec((rows, W), lambda i: (0, 0))
    seg_spec = pl.BlockSpec((C, W), lambda i: (0, 0))
    small = pl.BlockSpec(memory_space=pltpu.SMEM)
    params = pltpu.CompilerParams(vmem_limit_bytes=VLIM, dimension_semantics=("arbitrary",))

    def shaped(dtype, *shape):
        return jax.ShapeDtypeStruct(shape, dtype)

    full16, full32 = shaped(bf16, rows, width), shaped(f32, rows, width)
    entries, ends = shaped(f32, chunks, R, width), shaped(bf16, R, width)

    def send(x, way):
        return [lax.ppermute(x, "seq", [(i, (i + way * n) % devices) for i in range(devices)]) for n in shifts]

    def toeplitz(x, tap):
        return pl.pallas_call(
            toeplitz_kernel, grid=grid, in_specs=[small, wide, seg_spec, tapped], out_specs=wide, out_shape=full32,
            scratch_shapes=[pltpu.VMEM((NG, C, W), f32), pltpu.VMEM((NG, C, W), f32)], compiler_params=params,
            cost_estimate=pl.CostEstimate(flops=2 * rows * width * 512, bytes_accessed=6 * rows * width, transcendentals=0),
        )(top, x, seg_lanes, tap)

    product, ent_f, own_f = pl.pallas_call(
        first_kernel, grid=grid, in_specs=[small, wide, wide, whole, table, modes], out_specs=[wide, entry, modes],
        out_shape=[full16, entries, ends], compiler_params=params,
    )(join_f, key_branch, value_branch, last_mask, et_f, decay)
    got_f = send(own_f, 1)
    y_f = toeplitz(product, tap_f)
    conv, stat = pl.pallas_call(
        gate_kernel, grid=grid,
        in_specs=[small, small] + [modes] * 8 + [wide, entry, wide, wide, row1, lagged, modes, modes, whole],
        out_specs=[wide, pl.BlockSpec((8, rows), lambda i: (0, 0))], out_shape=[full32, shaped(f32, 8, rows)],
        scratch_shapes=[pltpu.VMEM((rows, 2 * W), f32)], compiler_params=params,
    )(join_f, keep_f, *got_f, y_f, ent_f, query_gate, cotangent, gain, lag_f, decay, far, same_prior)
    stat = lax.psum(stat, "ch")
    inv = lax.rsqrt(stat[0] / total_width + EPS)
    mean = inv * stat[1] / total_width
    layer_out, grad_query, grad_conv, ent_b, own_b = pl.pallas_call(
        grad_kernel, grid=grid,
        in_specs=[small, wide, wide, wide, row1, whole, whole, whole, table, modes],
        out_specs=[wide, wide, wide, entry, modes], out_shape=[full16, full16, full16, entries, ends],
        compiler_params=params,
    )(join_b, conv, query_gate, cotangent, gain, spread(inv, f32), spread(mean, f32), first_mask, et_b, decay)
    got_b = send(own_b, -1)
    y_b = toeplitz(grad_conv, tap_b)
    grad_key, grad_value = pl.pallas_call(
        last_kernel, grid=grid,
        in_specs=[small, small] + [modes] * 8 + [wide, entry, wide, wide, lagged, modes, modes, whole],
        out_specs=[wide, wide], out_shape=[full16, full16], compiler_params=params,
    )(join_b, keep_b, *got_b, y_b, ent_b, key_branch, value_branch, lag_b, decay, far, same_after)
    return layer_out, grad_query, grad_key, grad_value


def solution(mesh):
    tokens = P("seq", "ch")
    placed = (tokens, tokens, tokens, P("ch"), P("ch", None), P("ch", None), P(), tokens)
    return jax.shard_map(local, mesh=mesh, in_specs=placed, out_specs=(tokens,) * 4, check_vma=False)
```

profile of v0, /device:TPU:0, one launch (start us, length us, event | category | flops | bytes accessed | tf_op | source)
XLA Modules:
  0.0 120.8 jit_solution(2045500991164114507)
XLA Ops:
  0.7 0.7 copy.36
  1.4 0.1 reduce.1
  1.6 0.7 sub.84
  2.2 0.1 convert_reduce_fusion
  2.3 0.4 copy-done.12
  2.7 0.1 slice.31
  2.8 0.1 slice.29
  2.9 0.1 slice.27
  3.0 0.1 reshape.239
  3.1 0.2 slice_reduce_fusion
  3.3 0.1 eq.96
  3.5 0.1 sub.96
  3.6 0.1 eq.89
  3.8 0.1 eq.86
  3.9 0.7 exponential_bitcast_fusion
  4.6 0.1 copy.37
  4.7 0.1 neg.28
  4.8 0.3 broadcast_in_dim.29
  5.1 0.6 exp.35.dc_ref.refs_14_.refs_13_
  5.7 0.5 fusion
  6.3 0.3 pad_maximum_fusion.et_ref
  6.6 0.6 compare_convert_fusion
  7.2 0.1 broadcast_in_dim.28.mask_ref
  7.4 6.6 %shard_map.111 = (bf16[512,2048]{1,0:T(8,128)(2,1)S(1)}, f32[8,16,2048]{2,1,0:T(8,128)S(1)}, bf16[16,2048]{1,0:T(8,128)(2,1)}) custom-call(f32[1,8]{1,0:T(1,128)S(1)} %fusion.7.join_ref, bf16[512,2048]{1,0:T(8,128)(2,1)S(1)} %copy-done.1, bf16[512,2048]{1,0:T(8,128)(2,1)} %refs_11_.3, bf16[512,128]{1,0:T(8,128)(2,1)S(1)} %broadcast_in_dim.28.mask_ref, ...), custom_call_target="tpu_custom_call" | custom-call | tf_op jit(solution)/shard_map/pallas_call | solution.py:298
  14.0 1.3 %copy-done.3 = bf16[512,2048]{1,0:T(8,128)(2,1)} copy-done((bf16[512,2048]{1,0:T(8,128)(2,1)}, bf16[512,2048]{1,0:T(8,128)(2,1)S(1)}, u32[]{:S(2)}) %copy-start.3) | copy-done | bytes 2097176
  15.3 1.0 copy-done.5
  16.3 1.7 %collective-permute-start.7 = (bf16[16,2048]{1,0:T(8,128)(2,1)}, bf16[16,2048]{1,0:T(8,128)(2,1)S(1)}, u32[]{:S(2)}, u32[]{:S(2)}) collective-permute-start(bf16[16,2048]{1,0:T(8,128)(2,1)} %get-tuple-element.16), channel_id=1, source_target_pairs={{0,32},{4,36},{8,40},{12,44},{16,48},{20,52},{24,56},{28,60},{32,6... | collective-permute-start | bytes 196616 | tf_op jit(solution)/shard_map/ppermute | solution.py:289
  18.0 3.2 %collective-permute-start.6 = (bf16[16,2048]{1,0:T(8,128)(2,1)}, bf16[16,2048]{1,0:T(8,128)(2,1)S(1)}, u32[]{:S(2)}, u32[]{:S(2)}) collective-permute-start(bf16[16,2048]{1,0:T(8,128)(2,1)} %get-tuple-element.16), channel_id=1, source_target_pairs={{0,28},{4,32},{8,36},{12,40},{16,44},{20,48},{24,52},{28,56},{32,6... | collective-permute-start | bytes 196616 | tf_op jit(solution)/shard_map/ppermute | solution.py:289
  21.2 1.4 %collective-permute-start.5 = (bf16[16,2048]{1,0:T(8,128)(2,1)}, bf16[16,2048]{1,0:T(8,128)(2,1)S(1)}, u32[]{:S(2)}, u32[]{:S(2)}) collective-permute-start(bf16[16,2048]{1,0:T(8,128)(2,1)} %get-tuple-element.16), channel_id=1, source_target_pairs={{0,24},{4,28},{8,32},{12,36},{16,40},{20,44},{24,48},{28,52},{32,5... | collective-permute-start | bytes 196616 | tf_op jit(solution)/shard_map/ppermute | solution.py:289
  22.6 1.1 collective-permute-start.4
  23.7 3.6 %collective-permute-start.3 = (bf16[16,2048]{1,0:T(8,128)(2,1)}, bf16[16,2048]{1,0:T(8,128)(2,1)}, u32[]{:S(2)}, u32[]{:S(2)}) collective-permute-start(bf16[16,2048]{1,0:T(8,128)(2,1)} %get-tuple-element.16), channel_id=1, source_target_pairs={{0,16},{4,20},{8,24},{12,28},{16,32},{20,36},{24,40},{28,44},{32,4... | collective-permute-start | bytes 196616 | tf_op jit(solution)/shard_map/ppermute | solution.py:289
  27.3 0.6 iota_subtract_fusion
  27.9 0.6 fusion.11
  28.7 0.1 copy.39
  28.8 0.1 mul.156
  28.9 0.3 broadcast_in_dim.35
  29.3 0.6 exp.40.refs_15_.refs_14_
  29.9 0.7 convert_reduce_fusion.1
  30.6 0.7 fusion.5.keep_ref
  31.3 0.9 multiply_reduce_fusion
  32.2 0.3 pad_maximum_fusion.1.et_ref
  32.5 0.2 multiply_convert_fusion
  32.8 0.7 subtract_reduce_fusion
  33.5 0.1 collective-permute-start.1
  33.6 0.9 collective-permute-start
  34.5 13.9 %shard_map.112.refs_8_ = f32[512,2048]{1,0:T(8,128)} custom-call(s32[1,1]{1,0:T(1,128)} %bitcast.6.top_ref, bf16[512,2048]{1,0:T(8,128)(2,1)S(1)} %copy-done.4, s32[64,128]{1,0:T(8,128)S(1)} %copy.41.seg_ref, f32[128,128]{1,0:T(8,128)S(1)} %broadcast_select_fusion.1.tap_ref), custom_call_target="tpu_custom_call" | custom-call | flops 1073741824 | bytes 6291456 | tf_op jit(solution)/shard_map/pallas_call | solution.py:292
  48.4 0.1 broadcast_in_dim.36.refs_16_
  48.6 9.3 %shard_map.113 = (f32[512,2048]{1,0:T(8,128)}, f32[8,512]{1,0:T(8,128)S(1)}) custom-call(f32[1,8]{1,0:T(1,128)S(1)} %fusion.7.join_ref, f32[1,8]{1,0:T(1,128)S(1)} %fusion.5.keep_ref, bf16[16,2048]{1,0:T(8,128)(2,1)S(1)} %collective-permute-done.refs_0_, bf16[16,2048]{1,0:T(8,128)(2,1)S(1)} %collective-permute-done.1.refs_1_, ...), custom_call_target="tpu_custom_call" | custom-call | tf_op jit(solution)/shard_map/pallas_call | solution.py:304
  57.9 16.9 %psum.7 = f32[8,512]{1,0:T(8,128)S(1)} all-reduce(f32[8,512]{1,0:T(8,128)S(1)} %get-tuple-element.20), channel_id=1, replica_groups=mesh['seq'=32,'ch'=4] {'ch'}, use_global_device_ids=true, to_apply=%region_5.6 | all-reduce | flops 4096 | bytes 32768 | tf_op jit(solution)/shard_map/psum | solution.py:310
  74.8 0.1 broadcast_in_dim.39.mask_ref
  75.0 0.1 broadcast_in_dim.37.inv_ref
  75.1 0.1 broadcast_in_dim.38.mean_ref
  75.3 8.5 %shard_map.114 = (bf16[512,2048]{1,0:T(8,128)(2,1)}, bf16[512,2048]{1,0:T(8,128)(2,1)}, bf16[512,2048]{1,0:T(8,128)(2,1)S(1)}, f32[8,16,2048]{2,1,0:T(8,128)S(1)}, bf16[16,2048]{1,0:T(8,128)(2,1)S(1)}) custom-call(f32[1,8]{1,0:T(1,128)S(1)} %fusion.6.join_ref, f32[512,2048]{1,0:T(8,128)} %get-tuple-element.19.conv_ref, bf16[512,2048]{1,0:T(8,128)(2,1)} %q_ref.1, ...), custom_call_target="tpu_custom_call" | custom-call | tf_op jit(solution)/shard_map/pallas_call | solution.py:313
  83.8 2.8 %collective-permute-start.15 = (bf16[16,2048]{1,0:T(8,128)(2,1)S(1)}, bf16[16,2048]{1,0:T(8,128)(2,1)S(1)}, u32[]{:S(2)}, u32[]{:S(2)}) collective-permute-start(bf16[16,2048]{1,0:T(8,128)(2,1)S(1)} %get-tuple-element.23), channel_id=1, source_target_pairs={{0,96},{4,100},{8,104},{12,108},{16,112},{20,116},{24,120},{28,124... | collective-permute-start | bytes 196616 | tf_op jit(solution)/shard_map/ppermute | solution.py:289
  86.6 2.4 %collective-permute-start.13 = (bf16[16,2048]{1,0:T(8,128)(2,1)S(1)}, bf16[16,2048]{1,0:T(8,128)(2,1)S(1)}, u32[]{:S(2)}, u32[]{:S(2)}) collective-permute-start(bf16[16,2048]{1,0:T(8,128)(2,1)S(1)} %get-tuple-element.23), channel_id=1, source_target_pairs={{0,104},{4,108},{8,112},{12,116},{16,120},{20,124},{24,0},{28,4},{... | collective-permute-start | bytes 196616 | tf_op jit(solution)/shard_map/ppermute | solution.py:289
  89.0 0.7 fusion.4.keep_ref
  89.7 1.6 %collective-permute-start.12 = (bf16[16,2048]{1,0:T(8,128)(2,1)S(1)}, bf16[16,2048]{1,0:T(8,128)(2,1)S(1)}, u32[]{:S(2)}, u32[]{:S(2)}) collective-permute-start(bf16[16,2048]{1,0:T(8,128)(2,1)S(1)} %get-tuple-element.23), channel_id=1, source_target_pairs={{0,108},{4,112},{8,116},{12,120},{16,124},{20,0},{24,4},{28,8},{32... | collective-permute-start | bytes 196616 | tf_op jit(solution)/shard_map/ppermute | solution.py:289
  91.2 2.6 %collective-permute-start.11 = (bf16[16,2048]{1,0:T(8,128)(2,1)S(1)}, bf16[16,2048]{1,0:T(8,128)(2,1)S(1)}, u32[]{:S(2)}, u32[]{:S(2)}) collective-permute-start(bf16[16,2048]{1,0:T(8,128)(2,1)S(1)} %get-tuple-element.23), channel_id=1, source_target_pairs={{0,112},{4,116},{8,120},{12,124},{16,0},{20,4},{24,8},{28,12},{32,... | collective-permute-start | bytes 196616 | tf_op jit(solution)/shard_map/ppermute | solution.py:289
  93.8 1.0 collective-permute-start.10
  94.9 1.1 collective-permute-start.9
  96.0 2.3 %collective-permute-start.8 = (bf16[16,2048]{1,0:T(8,128)(2,1)S(1)}, bf16[16,2048]{1,0:T(8,128)(2,1)S(1)}, u32[]{:S(2)}, u32[]{:S(2)}) collective-permute-start(bf16[16,2048]{1,0:T(8,128)(2,1)S(1)} %get-tuple-element.23), channel_id=1, source_target_pairs={{0,124},{4,0},{8,4},{12,8},{16,12},{20,16},{24,20},{28,24},{32,28}... | collective-permute-start | bytes 196616 | tf_op jit(solution)/shard_map/ppermute | solution.py:289
  98.3 13.9 %shard_map.115.refs_8_ = f32[512,2048]{1,0:T(8,128)} custom-call(s32[1,1]{1,0:T(1,128)} %bitcast.6.top_ref, bf16[512,2048]{1,0:T(8,128)(2,1)S(1)} %get-tuple-element.24.x_ref, s32[64,128]{1,0:T(8,128)S(1)} %copy.41.seg_ref, f32[128,128]{1,0:T(8,128)S(1)} %broadcast_select_fusion.tap_ref), custom_call_target="tpu_custom_call" | custom-call | flops 1073741824 | bytes 6291456 | tf_op jit(solution)/shard_map/pallas_call | solution.py:292
  112.2 0.1 broadcast_in_dim.41.refs_15_
  112.3 8.4 %shard_map.116 = (bf16[512,2048]{1,0:T(8,128)(2,1)}, bf16[512,2048]{1,0:T(8,128)(2,1)}) custom-call(f32[1,8]{1,0:T(1,128)S(1)} %fusion.6.join_ref, f32[1,8]{1,0:T(1,128)S(1)} %fusion.4.keep_ref, bf16[16,2048]{1,0:T(8,128)(2,1)S(1)} %collective-permute-done.8.refs_0_, bf16[16,2048]{1,0:T(8,128)(2,1)S(1)} %collective-permute-done.9.refs_1_, ...), custom_call_target="tpu_custom_call" | custom-call | tf_op jit(solution)/shard_map/pallas_call | solution.py:321
  (70 shorter events, 0.7 us)
Async XLA Ops:
  2.2 0.5 copy-start.12
  4.7 1.6 %copy-start.8 = (f32[128,16]{1,0:T(8,128)}, f32[128,16]{1,0:T(8,128)S(1)}, u32[]{:S(2)}) copy-start(f32[128,16]{1,0:T(8,128)S(1)} %copy.37) | copy-start | bytes 24580
  5.7 1.6 %copy-start.1 = (bf16[512,2048]{1,0:T(8,128)(2,1)S(1)}, bf16[512,2048]{1,0:T(8,128)(2,1)}, u32[]{:S(2)}) copy-start(bf16[512,2048]{1,0:T(8,128)(2,1)} %refs_10_.3) | copy-start | bytes 6291460
  7.4 21.4 %copy-start.10 = (f32[128,16]{0,1:T(8,128)S(1)}, f32[128,16]{0,1:T(8,128)}, u32[]{:S(2)}) copy-start(f32[128,16]{0,1:T(8,128)} %param.12) | copy-start | bytes 24580
  14.0 1.3 %copy-start.3 = (bf16[512,2048]{1,0:T(8,128)(2,1)}, bf16[512,2048]{1,0:T(8,128)(2,1)S(1)}, u32[]{:S(2)}) copy-start(bf16[512,2048]{1,0:T(8,128)(2,1)S(1)} %get-tuple-element.17.x_ref) | copy-start | bytes 6291460
  15.3 1.0 copy-start.5
  16.3 13.6 %copy-start.13 = (s32[16]{0:T(128)S(1)}, s32[16]{0:T(128)}, u32[]{:S(2)}) copy-start(s32[16]{0:T(128)} %copy-done.12) | copy-start | bytes 196
  16.3 15.0 %copy-start.9 = (f32[128,16]{1,0:T(8,128)S(1)}, f32[128,16]{1,0:T(8,128)}, u32[]{:S(2)}) copy-start(f32[128,16]{1,0:T(8,128)} %copy-done.8) | copy-start | bytes 24580
  16.3 17.2 %collective-permute-start.7 = (bf16[16,2048]{1,0:T(8,128)(2,1)}, bf16[16,2048]{1,0:T(8,128)(2,1)S(1)}, u32[]{:S(2)}, u32[]{:S(2)}) collective-permute-start(bf16[16,2048]{1,0:T(8,128)(2,1)} %get-tuple-element.16), channel_id=1, source_target_pairs={{0,32},{4,36},{8,40},{12,44},{16,48},{20,52},{24,56},{28,60},{32,6... | collective-permute-start | bytes 196616 | tf_op jit(solution)/shard_map/ppermute | solution.py:289
  18.0 15.5 %collective-permute-start.6 = (bf16[16,2048]{1,0:T(8,128)(2,1)}, bf16[16,2048]{1,0:T(8,128)(2,1)S(1)}, u32[]{:S(2)}, u32[]{:S(2)}) collective-permute-start(bf16[16,2048]{1,0:T(8,128)(2,1)} %get-tuple-element.16), channel_id=1, source_target_pairs={{0,28},{4,32},{8,36},{12,40},{16,44},{20,48},{24,52},{28,56},{32,6... | collective-permute-start | bytes 196616 | tf_op jit(solution)/shard_map/ppermute | solution.py:289
  21.2 12.4 %collective-permute-start.5 = (bf16[16,2048]{1,0:T(8,128)(2,1)}, bf16[16,2048]{1,0:T(8,128)(2,1)S(1)}, u32[]{:S(2)}, u32[]{:S(2)}) collective-permute-start(bf16[16,2048]{1,0:T(8,128)(2,1)} %get-tuple-element.16), channel_id=1, source_target_pairs={{0,24},{4,28},{8,32},{12,36},{16,40},{20,44},{24,48},{28,52},{32,5... | collective-permute-start | bytes 196616 | tf_op jit(solution)/shard_map/ppermute | solution.py:289
  22.6 25.8 %collective-permute-start.4 = (bf16[16,2048]{1,0:T(8,128)(2,1)}, bf16[16,2048]{1,0:T(8,128)(2,1)S(1)}, u32[]{:S(2)}, u32[]{:S(2)}) collective-permute-start(bf16[16,2048]{1,0:T(8,128)(2,1)} %get-tuple-element.16), channel_id=1, source_target_pairs={{0,20},{4,24},{8,28},{12,32},{16,36},{20,40},{24,44},{28,48},{32,5... | collective-permute-start | bytes 196616 | tf_op jit(solution)/shard_map/ppermute | solution.py:289
  23.7 24.7 %collective-permute-start.3 = (bf16[16,2048]{1,0:T(8,128)(2,1)}, bf16[16,2048]{1,0:T(8,128)(2,1)}, u32[]{:S(2)}, u32[]{:S(2)}) collective-permute-start(bf16[16,2048]{1,0:T(8,128)(2,1)} %get-tuple-element.16), channel_id=1, source_target_pairs={{0,16},{4,20},{8,24},{12,28},{16,32},{20,36},{24,40},{28,44},{32,4... | collective-permute-start | bytes 196616 | tf_op jit(solution)/shard_map/ppermute | solution.py:289
  29.3 3.3 %copy-start.15 = (f32[64]{0:T(128)S(1)}, f32[64]{0:T(128)}, u32[]{:S(2)}) copy-start(f32[64]{0:T(128)} %get-tuple-element.57) | copy-start | bytes 772
  29.3 3.3 %copy-start.16 = (f32[64]{0:T(128)S(1)}, f32[64]{0:T(128)}, u32[]{:S(2)}) copy-start(f32[64]{0:T(128)} %get-tuple-element.58) | copy-start | bytes 772
  29.9 4.6 %copy-start.4 = (bf16[512,2048]{1,0:T(8,128)(2,1)S(1)}, bf16[512,2048]{1,0:T(8,128)(2,1)}, u32[]{:S(2)}) copy-start(bf16[512,2048]{1,0:T(8,128)(2,1)} %copy-done.3) | copy-start | bytes 6291460
  33.5 14.9 %collective-permute-start.2 = (bf16[16,2048]{1,0:T(8,128)(2,1)}, bf16[16,2048]{1,0:T(8,128)(2,1)S(1)}, u32[]{:S(2)}, u32[]{:S(2)}) collective-permute-start(bf16[16,2048]{1,0:T(8,128)(2,1)} %get-tuple-element.16), channel_id=1, source_target_pairs={{0,12},{4,16},{8,20},{12,24},{16,28},{20,32},{24,36},{28,40},{32,4... | collective-permute-start | bytes 196616 | tf_op jit(solution)/shard_map/ppermute | solution.py:289
  33.5 14.9 %collective-permute-start.1 = (bf16[16,2048]{1,0:T(8,128)(2,1)}, bf16[16,2048]{1,0:T(8,128)(2,1)S(1)}, u32[]{:S(2)}, u32[]{:S(2)}) collective-permute-start(bf16[16,2048]{1,0:T(8,128)(2,1)} %get-tuple-element.16), channel_id=1, source_target_pairs={{0,8},{4,12},{8,16},{12,20},{16,24},{20,28},{24,32},{28,36},{32,40... | collective-permute-start | bytes 196616 | tf_op jit(solution)/shard_map/ppermute | solution.py:289
  33.6 14.8 %collective-permute-start = (bf16[16,2048]{1,0:T(8,128)(2,1)}, bf16[16,2048]{1,0:T(8,128)(2,1)S(1)}, u32[]{:S(2)}, u32[]{:S(2)}) collective-permute-start(bf16[16,2048]{1,0:T(8,128)(2,1)} %get-tuple-element.16), channel_id=1, source_target_pairs={{0,4},{4,8},{8,12},{12,16},{16,20},{20,24},{24,28},{28,32},{32,36}... | collective-permute-start | bytes 196616 | tf_op jit(solution)/shard_map/ppermute | solution.py:289
  34.5 14.1 %copy-start = (bf16[512,2048]{1,0:T(8,128)(2,1)S(1)}, bf16[512,2048]{1,0:T(8,128)(2,1)}, u32[]{:S(2)}) copy-start(bf16[512,2048]{1,0:T(8,128)(2,1)} %q_ref.1) | copy-start | bytes 6291460
  34.5 14.1 %copy-start.6 = (f32[8,16,2048]{2,1,0:T(8,128)S(1)}, f32[8,16,2048]{2,1,0:T(8,128)}, u32[]{:S(2)}) copy-start(f32[8,16,2048]{2,1,0:T(8,128)} %copy-done.5) | copy-start | bytes 3145732
  34.5 14.1 %copy-start.7 = (f32[2048]{0:T(1024)S(1)}, f32[2048]{0:T(1024)}, u32[]{:S(2)}) copy-start(f32[2048]{0:T(1024)} %param.11) | copy-start | bytes 24580
  48.6 26.2 %copy-start.11 = (bf16[512]{0:T(512)(128)(2,1)S(1)}, bf16[512]{0:T(512)(128)(2,1)}, u32[]{:S(2)}) copy-start(bf16[512]{0:T(512)(128)(2,1)} %get-tuple-element.50) | copy-start | bytes 3076
  75.2 13.8 %copy-start.14 = (s32[8]{0:T(128)S(1)}, s32[8]{0:T(128)}, u32[]{:S(2)}) copy-start(s32[8]{0:T(128)} %get-tuple-element.32) | copy-start | bytes 100
  83.8 10.0 %collective-permute-start.15 = (bf16[16,2048]{1,0:T(8,128)(2,1)S(1)}, bf16[16,2048]{1,0:T(8,128)(2,1)S(1)}, u32[]{:S(2)}, u32[]{:S(2)}) collective-permute-start(bf16[16,2048]{1,0:T(8,128)(2,1)S(1)} %get-tuple-element.23), channel_id=1, source_target_pairs={{0,96},{4,100},{8,104},{12,108},{16,112},{20,116},{24,120},{28,124... | collective-permute-start | bytes 196616 | tf_op jit(solution)/shard_map/ppermute | solution.py:289
  86.6 8.3 %collective-permute-start.14 = (bf16[16,2048]{1,0:T(8,128)(2,1)S(1)}, bf16[16,2048]{1,0:T(8,128)(2,1)S(1)}, u32[]{:S(2)}, u32[]{:S(2)}) collective-permute-start(bf16[16,2048]{1,0:T(8,128)(2,1)S(1)} %get-tuple-element.23), channel_id=1, source_target_pairs={{0,100},{4,104},{8,108},{12,112},{16,116},{20,120},{24,124},{28,0}... | collective-permute-start | bytes 196616 | tf_op jit(solution)/shard_map/ppermute | solution.py:289
  86.6 9.4 %collective-permute-start.13 = (bf16[16,2048]{1,0:T(8,128)(2,1)S(1)}, bf16[16,2048]{1,0:T(8,128)(2,1)S(1)}, u32[]{:S(2)}, u32[]{:S(2)}) collective-permute-start(bf16[16,2048]{1,0:T(8,128)(2,1)S(1)} %get-tuple-element.23), channel_id=1, source_target_pairs={{0,104},{4,108},{8,112},{12,116},{16,120},{20,124},{24,0},{28,4},{... | collective-permute-start | bytes 196616 | tf_op jit(solution)/shard_map/ppermute | solution.py:289
  89.7 22.5 %collective-permute-start.12 = (bf16[16,2048]{1,0:T(8,128)(2,1)S(1)}, bf16[16,2048]{1,0:T(8,128)(2,1)S(1)}, u32[]{:S(2)}, u32[]{:S(2)}) collective-permute-start(bf16[16,2048]{1,0:T(8,128)(2,1)S(1)} %get-tuple-element.23), channel_id=1, source_target_pairs={{0,108},{4,112},{8,116},{12,120},{16,124},{20,0},{24,4},{28,8},{32... | collective-permute-start | bytes 196616 | tf_op jit(solution)/shard_map/ppermute | solution.py:289
  91.2 20.9 %collective-permute-start.11 = (bf16[16,2048]{1,0:T(8,128)(2,1)S(1)}, bf16[16,2048]{1,0:T(8,128)(2,1)S(1)}, u32[]{:S(2)}, u32[]{:S(2)}) collective-permute-start(bf16[16,2048]{1,0:T(8,128)(2,1)S(1)} %get-tuple-element.23), channel_id=1, source_target_pairs={{0,112},{4,116},{8,120},{12,124},{16,0},{20,4},{24,8},{28,12},{32,... | collective-permute-start | bytes 196616 | tf_op jit(solution)/shard_map/ppermute | solution.py:289
  93.8 18.4 %collective-permute-start.10 = (bf16[16,2048]{1,0:T(8,128)(2,1)S(1)}, bf16[16,2048]{1,0:T(8,128)(2,1)S(1)}, u32[]{:S(2)}, u32[]{:S(2)}) collective-permute-start(bf16[16,2048]{1,0:T(8,128)(2,1)S(1)} %get-tuple-element.23), channel_id=1, source_target_pairs={{0,116},{4,120},{8,124},{12,0},{16,4},{20,8},{24,12},{28,16},{32,2... | collective-permute-start | bytes 196616 | tf_op jit(solution)/shard_map/ppermute | solution.py:289
  94.9 17.3 %collective-permute-start.9 = (bf16[16,2048]{1,0:T(8,128)(2,1)S(1)}, bf16[16,2048]{1,0:T(8,128)(2,1)S(1)}, u32[]{:S(2)}, u32[]{:S(2)}) collective-permute-start(bf16[16,2048]{1,0:T(8,128)(2,1)S(1)} %get-tuple-element.23), channel_id=1, source_target_pairs={{0,120},{4,124},{8,0},{12,4},{16,8},{20,12},{24,16},{28,20},{32,24... | collective-permute-start | bytes 196616 | tf_op jit(solution)/shard_map/ppermute | solution.py:289
  96.0 16.2 %collective-permute-start.8 = (bf16[16,2048]{1,0:T(8,128)(2,1)S(1)}, bf16[16,2048]{1,0:T(8,128)(2,1)S(1)}, u32[]{:S(2)}, u32[]{:S(2)}) collective-permute-start(bf16[16,2048]{1,0:T(8,128)(2,1)S(1)} %get-tuple-element.23), channel_id=1, source_target_pairs={{0,124},{4,0},{8,4},{12,8},{16,12},{20,16},{24,20},{28,24},{32,28}... | collective-permute-start | bytes 196616 | tf_op jit(solution)/shard_map/ppermute | solution.py:289
  98.3 14.0 %copy-start.2 = (bf16[512,2048]{1,0:T(8,128)(2,1)S(1)}, bf16[512,2048]{1,0:T(8,128)(2,1)}, u32[]{:S(2)}) copy-start(bf16[512,2048]{1,0:T(8,128)(2,1)} %refs_10_.3) | copy-start | bytes 6291460
where the time goes:
time: 122 us; the launch traced here: 121 us
  Pallas kernels  60.7 us (50%)
  starting transfers between devices  25.7 us (21%)
  blocking collectives  16.9 us (14%)
  local copies, waits for them, and re-layouts  8.38 us (7%)
  other arithmetic  7.98 us (7%)
    pallas_call x2, Pallas kernels, toeplitz(): pl.pallas_call(toeplitz_kernel, grid=grid, in_specs=[small, wide, seg_spe...  27.8 us
    ppermute x16, starting transfers between devices, send(): lax.ppermute(x, 'seq', [(i, (i + way * n) % devices) for i in range(devic...  25.7 us
    psum x1, blocking collectives, local(): stat = lax.psum(stat, 'ch')  16.9 us
    pallas_call x1, Pallas kernels, local(): pl.pallas_call(gate_kernel, grid=grid, in_specs=[small, small] + [modes]...  9.3 us
    pallas_call x1, Pallas kernels, local(): pl.pallas_call(grad_kernel, grid=grid, in_specs=[small, wide, wide, wide,...  8.54 us
    pallas_call x1, Pallas kernels, local(): pl.pallas_call(last_kernel, grid=grid, in_specs=[small, small] + [modes]...  8.45 us
    pallas_call x1, Pallas kernels, local(): pl.pallas_call(first_kernel, grid=grid, in_specs=[small, wide, wide, whol...  6.64 us
    unnamed x35, local copies, waits for them, and re-layouts  2.9 us
  transfers between devices with their start and end apart: 16, of which 0 were waited for; matrix products, arithmetic and copies ran while one was open for 6% of the time, Pallas kernels for 23%

commit v1 on v0

v1 whole, which is shorter than its diff:
```python
import jax
import jax.numpy as jnp
from jax import lax
from jax.experimental import pallas as pl
from jax.experimental.pallas import tpu as pltpu
from jax.sharding import PartitionSpec as P

C = 64
W = 128
LB = 512
G = 16
R = 16
NG = W // G
DOCS = 16
REACH = 4096
DEPTH = C + 3 * R
EPS = 1e-6
f32, bf16, i32 = jnp.float32, jnp.bfloat16, jnp.int32
VLIM = 61 * 1024 * 1024


def dot(a, b):
    return jnp.dot(a, b, preferred_element_type=f32)


def iota(rows, axis):
    return lax.broadcasted_iota(i32, (rows, W), axis)


def turn(x, lanes):
    return pltpu.roll(x, lanes % W, 1)


def swap_blocks(parts):
    parts = list(parts)
    blk = iota(parts[0].shape[0], 1) // G
    bit = 1
    while bit < NG:
        low = (blk & bit) == 0
        for m in range(NG):
            if not m & bit:
                a, b = parts[m], parts[m | bit]
                parts[m] = jnp.where(low, a, turn(b, G * bit))
                parts[m | bit] = jnp.where(low, turn(a, -G * bit), b)
        bit *= 2
    return parts


def fan_out(x):
    blk = iota(x.shape[0], 1) // G
    parts, bit = [x], NG // 2
    while bit:
        low = (blk & bit) == 0
        parts = [
            y
            for x in parts
            for y in (jnp.where(low, x, turn(x, G * bit)), jnp.where(low, turn(x, -G * bit), x))
        ]
        bit //= 2
    return parts


def docs_at(places, len_ref):
    found, start = jnp.full(places.shape, -1, i32), i32(0)
    for n in range(DOCS):
        found += (places >= start).astype(i32)
        start += len_ref[n]
    return found


def chunk_places(here_ref, rows):
    return here_ref[0, 0] * (C * NG) + (iota(rows, 1) // G) * C


def state_masks(here_ref, len_ref, way):
    blk = iota(R, 1) // G
    base = chunk_places(here_ref, R)
    tokens = docs_at(chunk_places(here_ref, C) + iota(C, 0), len_ref)
    if way > 0:
        end, enter = C - 1, 0
        order = blk
    else:
        end, enter = 0, C - 1
        order = NG - 1 - blk
    ends = docs_at(chunk_places(here_ref, C) + end, len_ref)
    reach = (tokens == ends).astype(f32).astype(bf16)
    own = docs_at(base + end, len_ref)
    joins = []
    for n in (1, 2, 4):
        there = docs_at(base + end - way * n * C, len_ref)
        joins.append(((own == there) & (order >= n)).astype(f32))
    prior = docs_at(base + enter - way, len_ref)
    into = ((docs_at(base + enter, len_ref) == prior) & (order >= 1)).astype(f32)
    return reach, joins, into


def chunk_states(z, rate_ref, first_row, masks, way):
    reach, joins, into = masks
    lane = iota(R, 1).astype(f32)
    blk = iota(R, 1) // G
    away = (C - 1.0) - lane if way > 0 else lane
    entries, last = [], jnp.zeros((R, W), f32)
    for g in range(NG):
        rate = rate_ref[first_row + g * R : first_row + (g + 1) * R, :]
        fall = jnp.exp(-rate * away)[:, :C]
        hi = fall.astype(bf16)
        lo = (fall - hi.astype(f32)).astype(bf16)
        both = dot(jnp.concatenate([hi, lo], axis=0), z[g] * reach)
        state = both[:R] + both[R:]
        decay = jnp.exp(-rate * C)
        for n, join in zip((1, 2, 4), joins):
            state += (decay * join) * turn(state, way * n * G)
            decay *= decay
        entries.append(into * turn(state, way * G))
        end = NG - 1 if way > 0 else 0
        last = jnp.where(blk == g, turn(state, (g - end) * G), last)
    return entries, last


def first_kernel(here_ref, len_ref, k_ref, v_ref, rate_ref, z_ref, ent_ref, own_ref):
    masks = state_masks(here_ref, len_ref, 1)
    for s in range(LB // W):
        at = slice(s * W, (s + 1) * W)
        x = (k_ref[:, at].astype(f32) * v_ref[:, at].astype(f32)).astype(bf16).astype(f32)
        z = [part.astype(bf16) for part in swap_blocks([x[m * C : (m + 1) * C] for m in range(NG)])]
        entries, last = chunk_states(z, rate_ref, s * NG * R, masks, 1)
        for g in range(NG):
            n = s * NG + g
            z_ref[n * C : (n + 1) * C, :] = z[g]
            ent_ref[n * R : (n + 1) * R, :] = entries[g]
        own_ref[:, at] = last.astype(bf16)


def table_kernel(tapf_ref, tapb_ref, rate_ref, res_ref, lf_ref, lb_ref):
    lane, row = iota(C, 1), iota(C, 0).astype(f32)
    for g in range(LB // G):
        at = slice(g, g + 1)
        rate = jnp.broadcast_to(rate_ref[at, :], (C, W))
        res = jnp.broadcast_to(res_ref[at, :], (C, W))
        for tap_ref, out_ref, lag in ((tapf_ref, lf_ref, row + 1.0), (tapb_ref, lb_ref, C - row)):
            taps = jnp.broadcast_to(tap_ref[at, :], (C, W))
            square = pltpu.roll(taps, 0, 1, stride=1, stride_axis=0)
            carry = res * jnp.exp(-rate * lag)
            hi = carry.astype(bf16).astype(f32)
            carry = jnp.where(lane < C + 2 * R, hi, jnp.where(lane < DEPTH, carry - hi, 0.0))
            out_ref[g * C : (g + 1) * C, :] = jnp.where(lane < C, square, carry).astype(bf16)


def segments(here_ref, len_ref, way):
    first = chunk_places(here_ref, C)
    tokens = docs_at(first + iota(C, 0), len_ref)
    if way > 0:
        return tokens - docs_at(first, len_ref)
    return docs_at(first + (C - 1), len_ref) - tokens


def convolve(here_ref, len_ref, keep_ref, got, far_ref, rate_ref, z_ref, ent_ref, left_ref, o_ref, seg, s, way):
    at = slice(s * W, (s + 1) * W)
    total, far = jnp.zeros((R, W), f32), far_ref[:, at]
    for n in reversed(range(len(got))):
        total = keep_ref[0, n] * got[n][:, at].astype(f32) + far * total
    blk = iota(R, 1) // G
    base = chunk_places(here_ref, R)
    start = here_ref[0, 0] * (C * NG)
    if way > 0:
        order, edge, enter = blk, start - 1, 0
    else:
        order, edge, enter = NG - 1 - blk, start + C * NG, C - 1
    from_far = (docs_at(base + enter, len_ref) == docs_at(jnp.full((R, W), edge, i32), len_ref)).astype(f32)
    span = (order * C).astype(f32)
    m0, m1 = (seg == 0).astype(f32).astype(bf16), (seg == 1).astype(f32).astype(bf16)
    none = jnp.zeros((3 * R, W), bf16)
    for g, arrived in enumerate(fan_out(total)):
        n = s * NG + g
        rate = rate_ref[n * R : (n + 1) * R, :]
        entry = ent_ref[n * R : (n + 1) * R, :] + arrived * (jnp.exp(-rate * span) * from_far)
        hi = entry.astype(bf16)
        lo = (entry - hi.astype(f32)).astype(bf16)
        z = z_ref[n * C : (n + 1) * C, :]
        right = jnp.concatenate(
            [jnp.concatenate([z * m0, hi, lo, hi], axis=0), jnp.concatenate([z * m1, none], axis=0)], axis=1
        )
        y = dot(left_ref[n * C : (n + 1) * C, :DEPTH], right)
        o_ref[g] = jnp.where(seg == 0, y[:, :W], y[:, W:])

    top = jnp.max(seg)

    @pl.when(top > 1)
    def _():
        def again(p, carry):
            mask = (seg == p).astype(f32).astype(bf16)
            for g in range(NG):
                n = s * NG + g
                square = left_ref[n * C : (n + 1) * C, :C]
                o_ref[g] = jnp.where(seg == p, dot(square, z_ref[n * C : (n + 1) * C, :] * mask), o_ref[g])
            return carry

        lax.fori_loop(2, top + 1, again, 0)

    return swap_blocks([o_ref[g] for g in range(NG)])


def gate_kernel(here_ref, len_ref, keep_ref, *refs):
    got, refs = refs[:8], refs[8:]
    far_ref, rate_ref, z_ref, ent_ref, left_ref, q_ref, c_ref, gain_ref, conv_ref, stat_ref, acc_ref, o_ref = refs
    step = pl.program_id(0)

    @pl.when(step == 0)
    def _():
        acc_ref[...] = jnp.zeros_like(acc_ref)

    seg = segments(here_ref, len_ref, 1)
    for s in range(LB // W):
        at = slice(s * W, (s + 1) * W)
        parts = convolve(here_ref, len_ref, keep_ref, got, far_ref, rate_ref, z_ref, ent_ref, left_ref, o_ref, seg, s, 1)
        for m, conv in enumerate(parts):
            rows = slice(m * C, (m + 1) * C)
            conv_ref[rows, at] = conv
            gated = q_ref[rows, at].astype(f32) * conv
            acc_ref[rows, :W] += gated * gated
            acc_ref[rows, W:] += c_ref[rows, at].astype(f32) * gain_ref[:, at] * gated

    @pl.when(step == pl.num_programs(0) - 1)
    def _():
        row = lax.broadcasted_iota(i32, (8, 2 * W), 0)
        lane = lax.broadcasted_iota(i32, (8, 2 * W), 1)
        pick = (row == lane // W).astype(f32)
        stat_ref[...] = lax.dot_general(
            pick, acc_ref[...], (((1,), (1,)), ((), ())), precision=lax.Precision.HIGHEST, preferred_element_type=f32
        )


def grad_kernel(
    here_ref, len_ref, conv_ref, q_ref, c_ref, gain_ref, inv_ref, mean_ref, rate_ref, z_ref, ent_ref, own_ref
):
    masks = state_masks(here_ref, len_ref, -1)
    for s in range(LB // W):
        at = slice(s * W, (s + 1) * W)
        gain = gain_ref[:, at]
        parts = []
        for m in range(NG):
            rows = slice(m * C, (m + 1) * C)
            inv = inv_ref[rows, :]
            q = q_ref[rows, at].astype(f32)
            normed = q * conv_ref[rows, at] * inv
            parts.append(inv * (c_ref[rows, at].astype(f32) * gain - normed * mean_ref[rows, :]) * q)
        z = [part.astype(bf16) for part in swap_blocks(parts)]
        entries, last = chunk_states(z, rate_ref, s * NG * R, masks, -1)
        for g in range(NG):
            n = s * NG + g
            z_ref[n * C : (n + 1) * C, :] = z[g]
            ent_ref[n * R : (n + 1) * R, :] = entries[g]
        own_ref[:, at] = last.astype(bf16)


def out_kernel(conv_ref, q_ref, c_ref, gain_ref, inv_ref, mean_ref, out_ref, gq_ref):
    inv, mean = inv_ref[...], mean_ref[...]
    for s in range(LB // W):
        at = slice(s * W, (s + 1) * W)
        conv, gain = conv_ref[:, at], gain_ref[:, at]
        normed = q_ref[:, at].astype(f32) * conv * inv
        out_ref[:, at] = (normed * gain).astype(bf16)
        gq_ref[:, at] = (inv * (c_ref[:, at].astype(f32) * gain - normed * mean) * conv).astype(bf16)


def last_kernel(here_ref, len_ref, keep_ref, *refs):
    got, refs = refs[:8], refs[8:]
    far_ref, rate_ref, z_ref, ent_ref, left_ref, k_ref, v_ref, gk_ref, gv_ref, o_ref = refs
    seg = segments(here_ref, len_ref, -1)
    for s in range(LB // W):
        at = slice(s * W, (s + 1) * W)
        parts = convolve(here_ref, len_ref, keep_ref, got, far_ref, rate_ref, z_ref, ent_ref, left_ref, o_ref, seg, s, -1)
        for m, grad in enumerate(parts):
            rows = slice(m * C, (m + 1) * C)
            gk_ref[rows, at] = (grad * v_ref[rows, at].astype(f32)).astype(bf16)
            gv_ref[rows, at] = (grad * k_ref[rows, at].astype(f32)).astype(bf16)


def doc_index(places, doc_lengths):
    doc_ends = jnp.cumsum(doc_lengths)
    doc_starts = doc_ends - doc_lengths
    return jnp.sum((doc_starts[None, :] <= places[:, None]).astype(i32), axis=1) - 1


def local(query_gate, key_branch, value_branch, norm_gain, residues, decay_rate, doc_lengths, cotangent):
    rows, width = query_gate.shape
    groups = residues.shape[0]
    devices = lax.axis_size("seq")
    here = lax.axis_index("seq")
    total_width = width * lax.axis_size("ch")
    shifts = range(1, REACH // rows + 1)
    here_arr = here.astype(i32).reshape(1, 1)

    step = jnp.arange(len(shifts), dtype=i32) + 1
    places = jnp.concatenate([(here - step + 1) * rows - 1, (here + step) * rows])
    docs = doc_index(places, doc_lengths)
    back, ahead = docs[: len(shifts)], docs[len(shifts) :]
    keep_f = ((back == back[0]) & (here >= step)).astype(f32).reshape(1, -1)
    keep_b = ((ahead == ahead[0]) & (here + step < devices)).astype(f32).reshape(1, -1)

    rates = jnp.broadcast_to(decay_rate.reshape(groups * R, 1), (groups * R, W))
    lane = jnp.arange(W)

    def taps(lags):
        h = jnp.sum(residues[:, :, None] * jnp.exp(-decay_rate[:, :, None] * lags.astype(f32)), axis=1)
        return jnp.where(lags < C, h, 0.0)

    tap_f, tap_b = taps((W - lane) % W), taps(lane)
    rate_rep, res_rep = jnp.tile(decay_rate, (1, NG)), jnp.tile(residues, (1, NG))
    far = jnp.exp(-jnp.repeat(decay_rate.T, G, axis=1) * rows)
    gain = norm_gain.reshape(1, width)

    grid = (width // LB,)
    wide = pl.BlockSpec((rows, LB), lambda i: (0, i))
    modes = pl.BlockSpec((R, LB), lambda i: (0, i))
    stacked = pl.BlockSpec((LB // G * C, W), lambda i: (i, 0))
    states = pl.BlockSpec((LB // G * R, W), lambda i: (i, 0))
    tapped = pl.BlockSpec((LB // G, W), lambda i: (i, 0))
    row1 = pl.BlockSpec((1, LB), lambda i: (0, i))
    whole = pl.BlockSpec((rows, W), lambda i: (0, 0))
    small = pl.BlockSpec(memory_space=pltpu.SMEM)
    params = pltpu.CompilerParams(vmem_limit_bytes=VLIM, dimension_semantics=("arbitrary",))

    def shaped(dtype, *shape):
        return jax.ShapeDtypeStruct(shape, dtype)

    full16, full32 = shaped(bf16, rows, width), shaped(f32, rows, width)
    stack16 = shaped(bf16, groups * C, W)
    entries, ends = shaped(f32, groups * R, W), shaped(bf16, R, width)
    scratch = pltpu.VMEM((NG, C, W), f32)

    def send(x, way):
        return [lax.ppermute(x, "seq", [(i, (i + way * n) % devices) for i in range(devices)]) for n in shifts]

    def spread(column):
        return jnp.broadcast_to(column[:, None], (rows, W))

    z_f, ent_f, own_f = pl.pallas_call(
        first_kernel, grid=grid, in_specs=[small, small, wide, wide, states], out_specs=[stacked, states, modes],
        out_shape=[stack16, entries, ends], compiler_params=params, name="first",
    )(here_arr, doc_lengths, key_branch, value_branch, rates)
    got_f = send(own_f, 1)
    left_f, left_b = pl.pallas_call(
        table_kernel, grid=grid, in_specs=[tapped] * 4, out_specs=[stacked] * 2, out_shape=[stack16] * 2,
        compiler_params=params, name="tables",
        cost_estimate=pl.CostEstimate(flops=8 * rows * width, bytes_accessed=4 * rows * width, transcendentals=0),
    )(tap_f, tap_b, rate_rep, res_rep)
    conv, stat = pl.pallas_call(
        gate_kernel, grid=grid,
        in_specs=[small] * 3 + [modes] * 9 + [states, stacked, states, stacked, wide, wide, row1],
        out_specs=[wide, pl.BlockSpec((8, rows), lambda i: (0, 0))], out_shape=[full32, shaped(f32, 8, rows)],
        scratch_shapes=[pltpu.VMEM((rows, 2 * W), f32), scratch], compiler_params=params, name="gate",
    )(here_arr, doc_lengths, keep_f, *got_f, far, rates, z_f, ent_f, left_f, query_gate, cotangent, gain)
    stat = lax.psum(stat, "ch")
    inv = lax.rsqrt(stat[0] / total_width + EPS)
    mean = inv * stat[1] / total_width
    inv, mean = spread(inv), spread(mean)
    z_b, ent_b, own_b = pl.pallas_call(
        grad_kernel, grid=grid, in_specs=[small, small, wide, wide, wide, row1, whole, whole, states],
        out_specs=[stacked, states, modes], out_shape=[stack16, entries, ends], compiler_params=params, name="grad",
    )(here_arr, doc_lengths, conv, query_gate, cotangent, gain, inv, mean, rates)
    got_b = send(own_b, -1)
    layer_out, grad_query = pl.pallas_call(
        out_kernel, grid=grid, in_specs=[wide, wide, wide, row1, whole, whole],
        out_specs=[wide, wide], out_shape=[full16, full16], compiler_params=params, name="outputs",
        cost_estimate=pl.CostEstimate(flops=8 * rows * width, bytes_accessed=12 * rows * width, transcendentals=0),
    )(conv, query_gate, cotangent, gain, inv, mean)
    grad_key, grad_value = pl.pallas_call(
        last_kernel, grid=grid,
        in_specs=[small] * 3 + [modes] * 9 + [states, stacked, states, stacked, wide, wide],
        out_specs=[wide, wide], out_shape=[full16, full16], scratch_shapes=[scratch], compiler_params=params, name="last",
    )(here_arr, doc_lengths, keep_b, *got_b, far, rates, z_b, ent_b, left_b, key_branch, value_branch)
    return layer_out, grad_query, grad_key, grad_value


def solution(mesh):
    tokens = P("seq", "ch")
    placed = (tokens, tokens, tokens, P("ch"), P("ch", None), P("ch", None), P(), tokens)
    return jax.shard_map(local, mesh=mesh, in_specs=placed, out_specs=(tokens,) * 4, check_vma=False)
```

time: 122 us -> 112 us (0.918)
  Pallas kernels: 60.7 us -> 54.1 us
  other arithmetic: 7.98 us -> 3.92 us
    pallas_call x6, Pallas kernels: 60.7 us -> 54.1 us  [the longest x1 12.8 us: local(): pl.pallas_call(gate_kernel, grid=grid, in_specs=[small] * 3 + [modes] * 9...]
    convert_element_type x5 -> x0, other arithmetic: 2.75 us -> none  [the longest x1 0.69 us: local(): keep_f = ((end_docs == docs[0]) & (here >= step)).astype(f32).reshape(1, -1)]
    broadcast_in_dim x9 -> x5, local copies, waits for them, and re-layouts: 1.41 us -> 3.47 us  [the longest x2 1.67 us: spread(): return jnp.broadcast_to(column[:, None], (rows, W))]
    reshape x2 -> x1, other arithmetic: 0.01 us -> 1.91 us  [local(): ((ahead == ahead[0]) & (here + step < devices)).astype(f32).reshape(1, -1)]
    unnamed x35 -> x40, local copies, waits for them, and re-layouts: 2.9 us -> 2.18 us
  transfers between devices with their start and end apart: 16 -> 16, of which waited for: 0 -> 0; matrix products, arithmetic and copies ran while one was open for 6% -> 7% of each run, Pallas kernels for 23% -> 11%
where the time goes in v1:
time: 112 us; the launch traced here: 111 us
  Pallas kernels  54.1 us (48%)
  starting transfers between devices  25.5 us (23%)
  blocking collectives  17.5 us (16%)
  local copies, waits for them, and re-layouts  9.16 us (8%)
  other arithmetic  3.92 us (4%)
  between operations  1.13 us (1%)
    ppermute x16, starting transfers between devices, send(): lax.ppermute(x, 'seq', [(i, (i + way * n) % devices) for i in range(devic...  25.5 us
    psum x1, blocking collectives, local(): stat = lax.psum(stat, 'ch')  17.5 us
    pallas_call x1, Pallas kernels, local(): pl.pallas_call(gate_kernel, grid=grid, in_specs=[small] * 3 + [modes] * 9...  12.8 us
    pallas_call x1, Pallas kernels, local(): pl.pallas_call(last_kernel, grid=grid, in_specs=[small] * 3 + [modes] * 9...  12.1 us
    pallas_call x1, Pallas kernels, local(): pl.pallas_call(grad_kernel, grid=grid, in_specs=[small, small, wide, wide...  9.39 us
    pallas_call x1, Pallas kernels, local(): pl.pallas_call(first_kernel, grid=grid, in_specs=[small, small, wide, wid...  7.92 us
    pallas_call x1, Pallas kernels, local(): pl.pallas_call(out_kernel, grid=grid, in_specs=[wide, wide, wide, row1, w...  6.65 us
    pallas_call x1, Pallas kernels, local(): pl.pallas_call(table_kernel, grid=grid, in_specs=[tapped] * 4, out_specs=...  5.26 us
  transfers between devices with their start and end apart: 16, of which 0 were waited for; matrix products, arithmetic and copies ran while one was open for 7% of the time, Pallas kernels for 11%

profile of v1, /device:TPU:0, one launch (start us, length us, event | category | flops | bytes accessed | tf_op | source)
XLA Modules:
  0.0 111.3 jit_solution(3182394837575103250)
XLA Ops:
  0.6 0.8 copy.24
  1.4 0.1 broadcast_in_dim.22
  1.5 1.4 %broadcast_in_dim.23.rate_ref.refs_9_ = f32[2048,128]{1,0:T(8,128)} broadcast(f32[2048]{0:T(1024)S(1)} %broadcast_in_dim.22), dimensions={0} | broadcast | bytes 1056768 | tf_op jit(solution)/shard_map/broadcast_in_dim | solution.py:301
  2.9 7.9 %first.1 = (bf16[8192,128]{1,0:T(8,128)(2,1)}, f32[2048,128]{1,0:T(8,128)}, bf16[16,2048]{1,0:T(8,128)(2,1)}) custom-call(s32[1,1]{1,0:T(1,128)} %bitcast.here_ref, s32[16]{0:T(128)} %len_ref.7, bf16[512,2048]{1,0:T(8,128)(2,1)} %refs_13_.3, bf16[512,2048]{1,0:T(8,128)(2,1)} %refs_14_.3, f32[2048,128]{1,0:T(8,128)} %broadcast_in_dim.23.rate_ref.refs_9_), custom_call_target="tpu_custom_call" | custom-call | tf_op jit(solution)/shard_map/first/pallas_call | solution.py:338
  10.8 1.7 %collective-permute-start.7 = (bf16[16,2048]{1,0:T(8,128)(2,1)}, bf16[16,2048]{1,0:T(8,128)(2,1)S(1)}, u32[]{:S(2)}, u32[]{:S(2)}) collective-permute-start(bf16[16,2048]{1,0:T(8,128)(2,1)} %get-tuple-element.18), channel_id=1, source_target_pairs={{0,32},{4,36},{8,40},{12,44},{16,48},{20,52},{24,56},{28,60},{32,6... | collective-permute-start | bytes 196616 | tf_op jit(solution)/shard_map/ppermute | solution.py:333
  12.5 3.2 %collective-permute-start.6 = (bf16[16,2048]{1,0:T(8,128)(2,1)}, bf16[16,2048]{1,0:T(8,128)(2,1)S(1)}, u32[]{:S(2)}, u32[]{:S(2)}) collective-permute-start(bf16[16,2048]{1,0:T(8,128)(2,1)} %get-tuple-element.18), channel_id=1, source_target_pairs={{0,28},{4,32},{8,36},{12,40},{16,44},{20,48},{24,52},{28,56},{32,6... | collective-permute-start | bytes 196616 | tf_op jit(solution)/shard_map/ppermute | solution.py:333
  15.7 1.4 %collective-permute-start.5 = (bf16[16,2048]{1,0:T(8,128)(2,1)}, bf16[16,2048]{1,0:T(8,128)(2,1)S(1)}, u32[]{:S(2)}, u32[]{:S(2)}) collective-permute-start(bf16[16,2048]{1,0:T(8,128)(2,1)} %get-tuple-element.18), channel_id=1, source_target_pairs={{0,24},{4,28},{8,32},{12,36},{16,40},{20,44},{24,48},{28,52},{32,5... | collective-permute-start | bytes 196616 | tf_op jit(solution)/shard_map/ppermute | solution.py:333
  17.1 1.1 collective-permute-start.4
  18.2 3.6 %collective-permute-start.3 = (bf16[16,2048]{1,0:T(8,128)(2,1)}, bf16[16,2048]{1,0:T(8,128)(2,1)S(1)}, u32[]{:S(2)}, u32[]{:S(2)}) collective-permute-start(bf16[16,2048]{1,0:T(8,128)(2,1)} %get-tuple-element.18), channel_id=1, source_target_pairs={{0,16},{4,20},{8,24},{12,28},{16,32},{20,36},{24,40},{28,44},{32,4... | collective-permute-start | bytes 196616 | tf_op jit(solution)/shard_map/ppermute | solution.py:333
  21.9 0.1 copy.23
  22.0 0.1 reduce
  22.1 0.1 pad_add_fusion
  22.2 0.2 convert_reduce_fusion
  22.4 0.1 copy.26
  22.5 0.1 copy.25
  22.6 0.8 multiply_reduce_fusion
  23.5 0.7 broadcast_select_fusion
  24.1 0.6 fusion.10
  24.7 0.0 collective-permute-done.7.refs_7_
  24.7 0.0 collective-permute-start.2
  24.7 0.0 collective-permute-done.6.refs_6_
  24.8 0.1 collective-permute-start.1
  24.8 0.0 collective-permute-done.5.refs_5_
  24.9 0.9 collective-permute-start
  25.8 1.9 %fusion.5 = (f32[1,8]{1,0:T(1,128)}, f32[1,8]{1,0:T(1,128)}) fusion(s32[16]{0:T(128)S(1)} %broadcast_add_fusion, s32[]{:T(128)} %bitcast.10, s32[]{:T(128)} %axis_index.15, s32[]{:T(128)} %bitcast.2), kind=kLoop, calls=%fused_computation.23 | loop fusion | flops 80 | bytes 140 | tf_op jit(solution)/shard_map/reshape | solution.py:299
  27.7 0.7 copy.28.res_ref
  28.4 0.7 copy.27.rate_ref
  29.1 0.3 broadcast_in_dim.44
  29.5 1.3 %exp.15.refs_8_ = f32[16,2048]{1,0:T(8,128)} reshape(f32[16,128,16]{2,1,0:T(8,128)S(1)} %broadcast_in_dim.44) | data formatting | bytes 262144 | tf_op jit(solution)/shard_map/exp | solution.py:310
  30.7 5.3 %tables.1 = (bf16[8192,128]{1,0:T(8,128)(2,1)}, bf16[8192,128]{1,0:T(8,128)(2,1)}) custom-call(f32[128,128]{1,0:T(8,128)} %get-tuple-element.45.tapf_ref, f32[128,128]{1,0:T(8,128)} %get-tuple-element.44.tapb_ref, f32[128,128]{1,0:T(8,128)} %copy.27.rate_ref, f32[128,128]{1,0:T(8,128)} %copy.28.res_ref), custom_call_target="tpu_custom_call" | custom-call | flops 8388608 | bytes 4194304 | tf_op jit(solution)/shard_map/tables/pallas_call | solution.py:343
  36.0 0.0 collective-permute-done.4.refs_4_
  36.0 0.0 collective-permute-done.3.refs_3_
  36.0 0.0 collective-permute-done.2.refs_2_
  36.1 0.0 collective-permute-done.1.refs_1_
  36.1 0.0 collective-permute-done.refs_0_
  36.1 0.0 copy-start.13
  36.1 0.5 copy-done.4
  36.6 0.0 copy-done.5
  36.7 0.0 copy-done.8
  36.7 0.0 copy-done.11
  36.7 0.0 copy-done.13
  36.7 12.8 %gate.1 = (f32[512,2048]{1,0:T(8,128)}, f32[8,512]{1,0:T(8,128)}) custom-call(s32[1,1]{1,0:T(1,128)} %bitcast.here_ref, s32[16]{0:T(128)} %len_ref.7, f32[1,8]{1,0:T(1,128)} %get-tuple-element.39.keep_ref, bf16[16,2048]{1,0:T(8,128)(2,1)} %copy-done.13, bf16[16,2048]{1,0:T(8,128)(2,1)} %copy-done.11, bf16[16,2048]{1,0:T(8,128)(2,1)} %copy-done.8, ...), custom_call_target="tpu_custom_call" | custom-call | tf_op jit(solution)/shard_map/gate/pallas_call | solution.py:348
  49.5 17.5 %psum.7 = f32[8,512]{1,0:T(8,128)S(1)} all-reduce(f32[8,512]{1,0:T(8,128)} %get-tuple-element.23), channel_id=1, replica_groups=mesh['seq'=32,'ch'=4] {'ch'}, use_global_device_ids=true, to_apply=%region_4.5 | all-reduce | flops 4096 | bytes 32768 | tf_op jit(solution)/shard_map/psum | solution.py:354
  67.1 0.8 broadcast_in_dim.48.inv_ref
  67.9 0.8 broadcast_in_dim.49.mean_ref
  68.8 9.4 %grad.1 = (bf16[8192,128]{1,0:T(8,128)(2,1)}, f32[2048,128]{1,0:T(8,128)}, bf16[16,2048]{1,0:T(8,128)(2,1)}) custom-call(s32[1,1]{1,0:T(1,128)} %bitcast.here_ref, s32[16]{0:T(128)} %len_ref.7, f32[512,2048]{1,0:T(8,128)} %get-tuple-element.22.conv_ref, bf16[512,2048]{1,0:T(8,128)(2,1)} %q_ref.3, bf16[512,2048]{1,0:T(8,128)(2,1)} %c_ref.3, ...), custom_call_target="tpu_custom_call" | custom-call | tf_op jit(solution)/shard_map/grad/pallas_call | solution.py:358
  78.2 2.8 %collective-permute-start.15 = (bf16[16,2048]{1,0:T(8,128)(2,1)}, bf16[16,2048]{1,0:T(8,128)(2,1)S(1)}, u32[]{:S(2)}, u32[]{:S(2)}) collective-permute-start(bf16[16,2048]{1,0:T(8,128)(2,1)} %get-tuple-element.26), channel_id=1, source_target_pairs={{0,96},{4,100},{8,104},{12,108},{16,112},{20,116},{24,120},{28,124... | collective-permute-start | bytes 196616 | tf_op jit(solution)/shard_map/ppermute | solution.py:333
  80.9 0.0 collective-permute-start.14
  80.9 2.4 %collective-permute-start.13 = (bf16[16,2048]{1,0:T(8,128)(2,1)}, bf16[16,2048]{1,0:T(8,128)(2,1)S(1)}, u32[]{:S(2)}, u32[]{:S(2)}) collective-permute-start(bf16[16,2048]{1,0:T(8,128)(2,1)} %get-tuple-element.26), channel_id=1, source_target_pairs={{0,104},{4,108},{8,112},{12,116},{16,120},{20,124},{24,0},{28,4},{... | collective-permute-start | bytes 196616 | tf_op jit(solution)/shard_map/ppermute | solution.py:333
  83.4 1.3 %collective-permute-start.12 = (bf16[16,2048]{1,0:T(8,128)(2,1)}, bf16[16,2048]{1,0:T(8,128)(2,1)S(1)}, u32[]{:S(2)}, u32[]{:S(2)}) collective-permute-start(bf16[16,2048]{1,0:T(8,128)(2,1)} %get-tuple-element.26), channel_id=1, source_target_pairs={{0,108},{4,112},{8,116},{12,120},{16,124},{20,0},{24,4},{28,8},{32... | collective-permute-start | bytes 196616 | tf_op jit(solution)/shard_map/ppermute | solution.py:333
  84.7 2.6 %collective-permute-start.11 = (bf16[16,2048]{1,0:T(8,128)(2,1)}, bf16[16,2048]{1,0:T(8,128)(2,1)S(1)}, u32[]{:S(2)}, u32[]{:S(2)}) collective-permute-start(bf16[16,2048]{1,0:T(8,128)(2,1)} %get-tuple-element.26), channel_id=1, source_target_pairs={{0,112},{4,116},{8,120},{12,124},{16,0},{20,4},{24,8},{28,12},{32,... | collective-permute-start | bytes 196616 | tf_op jit(solution)/shard_map/ppermute | solution.py:333
  87.3 1.0 collective-permute-start.10
  88.3 2.1 %collective-permute-start.9 = (bf16[16,2048]{1,0:T(8,128)(2,1)}, bf16[16,2048]{1,0:T(8,128)(2,1)S(1)}, u32[]{:S(2)}, u32[]{:S(2)}) collective-permute-start(bf16[16,2048]{1,0:T(8,128)(2,1)} %get-tuple-element.26), channel_id=1, source_target_pairs={{0,120},{4,124},{8,0},{12,4},{16,8},{20,12},{24,16},{28,20},{32,24... | collective-permute-start | bytes 196616 | tf_op jit(solution)/shard_map/ppermute | solution.py:333
  90.5 1.3 %collective-permute-start.8 = (bf16[16,2048]{1,0:T(8,128)(2,1)}, bf16[16,2048]{1,0:T(8,128)(2,1)S(1)}, u32[]{:S(2)}, u32[]{:S(2)}) collective-permute-start(bf16[16,2048]{1,0:T(8,128)(2,1)} %get-tuple-element.26), channel_id=1, source_target_pairs={{0,124},{4,0},{8,4},{12,8},{16,12},{20,16},{24,20},{28,24},{32,28}... | collective-permute-start | bytes 196616 | tf_op jit(solution)/shard_map/ppermute | solution.py:333
  91.7 6.6 %outputs.1 = (bf16[512,2048]{1,0:T(8,128)(2,1)}, bf16[512,2048]{1,0:T(8,128)(2,1)}) custom-call(f32[512,2048]{1,0:T(8,128)} %get-tuple-element.22.conv_ref, bf16[512,2048]{1,0:T(8,128)(2,1)} %q_ref.3, bf16[512,2048]{1,0:T(8,128)(2,1)} %c_ref.3, f32[1,2048]{1,0:T(1,128)} %bitcast.19, f32[512,128]{1,0:T(8,128)} %broadcast_in_dim.48.inv_ref, ...), custom_call_target="tpu_custom_call" | custom-call | flops 8388608 | bytes 12582912 | tf_op jit(solution)/shard_map/outputs/pallas_call | solution.py:363
  98.4 0.0 collective-permute-done.12.refs_4_
  98.4 0.0 collective-permute-done.10.refs_2_
  98.5 0.0 collective-permute-done.9.refs_1_
  98.5 0.5 copy-done.10
  99.0 0.0 copy-done.12
  99.1 0.0 copy-done.14
  99.1 0.0 copy-done.15
  99.1 0.0 copy-done.16
  99.1 12.1 %last.1 = (bf16[512,2048]{1,0:T(8,128)(2,1)}, bf16[512,2048]{1,0:T(8,128)(2,1)}) custom-call(s32[1,1]{1,0:T(1,128)} %bitcast.here_ref, s32[16]{0:T(128)} %len_ref.7, f32[1,8]{1,0:T(1,128)} %get-tuple-element.38.keep_ref, bf16[16,2048]{1,0:T(8,128)(2,1)} %copy-done.16, bf16[16,2048]{1,0:T(8,128)(2,1)} %copy-done.15, bf16[16,2048]{1,0:T(8,128)(2,1)} %copy-done.14, ...), custom_call_target="tpu_custom_call" | custom-call | tf_op jit(solution)/shard_map/last/pallas_call | solution.py:368
  (45 shorter events, 0.2 us)
Async XLA Ops:
  2.9 19.0 %copy-start = (f32[128,16]{0,1:T(8,128)S(1)}, f32[128,16]{0,1:T(8,128)}, u32[]{:S(2)}) copy-start(f32[128,16]{0,1:T(8,128)} %param.13) | copy-start | bytes 24580
  2.9 19.0 %copy-start.18 = (s32[16]{0:T(128)S(1)}, s32[16]{0:T(128)}, u32[]{:S(2)}) copy-start(s32[16]{0:T(128)} %len_ref.7) | copy-start | bytes 196
  2.9 19.6 %copy-start.17 = (f32[128,16]{0,1:T(8,128)S(1)}, f32[128,16]{0,1:T(8,128)}, u32[]{:S(2)}) copy-start(f32[128,16]{0,1:T(8,128)} %param.12) | copy-start | bytes 24580
  10.8 13.9 %collective-permute-start.7 = (bf16[16,2048]{1,0:T(8,128)(2,1)}, bf16[16,2048]{1,0:T(8,128)(2,1)S(1)}, u32[]{:S(2)}, u32[]{:S(2)}) collective-permute-start(bf16[16,2048]{1,0:T(8,128)(2,1)} %get-tuple-element.18), channel_id=1, source_target_pairs={{0,32},{4,36},{8,40},{12,44},{16,48},{20,52},{24,56},{28,60},{32,6... | collective-permute-start | bytes 196616 | tf_op jit(solution)/shard_map/ppermute | solution.py:333
  12.5 12.2 %collective-permute-start.6 = (bf16[16,2048]{1,0:T(8,128)(2,1)}, bf16[16,2048]{1,0:T(8,128)(2,1)S(1)}, u32[]{:S(2)}, u32[]{:S(2)}) collective-permute-start(bf16[16,2048]{1,0:T(8,128)(2,1)} %get-tuple-element.18), channel_id=1, source_target_pairs={{0,28},{4,32},{8,36},{12,40},{16,44},{20,48},{24,52},{28,56},{32,6... | collective-permute-start | bytes 196616 | tf_op jit(solution)/shard_map/ppermute | solution.py:333
  15.7 9.1 %collective-permute-start.5 = (bf16[16,2048]{1,0:T(8,128)(2,1)}, bf16[16,2048]{1,0:T(8,128)(2,1)S(1)}, u32[]{:S(2)}, u32[]{:S(2)}) collective-permute-start(bf16[16,2048]{1,0:T(8,128)(2,1)} %get-tuple-element.18), channel_id=1, source_target_pairs={{0,24},{4,28},{8,32},{12,36},{16,40},{20,44},{24,48},{28,52},{32,5... | collective-permute-start | bytes 196616 | tf_op jit(solution)/shard_map/ppermute | solution.py:333
  17.1 18.9 %collective-permute-start.4 = (bf16[16,2048]{1,0:T(8,128)(2,1)}, bf16[16,2048]{1,0:T(8,128)(2,1)S(1)}, u32[]{:S(2)}, u32[]{:S(2)}) collective-permute-start(bf16[16,2048]{1,0:T(8,128)(2,1)} %get-tuple-element.18), channel_id=1, source_target_pairs={{0,20},{4,24},{8,28},{12,32},{16,36},{20,40},{24,44},{28,48},{32,5... | collective-permute-start | bytes 196616 | tf_op jit(solution)/shard_map/ppermute | solution.py:333
  18.2 17.8 %collective-permute-start.3 = (bf16[16,2048]{1,0:T(8,128)(2,1)}, bf16[16,2048]{1,0:T(8,128)(2,1)S(1)}, u32[]{:S(2)}, u32[]{:S(2)}) collective-permute-start(bf16[16,2048]{1,0:T(8,128)(2,1)} %get-tuple-element.18), channel_id=1, source_target_pairs={{0,16},{4,20},{8,24},{12,28},{16,32},{20,36},{24,40},{28,44},{32,4... | collective-permute-start | bytes 196616 | tf_op jit(solution)/shard_map/ppermute | solution.py:333
  24.7 11.4 %copy-start.1 = (bf16[16,2048]{1,0:T(8,128)(2,1)}, bf16[16,2048]{1,0:T(8,128)(2,1)S(1)}, u32[]{:S(2)}) copy-start(bf16[16,2048]{1,0:T(8,128)(2,1)S(1)} %collective-permute-done.7.refs_7_) | copy-start | bytes 196612
  24.7 11.3 %collective-permute-start.2 = (bf16[16,2048]{1,0:T(8,128)(2,1)}, bf16[16,2048]{1,0:T(8,128)(2,1)S(1)}, u32[]{:S(2)}, u32[]{:S(2)}) collective-permute-start(bf16[16,2048]{1,0:T(8,128)(2,1)} %get-tuple-element.18), channel_id=1, source_target_pairs={{0,12},{4,16},{8,20},{12,24},{16,28},{20,32},{24,36},{28,40},{32,4... | collective-permute-start | bytes 196616 | tf_op jit(solution)/shard_map/ppermute | solution.py:333
  24.7 11.4 %copy-start.2 = (bf16[16,2048]{1,0:T(8,128)(2,1)}, bf16[16,2048]{1,0:T(8,128)(2,1)S(1)}, u32[]{:S(2)}) copy-start(bf16[16,2048]{1,0:T(8,128)(2,1)S(1)} %collective-permute-done.6.refs_6_) | copy-start | bytes 196612
  24.8 11.3 %collective-permute-start.1 = (bf16[16,2048]{1,0:T(8,128)(2,1)}, bf16[16,2048]{1,0:T(8,128)(2,1)S(1)}, u32[]{:S(2)}, u32[]{:S(2)}) collective-permute-start(bf16[16,2048]{1,0:T(8,128)(2,1)} %get-tuple-element.18), channel_id=1, source_target_pairs={{0,8},{4,12},{8,16},{12,20},{16,24},{20,28},{24,32},{28,36},{32,40... | collective-permute-start | bytes 196616 | tf_op jit(solution)/shard_map/ppermute | solution.py:333
  24.8 11.3 %copy-start.3 = (bf16[16,2048]{1,0:T(8,128)(2,1)}, bf16[16,2048]{1,0:T(8,128)(2,1)S(1)}, u32[]{:S(2)}) copy-start(bf16[16,2048]{1,0:T(8,128)(2,1)S(1)} %collective-permute-done.5.refs_5_) | copy-start | bytes 196612
  24.9 11.2 %collective-permute-start = (bf16[16,2048]{1,0:T(8,128)(2,1)}, bf16[16,2048]{1,0:T(8,128)(2,1)S(1)}, u32[]{:S(2)}, u32[]{:S(2)}) collective-permute-start(bf16[16,2048]{1,0:T(8,128)(2,1)} %get-tuple-element.18), channel_id=1, source_target_pairs={{0,4},{4,8},{8,12},{12,16},{16,20},{20,24},{24,28},{28,32},{32,36}... | collective-permute-start | bytes 196616 | tf_op jit(solution)/shard_map/ppermute | solution.py:333
  36.0 0.6 copy-start.4
  36.0 0.6 copy-start.5
  36.0 0.6 copy-start.8
  36.1 0.6 copy-start.11
  36.1 0.6 copy-start.13
  78.2 9.1 %collective-permute-start.15 = (bf16[16,2048]{1,0:T(8,128)(2,1)}, bf16[16,2048]{1,0:T(8,128)(2,1)S(1)}, u32[]{:S(2)}, u32[]{:S(2)}) collective-permute-start(bf16[16,2048]{1,0:T(8,128)(2,1)} %get-tuple-element.26), channel_id=1, source_target_pairs={{0,96},{4,100},{8,104},{12,108},{16,112},{20,116},{24,120},{28,124... | collective-permute-start | bytes 196616 | tf_op jit(solution)/shard_map/ppermute | solution.py:333
  80.9 7.4 %collective-permute-start.14 = (bf16[16,2048]{1,0:T(8,128)(2,1)}, bf16[16,2048]{1,0:T(8,128)(2,1)S(1)}, u32[]{:S(2)}, u32[]{:S(2)}) collective-permute-start(bf16[16,2048]{1,0:T(8,128)(2,1)} %get-tuple-element.26), channel_id=1, source_target_pairs={{0,100},{4,104},{8,108},{12,112},{16,116},{20,120},{24,124},{28,0}... | collective-permute-start | bytes 196616 | tf_op jit(solution)/shard_map/ppermute | solution.py:333
  80.9 9.5 %collective-permute-start.13 = (bf16[16,2048]{1,0:T(8,128)(2,1)}, bf16[16,2048]{1,0:T(8,128)(2,1)S(1)}, u32[]{:S(2)}, u32[]{:S(2)}) collective-permute-start(bf16[16,2048]{1,0:T(8,128)(2,1)} %get-tuple-element.26), channel_id=1, source_target_pairs={{0,104},{4,108},{8,112},{12,116},{16,120},{20,124},{24,0},{28,4},{... | collective-permute-start | bytes 196616 | tf_op jit(solution)/shard_map/ppermute | solution.py:333
  83.4 15.0 %collective-permute-start.12 = (bf16[16,2048]{1,0:T(8,128)(2,1)}, bf16[16,2048]{1,0:T(8,128)(2,1)S(1)}, u32[]{:S(2)}, u32[]{:S(2)}) collective-permute-start(bf16[16,2048]{1,0:T(8,128)(2,1)} %get-tuple-element.26), channel_id=1, source_target_pairs={{0,108},{4,112},{8,116},{12,120},{16,124},{20,0},{24,4},{28,8},{32... | collective-permute-start | bytes 196616 | tf_op jit(solution)/shard_map/ppermute | solution.py:333
  84.7 13.7 %collective-permute-start.11 = (bf16[16,2048]{1,0:T(8,128)(2,1)}, bf16[16,2048]{1,0:T(8,128)(2,1)S(1)}, u32[]{:S(2)}, u32[]{:S(2)}) collective-permute-start(bf16[16,2048]{1,0:T(8,128)(2,1)} %get-tuple-element.26), channel_id=1, source_target_pairs={{0,112},{4,116},{8,120},{12,124},{16,0},{20,4},{24,8},{28,12},{32,... | collective-permute-start | bytes 196616 | tf_op jit(solution)/shard_map/ppermute | solution.py:333
  87.3 11.1 %copy-start.6 = (bf16[16,2048]{1,0:T(8,128)(2,1)}, bf16[16,2048]{1,0:T(8,128)(2,1)S(1)}, u32[]{:S(2)}) copy-start(bf16[16,2048]{1,0:T(8,128)(2,1)S(1)} %collective-permute-done.15.refs_7_) | copy-start | bytes 196612
  87.3 11.2 %collective-permute-start.10 = (bf16[16,2048]{1,0:T(8,128)(2,1)}, bf16[16,2048]{1,0:T(8,128)(2,1)S(1)}, u32[]{:S(2)}, u32[]{:S(2)}) collective-permute-start(bf16[16,2048]{1,0:T(8,128)(2,1)} %get-tuple-element.26), channel_id=1, source_target_pairs={{0,116},{4,120},{8,124},{12,0},{16,4},{20,8},{24,12},{28,16},{32,2... | collective-permute-start | bytes 196616 | tf_op jit(solution)/shard_map/ppermute | solution.py:333
  88.3 10.1 %copy-start.7 = (bf16[16,2048]{1,0:T(8,128)(2,1)}, bf16[16,2048]{1,0:T(8,128)(2,1)S(1)}, u32[]{:S(2)}) copy-start(bf16[16,2048]{1,0:T(8,128)(2,1)S(1)} %collective-permute-done.14.refs_6_) | copy-start | bytes 196612
  88.3 10.1 %collective-permute-start.9 = (bf16[16,2048]{1,0:T(8,128)(2,1)}, bf16[16,2048]{1,0:T(8,128)(2,1)S(1)}, u32[]{:S(2)}, u32[]{:S(2)}) collective-permute-start(bf16[16,2048]{1,0:T(8,128)(2,1)} %get-tuple-element.26), channel_id=1, source_target_pairs={{0,120},{4,124},{8,0},{12,4},{16,8},{20,12},{24,16},{28,20},{32,24... | collective-permute-start | bytes 196616 | tf_op jit(solution)/shard_map/ppermute | solution.py:333
  90.5 7.9 %copy-start.9 = (bf16[16,2048]{1,0:T(8,128)(2,1)}, bf16[16,2048]{1,0:T(8,128)(2,1)S(1)}, u32[]{:S(2)}) copy-start(bf16[16,2048]{1,0:T(8,128)(2,1)S(1)} %collective-permute-done.13.refs_5_) | copy-start | bytes 196612
  90.5 8.0 %collective-permute-start.8 = (bf16[16,2048]{1,0:T(8,128)(2,1)}, bf16[16,2048]{1,0:T(8,128)(2,1)S(1)}, u32[]{:S(2)}, u32[]{:S(2)}) collective-permute-start(bf16[16,2048]{1,0:T(8,128)(2,1)} %get-tuple-element.26), channel_id=1, source_target_pairs={{0,124},{4,0},{8,4},{12,8},{16,12},{20,16},{24,20},{28,24},{32,28}... | collective-permute-start | bytes 196616 | tf_op jit(solution)/shard_map/ppermute | solution.py:333
  98.4 0.6 copy-start.10
  98.4 0.6 copy-start.12
  98.4 0.6 copy-start.14
  98.5 0.7 copy-start.15
  98.5 0.6 copy-start.16

commit v2 on v1

v2 whole, which is shorter than its diff:
```python
import functools

import jax
import jax.numpy as jnp
from jax import lax
from jax.experimental import pallas as pl
from jax.experimental.pallas import tpu as pltpu
from jax.sharding import PartitionSpec as P

C = 64
W = 128
LB = 512
G = 16
R = 16
NG = W // G
DOCS = 16
REACH = 4096
HOP = 4
DEPTH = C + 3 * R
EPS = 1e-6
f32, bf16, i32 = jnp.float32, jnp.bfloat16, jnp.int32
VLIM = 61 * 1024 * 1024


def dot(a, b):
    return jnp.dot(a, b, preferred_element_type=f32)


def iota(rows, axis):
    return lax.broadcasted_iota(i32, (rows, W), axis)


def turn(x, lanes):
    return pltpu.roll(x, lanes % W, 1)


def swap_blocks(parts):
    parts = list(parts)
    blk = iota(parts[0].shape[0], 1) // G
    bit = 1
    while bit < NG:
        low = (blk & bit) == 0
        for m in range(NG):
            if not m & bit:
                a, b = parts[m], parts[m | bit]
                parts[m] = jnp.where(low, a, turn(b, G * bit))
                parts[m | bit] = jnp.where(low, turn(a, -G * bit), b)
        bit *= 2
    return parts


def fan_out(x):
    blk = iota(x.shape[0], 1) // G
    parts, bit = [x], NG // 2
    while bit:
        low = (blk & bit) == 0
        parts = [
            y
            for x in parts
            for y in (jnp.where(low, x, turn(x, G * bit)), jnp.where(low, turn(x, -G * bit), x))
        ]
        bit //= 2
    return parts


def docs_at(places, len_ref):
    found, start = jnp.full(places.shape, -1, i32), i32(0)
    for n in range(DOCS):
        found += (places >= start).astype(i32)
        start += len_ref[n]
    return found


def chunk_places(here_ref, rows):
    return here_ref[0, 0] * (C * NG) + (iota(rows, 1) // G) * C


def spread_rates(rate_ref, rate_out_ref):
    groups = rate_ref.shape[0]
    width = rate_out_ref.shape[1]
    row = lax.broadcasted_iota(i32, (groups, width), 0)
    lane = lax.broadcasted_iota(i32, (groups, width), 1)
    pick = (row == (pl.program_id(0) * width + lane) // G).astype(f32)
    rate_out_ref[...] = lax.dot_general(
        rate_ref[...], pick, (((0,), (0,)), ((), ())), precision=lax.Precision.HIGHEST, preferred_element_type=f32
    )


def put_masks(here_ref, len_ref, reach_ref, join_ref, way):
    @pl.when(pl.program_id(0) == 0)
    def _():
        reach, joins, into = state_masks(here_ref, len_ref, way)
        reach_ref[...] = reach
        for n, join in enumerate(joins + [into]):
            join_ref[n] = join

    return reach_ref[...], [join_ref[n] for n in range(3)], join_ref[3]


def state_masks(here_ref, len_ref, way):
    blk = iota(R, 1) // G
    base = chunk_places(here_ref, R)
    tokens = docs_at(chunk_places(here_ref, C) + iota(C, 0), len_ref)
    if way > 0:
        end, enter = C - 1, 0
        order = blk
    else:
        end, enter = 0, C - 1
        order = NG - 1 - blk
    ends = docs_at(chunk_places(here_ref, C) + end, len_ref)
    reach = (tokens == ends).astype(f32).astype(bf16)
    own = docs_at(base + end, len_ref)
    joins = []
    for n in (1, 2, 4):
        there = docs_at(base + end - way * n * C, len_ref)
        joins.append(((own == there) & (order >= n)).astype(f32))
    prior = docs_at(base + enter - way, len_ref)
    into = ((docs_at(base + enter, len_ref) == prior) & (order >= 1)).astype(f32)
    return reach, joins, into


def chunk_states(z_ref, rates, masks, way):
    reach, joins, into = masks
    passes = LB // W
    lane = iota(R, 1).astype(f32)
    blk = iota(R, 1) // G
    away = (C - 1.0) - lane if way > 0 else lane
    rows = jnp.concatenate([rates[:, s * W : (s + 1) * W] for s in range(passes)], axis=0)
    spread = fan_out(rows)
    order = [(s, g) for s in range(passes) for g in range(NG)]
    rate = jnp.concatenate([spread[g][s * R : (s + 1) * R] for s, g in order], axis=0)
    fall = jnp.exp(-rate * jnp.concatenate([away] * len(order), axis=0))[:, :C]
    hi = fall.astype(bf16)
    lo = (fall - hi.astype(f32)).astype(bf16)
    states = []
    for n in range(len(order)):
        at = slice(n * R, (n + 1) * R)
        both = dot(jnp.concatenate([hi[at], lo[at]], axis=0), z_ref[n * C : (n + 1) * C, :] * reach)
        states.append(both[:R] + both[R:])
    decay = jnp.exp(-rate * C)
    for n, join in zip((1, 2, 4), joins):
        scales = [decay[k * R : (k + 1) * R] * join for k in range(len(order))]
        states = [x + scale * turn(x, way * n * G) for x, scale in zip(states, scales)]
        decay *= decay
    entries = [into * turn(x, way * G) for x in states]
    end = NG - 1 if way > 0 else 0
    last = []
    for s in range(passes):
        row = jnp.zeros((R, W), f32)
        for g in range(NG):
            row = jnp.where(blk == g, turn(states[s * NG + g], (g - end) * G), row)
        last.append(row)
    return entries, last


def put_states(z_ref, ent_ref, own_ref, rates, masks, way):
    entries, last = chunk_states(z_ref, rates, masks, way)
    for n, entry in enumerate(entries):
        ent_ref[n * R : (n + 1) * R, :] = entry
    for s, row in enumerate(last):
        own_ref[:, s * W : (s + 1) * W] = row.astype(bf16)


def first_kernel(here_ref, len_ref, k_ref, v_ref, rate_ref, z_ref, ent_ref, own_ref, rates_ref, reach_ref, join_ref):
    spread_rates(rate_ref, rates_ref)
    masks = put_masks(here_ref, len_ref, reach_ref, join_ref, 1)
    for s in range(LB // W):
        at = slice(s * W, (s + 1) * W)
        x = (k_ref[:, at].astype(f32) * v_ref[:, at].astype(f32)).astype(bf16)
        z = swap_blocks([x[m * C : (m + 1) * C] for m in range(NG)])
        for g in range(NG):
            n = s * NG + g
            z_ref[n * C : (n + 1) * C, :] = z[g]
    put_states(z_ref, ent_ref, own_ref, rates_ref[...], masks, 1)


def table_kernel(tapf_ref, tapb_ref, rate_ref, res_ref, lf_ref, lb_ref):
    lane, row = iota(C, 1), iota(C, 0).astype(f32)
    for g in range(LB // G):
        at = slice(g, g + 1)
        rate = jnp.broadcast_to(rate_ref[at, :], (C, W))
        res = jnp.broadcast_to(res_ref[at, :], (C, W))
        for tap_ref, out_ref, lag in ((tapf_ref, lf_ref, row + 1.0), (tapb_ref, lb_ref, C - row)):
            taps = jnp.broadcast_to(tap_ref[at, :], (C, W))
            square = pltpu.roll(taps, 0, 1, stride=1, stride_axis=0)
            carry = res * jnp.exp(-rate * lag)
            hi = carry.astype(bf16).astype(f32)
            carry = jnp.where(lane < C + 2 * R, hi, jnp.where(lane < DEPTH, carry - hi, 0.0))
            out_ref[g * C : (g + 1) * C, :] = jnp.where(lane < C, square, carry).astype(bf16)


def segments(here_ref, len_ref, way):
    first = chunk_places(here_ref, C)
    tokens = docs_at(first + iota(C, 0), len_ref)
    if way > 0:
        return tokens - docs_at(first, len_ref)
    return docs_at(first + (C - 1), len_ref) - tokens


def local_kernel(way, here_ref, len_ref, z_ref, ent_ref, left_ref, y_ref, seg_ref, o_ref):
    @pl.when(pl.program_id(0) == 0)
    def _():
        seg_ref[...] = segments(here_ref, len_ref, way)

    seg = seg_ref[...]
    top = jnp.max(seg)
    m0, m1 = (seg == 0).astype(f32).astype(bf16), (seg == 1).astype(f32).astype(bf16)
    none = jnp.zeros((3 * R, W), bf16)
    for n in range(LB // G):
        entry = ent_ref[n * R : (n + 1) * R, :]
        hi = entry.astype(bf16)
        lo = (entry - hi.astype(f32)).astype(bf16)
        z = z_ref[n * C : (n + 1) * C, :]
        right = jnp.concatenate(
            [jnp.concatenate([z * m0, hi, lo, hi], axis=0), jnp.concatenate([z * m1, none], axis=0)], axis=1
        )
        y = dot(left_ref[n * C : (n + 1) * C, :DEPTH], right)
        o_ref[n] = jnp.where(seg == 0, y[:, :W], y[:, W:]).astype(bf16)

    @pl.when(top > 1)
    def _():
        def again(p, carry):
            mask = (seg == p).astype(f32).astype(bf16)
            for n in range(LB // G):
                square = left_ref[n * C : (n + 1) * C, :C]
                o_ref[n] = jnp.where(seg == p, dot(square, z_ref[n * C : (n + 1) * C, :] * mask), o_ref[n].astype(f32)).astype(bf16)
            return carry

        lax.fori_loop(2, top + 1, again, 0)

    for s in range(LB // W):
        for m, part in enumerate(swap_blocks([o_ref[s * NG + g] for g in range(NG)])):
            y_ref[m * C : (m + 1) * C, s * W : (s + 1) * W] = part


def edge_lags(here_ref, len_ref, flat_ref, s, rows, way):
    start = here_ref[0, 0] * rows
    begin, head, tail = i32(0), i32(1 << 30), i32(0)
    for n in range(DOCS):
        head = jnp.where(begin >= start, jnp.minimum(head, begin), head)
        tail = jnp.where(begin <= start + rows, begin, tail)
        begin += len_ref[n]
    lanes = slice(s * W, (s + 1) * W)
    rate, res = flat_ref[0:1, lanes], flat_ref[1:2, lanes]
    row = iota(C, 0)
    within = row.astype(f32)
    near = res * jnp.exp(-rate * (within + 1.0 if way > 0 else C - within))
    out = []
    for m in range(rows // C):
        token = start + m * C + row
        reached = token < head if way > 0 else token >= tail
        chunks = m if way > 0 else rows // C - 1 - m
        out.append(jnp.where(reached, near * jnp.exp(-rate * (C * chunks)), 0.0).astype(bf16))
    return jnp.concatenate(out, axis=0)


def arrived(here_ref, len_ref, keep_ref, near_ref, far_ref, rates_ref, flat_ref, s, rows, way):
    at = slice(s * W, (s + 1) * W)
    span = jnp.exp(-rates_ref[:, at] * (HOP * rows))
    total = keep_ref[0, 0] * near_ref[:, at].astype(f32) + keep_ref[0, 1] * (span * far_ref[:, at].astype(f32))
    diag = (iota(W, 0) // R) == (iota(W, 1) // G)
    square = jnp.where(diag, jnp.concatenate([total] * NG, axis=0), 0.0)
    hi = square.astype(bf16)
    lo = (square - hi.astype(f32)).astype(bf16)
    lag = edge_lags(here_ref, len_ref, flat_ref, s, rows, way)
    return dot(jnp.concatenate([lag, lag], axis=1), jnp.concatenate([hi, lo], axis=0))


def gate_kernel(
    here_ref, len_ref, keep_ref, near_ref, far_ref, rate_ref, flat_ref, y_ref, q_ref, c_ref, gain_ref,
    conv_ref, stat_ref, acc_ref,
):
    step = pl.program_id(0)
    rows = y_ref.shape[0]

    @pl.when(step == 0)
    def _():
        acc_ref[...] = jnp.zeros_like(acc_ref)

    for s in range(LB // W):
        at = slice(s * W, (s + 1) * W)
        carry = arrived(here_ref, len_ref, keep_ref, near_ref, far_ref, rate_ref, flat_ref, s, rows, 1)
        conv_ref[:, at] = (y_ref[:, at].astype(f32) + carry).astype(bf16)
    for m in range(rows // C):
        part = slice(m * C, (m + 1) * C)
        squares, inner = acc_ref[part, :W], acc_ref[part, W:]
        for s in range(LB // W):
            at = slice(s * W, (s + 1) * W)
            gated = q_ref[part, at].astype(f32) * conv_ref[part, at].astype(f32)
            squares += gated * gated
            inner += c_ref[part, at].astype(f32) * gain_ref[:, at] * gated
        acc_ref[part, :W] = squares
        acc_ref[part, W:] = inner

    @pl.when(step == pl.num_programs(0) - 1)
    def _():
        row = lax.broadcasted_iota(i32, (8, 2 * W), 0)
        lane = lax.broadcasted_iota(i32, (8, 2 * W), 1)
        pick = (row == lane // W).astype(f32)
        stat_ref[...] = lax.dot_general(
            pick, acc_ref[...], (((1,), (1,)), ((), ())), precision=lax.Precision.HIGHEST, preferred_element_type=f32
        )


def grad_kernel(
    total_width, here_ref, len_ref, s0_ref, s1_ref, s2_ref, s3_ref, conv_ref, q_ref, c_ref, gain_ref, rate_ref,
    out_ref, gq_ref, z_ref, ent_ref, own_ref, rates_ref, inv_ref, mean_ref, reach_ref, join_ref,
):
    spread_rates(rate_ref, rates_ref)

    @pl.when(pl.program_id(0) == 0)
    def _():
        stat = s0_ref[...] + s1_ref[...] + s2_ref[...] + s3_ref[...]
        row = iota(8, 0)

        def column(n):
            pick = (row == n).astype(f32)
            return lax.dot_general(
                stat, pick, (((0,), (0,)), ((), ())), precision=lax.Precision.HIGHEST, preferred_element_type=f32
            )

        inv = lax.rsqrt(column(0) / total_width + EPS)
        inv_ref[...] = inv
        mean_ref[...] = inv * column(1) / total_width

    masks = put_masks(here_ref, len_ref, reach_ref, join_ref, -1)
    for s in range(LB // W):
        at = slice(s * W, (s + 1) * W)
        gain = gain_ref[:, at]
        parts = []
        for m in range(NG):
            rows = slice(m * C, (m + 1) * C)
            inv = inv_ref[rows, :]
            q = q_ref[rows, at].astype(f32)
            conv = conv_ref[rows, at].astype(f32)
            normed = q * conv * inv
            out_ref[rows, at] = (normed * gain).astype(bf16)
            grad_gated = inv * (c_ref[rows, at].astype(f32) * gain - normed * mean_ref[rows, :])
            gq_ref[rows, at] = (grad_gated * conv).astype(bf16)
            parts.append((grad_gated * q).astype(bf16))
        z = swap_blocks(parts)
        for g in range(NG):
            n = s * NG + g
            z_ref[n * C : (n + 1) * C, :] = z[g]
    put_states(z_ref, ent_ref, own_ref, rates_ref[...], masks, -1)


def last_kernel(here_ref, len_ref, keep_ref, near_ref, far_ref, rate_ref, flat_ref, y_ref, k_ref, v_ref, gk_ref, gv_ref):
    rows = y_ref.shape[0]
    for s in range(LB // W):
        at = slice(s * W, (s + 1) * W)
        carry = arrived(here_ref, len_ref, keep_ref, near_ref, far_ref, rate_ref, flat_ref, s, rows, -1)
        grad = y_ref[:, at].astype(f32) + carry
        gk_ref[:, at] = (grad * v_ref[:, at].astype(f32)).astype(bf16)
        gv_ref[:, at] = (grad * k_ref[:, at].astype(f32)).astype(bf16)


def doc_index(places, doc_lengths):
    doc_ends = jnp.cumsum(doc_lengths)
    doc_starts = doc_ends - doc_lengths
    return jnp.sum((doc_starts[None, :] <= places[:, None]).astype(i32), axis=1) - 1


def local(query_gate, key_branch, value_branch, norm_gain, residues, decay_rate, doc_lengths, cotangent):
    rows, width = query_gate.shape
    groups = residues.shape[0]
    devices = lax.axis_size("seq")
    here = lax.axis_index("seq")
    total_width = width * lax.axis_size("ch")
    here_arr = here.astype(i32).reshape(1, 1)

    offset = jnp.arange(REACH // rows + 1, dtype=i32)
    docs = doc_index(jnp.concatenate([(here - offset + 1) * rows - 1, (here + offset) * rows]), doc_lengths)
    ends, begins = docs[: len(offset)], docs[len(offset) :]

    def keep(edge, from_, to, way):
        inside = here >= to if way > 0 else here + to < devices
        return ((edge[from_] == edge[to]) & inside).astype(f32)

    keep_f = jnp.stack([keep(ends, 1, 1, 1), keep(ends, 1, 1 + HOP, 1)]).reshape(1, 2)
    keep_b = jnp.stack([keep(begins, 1, 1, -1), keep(begins, 1, 1 + HOP, -1)]).reshape(1, 2)

    rates = jnp.repeat(decay_rate.T, G, axis=1)
    lane = jnp.arange(W)

    def taps(lags):
        h = jnp.sum(residues[:, :, None] * jnp.exp(-decay_rate[:, :, None] * lags.astype(f32)), axis=1)
        return jnp.where(lags < C, h, 0.0)

    tap_f, tap_b = taps((W - lane) % W), taps(lane)
    rate_rep, res_rep = jnp.tile(decay_rate, (1, NG)), jnp.tile(residues, (1, NG))
    flat = jnp.stack([decay_rate.reshape(groups * R), residues.reshape(groups * R)])
    gain = norm_gain.reshape(1, width)

    grid = (width // LB,)
    wide = pl.BlockSpec((rows, LB), lambda i: (0, i))
    modes = pl.BlockSpec((R, LB), lambda i: (0, i))
    stacked = pl.BlockSpec((LB // G * C, W), lambda i: (i, 0))
    states = pl.BlockSpec((LB // G * R, W), lambda i: (i, 0))
    tapped = pl.BlockSpec((LB // G, W), lambda i: (i, 0))
    row1 = pl.BlockSpec((1, LB), lambda i: (0, i))
    small = pl.BlockSpec(memory_space=pltpu.SMEM)
    params = pltpu.CompilerParams(vmem_limit_bytes=VLIM, dimension_semantics=("arbitrary",))

    def shaped(dtype, *shape):
        return jax.ShapeDtypeStruct(shape, dtype)

    full16 = shaped(bf16, rows, width)
    stack16 = shaped(bf16, groups * C, W)
    entries, ends_shape = shaped(f32, groups * R, W), shaped(bf16, R, width)
    rates_of = pl.BlockSpec((groups, R), lambda i: (0, 0))
    kept = [pltpu.VMEM((C, W), bf16), pltpu.VMEM((4, R, W), f32)]
    flat2 = pl.BlockSpec((2, LB), lambda i: (0, i))
    stat_spec = pl.BlockSpec((8, rows), lambda i: (0, 0))

    def ring(x, axis, by):
        size = lax.axis_size(axis)
        return lax.ppermute(x, axis, [(i, (i + by) % size) for i in range(size)])

    def gather(own, way):
        return [own] + [ring(own, "seq", way * n) for n in range(1, HOP)]

    def pass_on(parts, beside, edge, way):
        parts, beside = lax.optimization_barrier((parts, beside))
        total, scale = 0.0, 1.0
        for n, part in enumerate(parts):
            total += keep(edge, 0, n, way) * scale * part.astype(f32)
            scale *= jnp.exp(-rates * rows)
        total = total.astype(bf16)
        return beside, total, ring(total, "seq", way), ring(total, "seq", way * (1 + HOP))

    def within(z, ent, left, way):
        return pl.pallas_call(
            functools.partial(local_kernel, way), grid=grid, in_specs=[small, small, stacked, states, stacked],
            out_specs=wide, out_shape=full16, scratch_shapes=[pltpu.VMEM((C, W), i32), pltpu.VMEM((LB // G, C, W), bf16)],
            compiler_params=params, name="local",
            cost_estimate=pl.CostEstimate(flops=16 * rows * width, bytes_accessed=14 * rows * width, transcendentals=0),
        )(here_arr, doc_lengths, z, ent, left)

    z_f, ent_f, own_f = pl.pallas_call(
        first_kernel, grid=grid, in_specs=[small, small, wide, wide, rates_of], out_specs=[stacked, states, modes],
        out_shape=[stack16, entries, ends_shape], scratch_shapes=[pltpu.VMEM((R, LB), f32)] + kept,
        compiler_params=params, name="first",
    )(here_arr, doc_lengths, key_branch, value_branch, decay_rate)
    parts_f = gather(own_f, 1)
    left_f, left_b = pl.pallas_call(
        table_kernel, grid=grid, in_specs=[tapped] * 4, out_specs=[stacked] * 2,
        out_shape=[stack16] * 2, compiler_params=params, name="tables",
        cost_estimate=pl.CostEstimate(flops=8 * rows * width, bytes_accessed=12 * rows * width, transcendentals=0),
    )(tap_f, tap_b, rate_rep, res_rep)
    left_f, gathered, near_f, far_f = pass_on(parts_f, left_f, ends, 1)
    ent_f, _ = lax.optimization_barrier((ent_f, gathered))
    y_f = within(z_f, ent_f, left_f, 1)
    conv, stat = pl.pallas_call(
        gate_kernel, grid=grid, in_specs=[small] * 3 + [modes] * 3 + [flat2] + [wide] * 3 + [row1],
        out_specs=[wide, stat_spec], out_shape=[full16, shaped(f32, 8, rows)],
        scratch_shapes=[pltpu.VMEM((rows, 2 * W), f32)], compiler_params=params, name="gate",
    )(here_arr, doc_lengths, keep_f, near_f, far_f, rates, flat, y_f, query_gate, cotangent, gain)
    stats = [stat] + [ring(stat, "ch", n) for n in range(1, 4)]
    layer_out, grad_query, z_b, ent_b, own_b = pl.pallas_call(
        functools.partial(grad_kernel, total_width), grid=grid,
        in_specs=[small, small] + [stat_spec] * 4 + [wide] * 3 + [row1, rates_of],
        out_specs=[wide, wide, stacked, states, modes],
        out_shape=[full16, full16, stack16, entries, ends_shape],
        scratch_shapes=[pltpu.VMEM((R, LB), f32)] + [pltpu.VMEM((rows, W), f32)] * 2 + kept,
        compiler_params=params, name="grad",
    )(here_arr, doc_lengths, *stats, conv, query_gate, cotangent, gain, decay_rate)
    parts_b = gather(own_b, -1)
    left_b, gathered, near_b, far_b = pass_on(parts_b, left_b, begins, -1)
    ent_b, _ = lax.optimization_barrier((ent_b, gathered))
    y_b = within(z_b, ent_b, left_b, -1)
    grad_key, grad_value = pl.pallas_call(
        last_kernel, grid=grid, in_specs=[small] * 3 + [modes] * 3 + [flat2] + [wide] * 3, out_specs=[wide, wide],
        out_shape=[full16, full16], compiler_params=params, name="last",
    )(here_arr, doc_lengths, keep_b, near_b, far_b, rates, flat, y_b, key_branch, value_branch)
    return layer_out, grad_query, grad_key, grad_value


def solution(mesh):
    tokens = P("seq", "ch")
    placed = (tokens, tokens, tokens, P("ch"), P("ch", None), P("ch", None), P(), tokens)
    return jax.shard_map(local, mesh=mesh, in_specs=placed, out_specs=(tokens,) * 4, check_vma=False)
```

time: 112 us -> 103 us (0.920)
  blocking collectives: 17.5 us -> 0 us
  between operations: 1.13 us -> 10.7 us
  starting transfers between devices: 25.5 us -> 21 us
  waiting for transfers between devices: 0.04 us -> 4.3 us
  local copies, waits for them, and re-layouts: 9.16 us -> 7.44 us
    psum x1 -> x0, blocking collectives: 17.5 us -> none  [local(): stat = lax.psum(stat, 'ch')]
    ppermute x16 -> x13, starting transfers between devices: 25.5 us -> 21 us  [ring(): return lax.ppermute(x, axis, [(i, (i + by) % size) for i in range(size)])]
    ppermute x16 -> x13, waiting for transfers between devices: 0.04 us -> 4.3 us  [ring(): return lax.ppermute(x, axis, [(i, (i + by) % size) for i in range(size)])]
    broadcast_in_dim x5 -> x1, local copies, waits for them, and re-layouts: 3.47 us -> 0.32 us  [local(): rates = jnp.repeat(decay_rate.T, G, axis=1)]
    unnamed x40 -> x30, local copies, waits for them, and re-layouts: 2.18 us -> 3.99 us
    pallas_call x1, Pallas kernels: 7.92 us -> 9.3 us  [local(): pl.pallas_call(first_kernel, grid=grid, in_specs=[small, small, wide, wid...]
    exp x1 -> x0, local copies, waits for them, and re-layouts: 1.28 us -> none  [local(): far = jnp.exp(-jnp.repeat(decay_rate.T, G, axis=1) * rows)]
    pallas_call x4 -> x5, Pallas kernels: 40.9 us -> 39.7 us  [the longest x2 15 us: within(): pl.pallas_call(functools.partial(local_kernel, way), grid=grid, in_specs=...]
  transfers between devices with their start and end apart: 16 -> 13, of which waited for: 0 -> 2; matrix products, arithmetic and copies ran while one was open for 7% -> 7% of each run, Pallas kernels for 11% -> 20%
where the time goes in v2:
time: 103 us
  Pallas kernels  54.3 us (53%)
  starting transfers between devices  21 us (20%)
  between operations  10.7 us (10%)
  local copies, waits for them, and re-layouts  7.44 us (7%)
  other arithmetic  4.82 us (5%)
  waiting for transfers between devices  4.3 us (4%)
    ppermute x13, starting transfers between devices, ring(): return lax.ppermute(x, axis, [(i, (i + by) % size) for i in range(size)])  21 us
    pallas_call x2, Pallas kernels, within(): pl.pallas_call(functools.partial(local_kernel, way), grid=grid, in_specs=...  15 us
    pallas_call x1, Pallas kernels, local(): pl.pallas_call(functools.partial(grad_kernel, total_width), grid=grid, in...  11.4 us
    pallas_call x1, Pallas kernels, local(): pl.pallas_call(first_kernel, grid=grid, in_specs=[small, small, wide, wid...  9.3 us
    pallas_call x1, Pallas kernels, local(): pl.pallas_call(gate_kernel, grid=grid, in_specs=[small] * 3 + [modes] * 3...  7.05 us
    pallas_call x1, Pallas kernels, local(): pl.pallas_call(last_kernel, grid=grid, in_specs=[small] * 3 + [modes] * 3...  6.34 us
    pallas_call x1, Pallas kernels, local(): pl.pallas_call(table_kernel, grid=grid, in_specs=[tapped] * 4, out_specs=...  5.3 us
    ppermute x13, waiting for transfers between devices, ring(): return lax.ppermute(x, axis, [(i, (i + by) % size) for i in range(size)])  4.3 us
  transfers between devices with their start and end apart: 13, of which 2 were waited for; matrix products, arithmetic and copies ran while one was open for 7% of the time, Pallas kernels for 20%

profile of v2, /device:TPU:0, one launch (start us, length us, event | category | flops | bytes accessed | tf_op | source)
XLA Modules:
  0.0 102.6 jit_solution(12736017854426718466)
XLA Ops:
  0.6 1.4 %copy.31.rate_ref = f32[128,16]{1,0:T(8,128)} copy(f32[128,16]{0,1:T(8,128)} %param.13) | data formatting | bytes 16384 | tf_op args[5]
  2.1 9.3 %first.1 = (bf16[8192,128]{1,0:T(8,128)(2,1)}, f32[2048,128]{1,0:T(8,128)}, bf16[16,2048]{1,0:T(8,128)(2,1)}) custom-call(s32[1,1]{1,0:T(1,128)} %bitcast.here_ref, s32[16]{0:T(128)} %len_ref.11, bf16[512,2048]{1,0:T(8,128)(2,1)} %k_ref.3, bf16[512,2048]{1,0:T(8,128)(2,1)} %v_ref.3, f32[128,16]{1,0:T(8,128)} %copy.31.rate_ref), custom_call_target="tpu_custom_call" | custom-call | tf_op jit(solution)/shard_map/first/pallas_call | solution.py:440
  11.4 1.4 %collective-permute-start.2 = (bf16[16,2048]{1,0:T(8,128)(2,1)}, bf16[16,2048]{1,0:T(8,128)(2,1)S(1)}, u32[]{:S(2)}, u32[]{:S(2)}) collective-permute-start(bf16[16,2048]{1,0:T(8,128)(2,1)} %get-tuple-element.32), channel_id=1, source_target_pairs={{0,12},{4,16},{8,20},{12,24},{16,28},{20,32},{24,36},{28,40},{32,4... | collective-permute-start | bytes 196616 | tf_op jit(solution)/shard_map/ppermute | solution.py:418
  12.8 1.9 %collective-permute-start.1 = (bf16[16,2048]{1,0:T(8,128)(2,1)}, bf16[16,2048]{1,0:T(8,128)(2,1)S(1)}, u32[]{:S(2)}, u32[]{:S(2)}) collective-permute-start(bf16[16,2048]{1,0:T(8,128)(2,1)} %get-tuple-element.32), channel_id=1, source_target_pairs={{0,8},{4,12},{8,16},{12,20},{16,24},{20,28},{24,32},{28,36},{32,40... | collective-permute-start | bytes 196616 | tf_op jit(solution)/shard_map/ppermute | solution.py:418
  14.7 1.5 %collective-permute-start = (bf16[16,2048]{1,0:T(8,128)(2,1)}, bf16[16,2048]{1,0:T(8,128)(2,1)S(1)}, u32[]{:S(2)}, u32[]{:S(2)}) collective-permute-start(bf16[16,2048]{1,0:T(8,128)(2,1)} %get-tuple-element.32), channel_id=1, source_target_pairs={{0,4},{4,8},{8,12},{12,16},{16,20},{20,24},{24,28},{28,32},{32,36}... | collective-permute-start | bytes 196616 | tf_op jit(solution)/shard_map/ppermute | solution.py:418
  16.2 0.0 copy-done.3
  16.3 0.1 stack_reshape.6
  16.4 0.1 copy.30
  16.5 0.1 reduce
  16.6 0.1 pad_add_fusion
  16.7 0.1 convert_reduce_fusion
  16.8 0.1 copy.33
  16.9 0.1 copy.32
  17.0 0.1 stack_reshape.7
  17.1 0.6 pad_maximum_fusion.flat_ref
  17.7 0.8 multiply_reduce_fusion
  18.6 0.7 broadcast_select_fusion
  19.2 0.7 fusion.12
  25.0 0.7 copy.35.res_ref
  25.8 0.7 copy.34.rate_ref
  26.5 0.3 broadcast_in_dim.26
  26.8 0.6 reshape.99.rate_ref
  27.4 5.3 %tables.1 = (bf16[8192,128]{1,0:T(8,128)(2,1)}, bf16[8192,128]{1,0:T(8,128)(2,1)}) custom-call(f32[128,128]{1,0:T(8,128)} %get-tuple-element.71.tapf_ref, f32[128,128]{1,0:T(8,128)} %get-tuple-element.70.tapb_ref, f32[128,128]{1,0:T(8,128)} %copy.34.rate_ref, f32[128,128]{1,0:T(8,128)} %copy.35.res_ref), custom_call_target="tpu_custom_call" | custom-call | flops 8388608 | bytes 12582912 | tf_op jit(solution)/shard_map/tables/pallas_call | solution.py:446
  32.8 0.0 collective-permute-done.2
  32.8 0.0 collective-permute-done.1
  32.8 0.0 collective-permute-done
  32.8 0.0 copy-done.8
  32.8 0.1 fusion.3
  32.9 2.1 %collective-permute-start.4 = (bf16[16,2048]{1,0:T(8,128)(2,1)S(1)}, bf16[16,2048]{1,0:T(8,128)(2,1)S(1)}, u32[]{:S(2)}, u32[]{:S(2)}) collective-permute-start(bf16[16,2048]{1,0:T(8,128)(2,1)S(1)} %fusion.3), channel_id=1, source_target_pairs={{0,20},{4,24},{8,28},{12,32},{16,36},{20,40},{24,44},{28,48},{32,5... | collective-permute-start | bytes 196616 | tf_op jit(solution)/shard_map/ppermute | solution.py:418
  35.0 1.3 %collective-permute-start.3 = (bf16[16,2048]{1,0:T(8,128)(2,1)S(1)}, bf16[16,2048]{1,0:T(8,128)(2,1)S(1)}, u32[]{:S(2)}, u32[]{:S(2)}) collective-permute-start(bf16[16,2048]{1,0:T(8,128)(2,1)S(1)} %fusion.3), channel_id=1, source_target_pairs={{0,4},{4,8},{8,12},{12,16},{16,20},{20,24},{24,28},{28,32},{32,36}... | collective-permute-start | bytes 196616 | tf_op jit(solution)/shard_map/ppermute | solution.py:418
  36.3 0.6 fusion.10.keep_ref
  36.9 7.5 %local.2.y_ref = bf16[512,2048]{1,0:T(8,128)(2,1)} custom-call(s32[1,1]{1,0:T(1,128)} %bitcast.here_ref, s32[16]{0:T(128)} %len_ref.11, bf16[8192,128]{1,0:T(8,128)(2,1)} %get-tuple-element.36.z_ref, f32[2048,128]{1,0:T(8,128)} %get-tuple-element.38.ent_ref, bf16[8192,128]{1,0:T(8,128)(2,1)} %get-tuple-element.39.left_ref), custom_call_target="tpu_custom_call" | custom-call | flops 16777216 | bytes 14680064 | tf_op jit(solution)/shard_map/local/pallas_call | solution.py:433
  44.4 0.0 collective-permute-done.4.far_ref
  44.4 0.0 copy-start.5
  44.4 0.0 collective-permute-done.3.near_ref
  44.4 0.0 copy-start.7
  44.4 0.6 copy-done.5
  45.0 0.0 copy-done.7
  45.0 7.0 %gate.1 = (bf16[512,2048]{1,0:T(8,128)(2,1)}, f32[8,512]{1,0:T(8,128)}) custom-call(s32[1,1]{1,0:T(1,128)} %bitcast.here_ref, s32[16]{0:T(128)} %len_ref.11, f32[1,2]{1,0:T(1,128)} %fusion.10.keep_ref, bf16[16,2048]{1,0:T(8,128)(2,1)} %copy-done.7, bf16[16,2048]{1,0:T(8,128)(2,1)} %copy-done.5, f32[16,2048]{1,0:T(8,128)} %copy-done, ...), custom_call_target="tpu_custom_call" | custom-call | tf_op jit(solution)/shard_map/gate/pallas_call | solution.py:454
  52.1 2.9 %collective-permute-start.7 = (f32[8,512]{1,0:T(8,128)}, f32[8,512]{1,0:T(8,128)S(1)}, u32[]{:S(2)}, u32[]{:S(2)}) collective-permute-start(f32[8,512]{1,0:T(8,128)} %get-tuple-element.40.s0_ref), channel_id=1, source_target_pairs={{0,3},{1,0},{2,1},{3,2},{4,7},{5,4},{6,5},{7,6},{8,11},{9,8},{10,9... | collective-permute-start | bytes 49160 | tf_op jit(solution)/shard_map/ppermute | solution.py:418
  54.9 0.8 collective-permute-start.6
  55.7 0.9 collective-permute-start.5
  56.6 0.0 collective-permute-done.7.s3_ref
  56.6 3.8 %collective-permute-done.6.s2_ref = f32[8,512]{1,0:T(8,128)S(1)} collective-permute-done((f32[8,512]{1,0:T(8,128)}, f32[8,512]{1,0:T(8,128)S(1)}, u32[]{:S(2)}, u32[]{:S(2)}) %collective-permute-start.6) | collective-permute-done | bytes 16416 | tf_op jit(solution)/shard_map/ppermute | solution.py:418
  60.4 0.5 collective-permute-done.5.s1_ref
  60.9 0.1 copy-done.12
  61.0 0.5 copy-done.13
  61.5 11.4 %grad.1 = (bf16[512,2048]{1,0:T(8,128)(2,1)}, bf16[512,2048]{1,0:T(8,128)(2,1)}, bf16[8192,128]{1,0:T(8,128)(2,1)}, f32[2048,128]{1,0:T(8,128)}, bf16[16,2048]{1,0:T(8,128)(2,1)}) custom-call(s32[1,1]{1,0:T(1,128)} %bitcast.here_ref, s32[16]{0:T(128)} %len_ref.11, f32[8,512]{1,0:T(8,128)} %get-tuple-element.40.s0_ref, f32[8,512]{1,0:T(8,128)} %copy-done.13, ...), custom_call_target="tpu_custom_call" | custom-call | tf_op jit(solution)/shard_map/grad/pallas_call | solution.py:460
  72.8 2.1 %collective-permute-start.10 = (bf16[16,2048]{1,0:T(8,128)(2,1)}, bf16[16,2048]{1,0:T(8,128)(2,1)S(1)}, u32[]{:S(2)}, u32[]{:S(2)}) collective-permute-start(bf16[16,2048]{1,0:T(8,128)(2,1)} %get-tuple-element.46), channel_id=1, source_target_pairs={{0,116},{4,120},{8,124},{12,0},{16,4},{20,8},{24,12},{28,16},{32,2... | collective-permute-start | bytes 196616 | tf_op jit(solution)/shard_map/ppermute | solution.py:418
  74.9 1.3 %collective-permute-start.9 = (bf16[16,2048]{1,0:T(8,128)(2,1)}, bf16[16,2048]{1,0:T(8,128)(2,1)S(1)}, u32[]{:S(2)}, u32[]{:S(2)}) collective-permute-start(bf16[16,2048]{1,0:T(8,128)(2,1)} %get-tuple-element.46), channel_id=1, source_target_pairs={{0,120},{4,124},{8,0},{12,4},{16,8},{20,12},{24,16},{28,20},{32,24... | collective-permute-start | bytes 196616 | tf_op jit(solution)/shard_map/ppermute | solution.py:418
  76.2 0.4 collective-permute-start.8
  81.3 0.0 collective-permute-done.10
  81.4 0.0 collective-permute-done.9
  81.4 0.0 collective-permute-done.8
  81.4 0.9 fusion.7
  82.3 1.8 %collective-permute-start.12 = (bf16[16,2048]{1,0:T(8,128)(2,1)S(1)}, bf16[16,2048]{1,0:T(8,128)(2,1)S(1)}, u32[]{:S(2)}, u32[]{:S(2)}) collective-permute-start(bf16[16,2048]{1,0:T(8,128)(2,1)S(1)} %fusion.7), channel_id=1, source_target_pairs={{0,108},{4,112},{8,116},{12,120},{16,124},{20,0},{24,4},{28,8},{32... | collective-permute-start | bytes 196616 | tf_op jit(solution)/shard_map/ppermute | solution.py:418
  84.1 2.7 %collective-permute-start.11 = (bf16[16,2048]{1,0:T(8,128)(2,1)S(1)}, bf16[16,2048]{1,0:T(8,128)(2,1)S(1)}, u32[]{:S(2)}, u32[]{:S(2)}) collective-permute-start(bf16[16,2048]{1,0:T(8,128)(2,1)S(1)} %fusion.7), channel_id=1, source_target_pairs={{0,124},{4,0},{8,4},{12,8},{16,12},{20,16},{24,20},{28,24},{32,28}... | collective-permute-start | bytes 196616 | tf_op jit(solution)/shard_map/ppermute | solution.py:418
  86.8 0.7 fusion.9.keep_ref
  87.5 7.5 %local.3.y_ref = bf16[512,2048]{1,0:T(8,128)(2,1)} custom-call(s32[1,1]{1,0:T(1,128)} %bitcast.here_ref, s32[16]{0:T(128)} %len_ref.11, bf16[8192,128]{1,0:T(8,128)(2,1)} %get-tuple-element.50.z_ref, f32[2048,128]{1,0:T(8,128)} %get-tuple-element.52.ent_ref, bf16[8192,128]{1,0:T(8,128)(2,1)} %get-tuple-element.53.left_ref), custom_call_target="tpu_custom_call" | custom-call | flops 16777216 | bytes 14680064 | tf_op jit(solution)/shard_map/local/pallas_call | solution.py:433
  95.0 0.0 collective-permute-done.12.far_ref
  95.0 0.0 collective-permute-done.11.near_ref
  95.0 0.6 copy-done.4
  95.6 0.6 copy-done.6
  96.2 6.3 %last.1 = (bf16[512,2048]{1,0:T(8,128)(2,1)}, bf16[512,2048]{1,0:T(8,128)(2,1)}) custom-call(s32[1,1]{1,0:T(1,128)} %bitcast.here_ref, s32[16]{0:T(128)} %len_ref.11, f32[1,2]{1,0:T(1,128)} %fusion.9.keep_ref, bf16[16,2048]{1,0:T(8,128)(2,1)} %copy-done.6, bf16[16,2048]{1,0:T(8,128)(2,1)} %copy-done.4, f32[16,2048]{1,0:T(8,128)} %copy-done, ...), custom_call_target="tpu_custom_call" | custom-call | tf_op jit(solution)/shard_map/last/pallas_call | solution.py:472
  (29 shorter events, 0.1 us)
Async XLA Ops:
  2.0 14.2 %copy-start.3 = (f32[128,16]{0,1:T(8,128)S(1)}, f32[128,16]{0,1:T(8,128)}, u32[]{:S(2)}) copy-start(f32[128,16]{0,1:T(8,128)} %param.13) | copy-start | bytes 24580
  2.1 14.2 %copy-start.2 = (f32[128,16]{1,0:T(8,128)S(1)}, f32[128,16]{1,0:T(8,128)}, u32[]{:S(2)}) copy-start(f32[128,16]{1,0:T(8,128)} %copy.31.rate_ref) | copy-start | bytes 24580
  2.1 14.3 %copy-start.10 = (s32[16]{0:T(128)S(1)}, s32[16]{0:T(128)}, u32[]{:S(2)}) copy-start(s32[16]{0:T(128)} %len_ref.11) | copy-start | bytes 196
  2.1 14.8 %copy-start.9 = (f32[128,16]{0,1:T(8,128)S(1)}, f32[128,16]{0,1:T(8,128)}, u32[]{:S(2)}) copy-start(f32[128,16]{0,1:T(8,128)} %param.12) | copy-start | bytes 24580
  11.4 21.4 %collective-permute-start.2 = (bf16[16,2048]{1,0:T(8,128)(2,1)}, bf16[16,2048]{1,0:T(8,128)(2,1)S(1)}, u32[]{:S(2)}, u32[]{:S(2)}) collective-permute-start(bf16[16,2048]{1,0:T(8,128)(2,1)} %get-tuple-element.32), channel_id=1, source_target_pairs={{0,12},{4,16},{8,20},{12,24},{16,28},{20,32},{24,36},{28,40},{32,4... | collective-permute-start | bytes 196616 | tf_op jit(solution)/shard_map/ppermute | solution.py:418
  12.8 20.0 %collective-permute-start.1 = (bf16[16,2048]{1,0:T(8,128)(2,1)}, bf16[16,2048]{1,0:T(8,128)(2,1)S(1)}, u32[]{:S(2)}, u32[]{:S(2)}) collective-permute-start(bf16[16,2048]{1,0:T(8,128)(2,1)} %get-tuple-element.32), channel_id=1, source_target_pairs={{0,8},{4,12},{8,16},{12,20},{16,24},{20,28},{24,32},{28,36},{32,40... | collective-permute-start | bytes 196616 | tf_op jit(solution)/shard_map/ppermute | solution.py:418
  14.7 18.0 %collective-permute-start = (bf16[16,2048]{1,0:T(8,128)(2,1)}, bf16[16,2048]{1,0:T(8,128)(2,1)S(1)}, u32[]{:S(2)}, u32[]{:S(2)}) collective-permute-start(bf16[16,2048]{1,0:T(8,128)(2,1)} %get-tuple-element.32), channel_id=1, source_target_pairs={{0,4},{4,8},{8,12},{12,16},{16,20},{20,24},{24,28},{28,32},{32,36}... | collective-permute-start | bytes 196616 | tf_op jit(solution)/shard_map/ppermute | solution.py:418
  17.7 15.1 %copy-start.8 = (bf16[16,2048]{1,0:T(8,128)(2,1)S(1)}, bf16[16,2048]{1,0:T(8,128)(2,1)}, u32[]{:S(2)}) copy-start(bf16[16,2048]{1,0:T(8,128)(2,1)} %get-tuple-element.32) | copy-start | bytes 196612
  27.4 16.9 %copy-start = (f32[16,2048]{1,0:T(8,128)}, f32[16,2048]{1,0:T(8,128)S(1)}, u32[]{:S(2)}) copy-start(f32[16,2048]{1,0:T(8,128)S(1)} %reshape.99.rate_ref) | copy-start | bytes 393220
  32.9 11.5 %collective-permute-start.4 = (bf16[16,2048]{1,0:T(8,128)(2,1)S(1)}, bf16[16,2048]{1,0:T(8,128)(2,1)S(1)}, u32[]{:S(2)}, u32[]{:S(2)}) collective-permute-start(bf16[16,2048]{1,0:T(8,128)(2,1)S(1)} %fusion.3), channel_id=1, source_target_pairs={{0,20},{4,24},{8,28},{12,32},{16,36},{20,40},{24,44},{28,48},{32,5... | collective-permute-start | bytes 196616 | tf_op jit(solution)/shard_map/ppermute | solution.py:418
  35.0 9.4 %collective-permute-start.3 = (bf16[16,2048]{1,0:T(8,128)(2,1)S(1)}, bf16[16,2048]{1,0:T(8,128)(2,1)S(1)}, u32[]{:S(2)}, u32[]{:S(2)}) collective-permute-start(bf16[16,2048]{1,0:T(8,128)(2,1)S(1)} %fusion.3), channel_id=1, source_target_pairs={{0,4},{4,8},{8,12},{12,16},{16,20},{20,24},{24,28},{28,32},{32,36}... | collective-permute-start | bytes 196616 | tf_op jit(solution)/shard_map/ppermute | solution.py:418
  44.4 0.6 copy-start.5
  44.4 0.6 copy-start.7
  52.1 4.5 %collective-permute-start.7 = (f32[8,512]{1,0:T(8,128)}, f32[8,512]{1,0:T(8,128)S(1)}, u32[]{:S(2)}, u32[]{:S(2)}) collective-permute-start(f32[8,512]{1,0:T(8,128)} %get-tuple-element.40.s0_ref), channel_id=1, source_target_pairs={{0,3},{1,0},{2,1},{3,2},{4,7},{5,4},{6,5},{7,6},{8,11},{9,8},{10,9... | collective-permute-start | bytes 49160 | tf_op jit(solution)/shard_map/ppermute | solution.py:418
  54.9 5.5 %collective-permute-start.6 = (f32[8,512]{1,0:T(8,128)}, f32[8,512]{1,0:T(8,128)S(1)}, u32[]{:S(2)}, u32[]{:S(2)}) collective-permute-start(f32[8,512]{1,0:T(8,128)} %get-tuple-element.40.s0_ref), channel_id=1, source_target_pairs={{0,2},{1,3},{2,0},{3,1},{4,6},{5,7},{6,4},{7,5},{8,10},{9,11},{10,... | collective-permute-start | bytes 49160 | tf_op jit(solution)/shard_map/ppermute | solution.py:418
  55.7 5.2 %collective-permute-start.5 = (f32[8,512]{1,0:T(8,128)}, f32[8,512]{1,0:T(8,128)S(1)}, u32[]{:S(2)}, u32[]{:S(2)}) collective-permute-start(f32[8,512]{1,0:T(8,128)} %get-tuple-element.40.s0_ref), channel_id=1, source_target_pairs={{0,1},{1,2},{2,3},{3,0},{4,5},{5,6},{6,7},{7,4},{8,9},{9,10},{10,1... | collective-permute-start | bytes 49160 | tf_op jit(solution)/shard_map/ppermute | solution.py:418
  56.6 4.3 %copy-start.11 = (f32[8,512]{1,0:T(8,128)}, f32[8,512]{1,0:T(8,128)S(1)}, u32[]{:S(2)}) copy-start(f32[8,512]{1,0:T(8,128)S(1)} %collective-permute-done.7.s3_ref) | copy-start | bytes 49156
  60.4 0.6 copy-start.12
  60.9 0.6 copy-start.13
  61.5 19.9 %copy-start.1 = (f32[16,2048]{1,0:T(8,128)S(1)}, f32[16,2048]{1,0:T(8,128)}, u32[]{:S(2)}) copy-start(f32[16,2048]{1,0:T(8,128)} %copy-done) | copy-start | bytes 393220
  72.8 8.5 %collective-permute-start.10 = (bf16[16,2048]{1,0:T(8,128)(2,1)}, bf16[16,2048]{1,0:T(8,128)(2,1)S(1)}, u32[]{:S(2)}, u32[]{:S(2)}) collective-permute-start(bf16[16,2048]{1,0:T(8,128)(2,1)} %get-tuple-element.46), channel_id=1, source_target_pairs={{0,116},{4,120},{8,124},{12,0},{16,4},{20,8},{24,12},{28,16},{32,2... | collective-permute-start | bytes 196616 | tf_op jit(solution)/shard_map/ppermute | solution.py:418
  74.9 6.4 %collective-permute-start.9 = (bf16[16,2048]{1,0:T(8,128)(2,1)}, bf16[16,2048]{1,0:T(8,128)(2,1)S(1)}, u32[]{:S(2)}, u32[]{:S(2)}) collective-permute-start(bf16[16,2048]{1,0:T(8,128)(2,1)} %get-tuple-element.46), channel_id=1, source_target_pairs={{0,120},{4,124},{8,0},{12,4},{16,8},{20,12},{24,16},{28,20},{32,24... | collective-permute-start | bytes 196616 | tf_op jit(solution)/shard_map/ppermute | solution.py:418
  76.2 5.1 %collective-permute-start.8 = (bf16[16,2048]{1,0:T(8,128)(2,1)}, bf16[16,2048]{1,0:T(8,128)(2,1)S(1)}, u32[]{:S(2)}, u32[]{:S(2)}) collective-permute-start(bf16[16,2048]{1,0:T(8,128)(2,1)} %get-tuple-element.46), channel_id=1, source_target_pairs={{0,124},{4,0},{8,4},{12,8},{16,12},{20,16},{24,20},{28,24},{32,28}... | collective-permute-start | bytes 196616 | tf_op jit(solution)/shard_map/ppermute | solution.py:418
  82.3 12.7 %collective-permute-start.12 = (bf16[16,2048]{1,0:T(8,128)(2,1)S(1)}, bf16[16,2048]{1,0:T(8,128)(2,1)S(1)}, u32[]{:S(2)}, u32[]{:S(2)}) collective-permute-start(bf16[16,2048]{1,0:T(8,128)(2,1)S(1)} %fusion.7), channel_id=1, source_target_pairs={{0,108},{4,112},{8,116},{12,120},{16,124},{20,0},{24,4},{28,8},{32... | collective-permute-start | bytes 196616 | tf_op jit(solution)/shard_map/ppermute | solution.py:418
  84.1 10.9 %collective-permute-start.11 = (bf16[16,2048]{1,0:T(8,128)(2,1)S(1)}, bf16[16,2048]{1,0:T(8,128)(2,1)S(1)}, u32[]{:S(2)}, u32[]{:S(2)}) collective-permute-start(bf16[16,2048]{1,0:T(8,128)(2,1)S(1)} %fusion.7), channel_id=1, source_target_pairs={{0,124},{4,0},{8,4},{12,8},{16,12},{20,16},{24,20},{28,24},{32,28}... | collective-permute-start | bytes 196616 | tf_op jit(solution)/shard_map/ppermute | solution.py:418
  95.0 0.6 copy-start.4
  95.6 0.6 copy-start.6

commit v3 on v2

--- a/solution.py
+++ b/solution.py
@@ -9,7 +9,7 @@
 
 C = 64
 W = 128
-LB = 512
+LB = 1024
 G = 16
 R = 16
 NG = W // G
@@ -35,18 +35,14 @@
 
 
 def swap_blocks(parts):
-    parts = list(parts)
+    parts = [part if m == 0 else turn(part, G * m) for m, part in enumerate(parts)]
     blk = iota(parts[0].shape[0], 1) // G
     bit = 1
     while bit < NG:
-        low = (blk & bit) == 0
-        for m in range(NG):
-            if not m & bit:
-                a, b = parts[m], parts[m | bit]
-                parts[m] = jnp.where(low, a, turn(b, G * bit))
-                parts[m | bit] = jnp.where(low, turn(a, -G * bit), b)
+        up = (blk & bit).astype(f32).astype(parts[0].dtype) > 0
+        parts = [jnp.where(up, parts[(m + bit) % NG], parts[m]) for m in range(NG)]
         bit *= 2
-    return parts
+    return [parts[0] if g == 0 else turn(parts[NG - g], -G * g) for g in range(NG)]
 
 
 def fan_out(x):
@@ -75,15 +71,21 @@
     return here_ref[0, 0] * (C * NG) + (iota(rows, 1) // G) * C
 
 
+def split3(x):
+    high = x.astype(bf16)
+    rest = x - high.astype(f32)
+    middle = rest.astype(bf16)
+    return high, middle, (rest - middle.astype(f32)).astype(bf16)
+
+
 def spread_rates(rate_ref, rate_out_ref):
-    groups = rate_ref.shape[0]
+    groups = rate_ref.shape[1]
     width = rate_out_ref.shape[1]
     row = lax.broadcasted_iota(i32, (groups, width), 0)
     lane = lax.broadcasted_iota(i32, (groups, width), 1)
-    pick = (row == (pl.program_id(0) * width + lane) // G).astype(f32)
-    rate_out_ref[...] = lax.dot_general(
-        rate_ref[...], pick, (((0,), (0,)), ((), ())), precision=lax.Precision.HIGHEST, preferred_element_type=f32
-    )
+    pick = (row == (pl.program_id(0) * width + lane) // G).astype(f32).astype(bf16)
+    out = dot(jnp.concatenate(split3(rate_ref[...]), axis=0), pick)
+    rate_out_ref[...] = out[:R] + out[R : 2 * R] + out[2 * R :]
 
 
 def put_masks(here_ref, len_ref, reach_ref, join_ref, way):
@@ -174,12 +176,23 @@
     put_states(z_ref, ent_ref, own_ref, rates_ref[...], masks, 1)
 
 
-def table_kernel(tapf_ref, tapb_ref, rate_ref, res_ref, lf_ref, lb_ref):
+def table_kernel(tapf_ref, tapb_ref, rates_ref, ress_ref, lf_ref, lb_ref, rate_ref, res_ref):
+    step = pl.program_id(0)
+
+    @pl.when(step == 0)
+    def _():
+        pick = (iota(R, 0) == iota(R, 1) % R).astype(f32).astype(bf16)
+        pick = jnp.concatenate([pick] * 3, axis=0)
+        for from_ref, to_ref in ((rates_ref, rate_ref), (ress_ref, res_ref)):
+            parts = jnp.concatenate(split3(from_ref[...]), axis=0)
+            to_ref[...] = lax.dot_general(parts, pick, (((0,), (0,)), ((), ())), preferred_element_type=f32)
+
     lane, row = iota(C, 1), iota(C, 0).astype(f32)
     for g in range(LB // G):
         at = slice(g, g + 1)
-        rate = jnp.broadcast_to(rate_ref[at, :], (C, W))
-        res = jnp.broadcast_to(res_ref[at, :], (C, W))
+        mine = pl.ds(step * (LB // G) + g, 1)
+        rate = jnp.broadcast_to(rate_ref[mine, :], (C, W))
+        res = jnp.broadcast_to(res_ref[mine, :], (C, W))
         for tap_ref, out_ref, lag in ((tapf_ref, lf_ref, row + 1.0), (tapb_ref, lb_ref, C - row)):
             taps = jnp.broadcast_to(tap_ref[at, :], (C, W))
             square = pltpu.roll(taps, 0, 1, stride=1, stride_axis=0)
@@ -304,10 +317,8 @@
 
 def grad_kernel(
     total_width, here_ref, len_ref, s0_ref, s1_ref, s2_ref, s3_ref, conv_ref, q_ref, c_ref, gain_ref, rate_ref,
-    out_ref, gq_ref, z_ref, ent_ref, own_ref, rates_ref, inv_ref, mean_ref, reach_ref, join_ref,
+    out_ref, gq_ref, z_ref, ent_ref, own_ref, inv_ref, mean_ref, reach_ref, join_ref,
 ):
-    spread_rates(rate_ref, rates_ref)
-
     @pl.when(pl.program_id(0) == 0)
     def _():
         stat = s0_ref[...] + s1_ref[...] + s2_ref[...] + s3_ref[...]
@@ -342,7 +353,7 @@
         for g in range(NG):
             n = s * NG + g
             z_ref[n * C : (n + 1) * C, :] = z[g]
-    put_states(z_ref, ent_ref, own_ref, rates_ref[...], masks, -1)
+    put_states(z_ref, ent_ref, own_ref, rate_ref[...], masks, -1)
 
 
 def last_kernel(here_ref, len_ref, keep_ref, near_ref, far_ref, rate_ref, flat_ref, y_ref, k_ref, v_ref, gk_ref, gv_ref):
@@ -380,7 +391,6 @@
     keep_f = jnp.stack([keep(ends, 1, 1, 1), keep(ends, 1, 1 + HOP, 1)]).reshape(1, 2)
     keep_b = jnp.stack([keep(begins, 1, 1, -1), keep(begins, 1, 1 + HOP, -1)]).reshape(1, 2)
 
-    rates = jnp.repeat(decay_rate.T, G, axis=1)
     lane = jnp.arange(W)
 
     def taps(lags):
@@ -388,7 +398,6 @@
         return jnp.where(lags < C, h, 0.0)
 
     tap_f, tap_b = taps((W - lane) % W), taps(lane)
-    rate_rep, res_rep = jnp.tile(decay_rate, (1, NG)), jnp.tile(residues, (1, NG))
     flat = jnp.stack([decay_rate.reshape(groups * R), residues.reshape(groups * R)])
     gain = norm_gain.reshape(1, width)
 
@@ -408,7 +417,7 @@
     full16 = shaped(bf16, rows, width)
     stack16 = shaped(bf16, groups * C, W)
     entries, ends_shape = shaped(f32, groups * R, W), shaped(bf16, R, width)
-    rates_of = pl.BlockSpec((groups, R), lambda i: (0, 0))
+    rates_of = pl.BlockSpec((R, groups), lambda i: (0, 0))
     kept = [pltpu.VMEM((C, W), bf16), pltpu.VMEM((4, R, W), f32)]
     flat2 = pl.BlockSpec((2, LB), lambda i: (0, i))
     stat_spec = pl.BlockSpec((8, rows), lambda i: (0, 0))
@@ -437,17 +446,17 @@
             cost_estimate=pl.CostEstimate(flops=16 * rows * width, bytes_accessed=14 * rows * width, transcendentals=0),
         )(here_arr, doc_lengths, z, ent, left)
 
-    z_f, ent_f, own_f = pl.pallas_call(
-        first_kernel, grid=grid, in_specs=[small, small, wide, wide, rates_of], out_specs=[stacked, states, modes],
-        out_shape=[stack16, entries, ends_shape], scratch_shapes=[pltpu.VMEM((R, LB), f32)] + kept,
+    z_f, ent_f, own_f, rates = pl.pallas_call(
+        first_kernel, grid=grid, in_specs=[small, small, wide, wide, rates_of], out_specs=[stacked, states, modes, modes],
+        out_shape=[stack16, entries, ends_shape, shaped(f32, R, width)], scratch_shapes=kept,
         compiler_params=params, name="first",
-    )(here_arr, doc_lengths, key_branch, value_branch, decay_rate)
+    )(here_arr, doc_lengths, key_branch, value_branch, decay_rate.T)
     parts_f = gather(own_f, 1)
     left_f, left_b = pl.pallas_call(
-        table_kernel, grid=grid, in_specs=[tapped] * 4, out_specs=[stacked] * 2,
-        out_shape=[stack16] * 2, compiler_params=params, name="tables",
+        table_kernel, grid=grid, in_specs=[tapped] * 2 + [rates_of] * 2, out_specs=[stacked] * 2,
+        out_shape=[stack16] * 2, scratch_shapes=[pltpu.VMEM((groups, W), f32)] * 2, compiler_params=params, name="tables",
         cost_estimate=pl.CostEstimate(flops=8 * rows * width, bytes_accessed=12 * rows * width, transcendentals=0),
-    )(tap_f, tap_b, rate_rep, res_rep)
+    )(tap_f, tap_b, decay_rate.T, residues.T)
     left_f, gathered, near_f, far_f = pass_on(parts_f, left_f, ends, 1)
     ent_f, _ = lax.optimization_barrier((ent_f, gathered))
     y_f = within(z_f, ent_f, left_f, 1)
@@ -459,12 +468,12 @@
     stats = [stat] + [ring(stat, "ch", n) for n in range(1, 4)]
     layer_out, grad_query, z_b, ent_b, own_b = pl.pallas_call(
         functools.partial(grad_kernel, total_width), grid=grid,
-        in_specs=[small, small] + [stat_spec] * 4 + [wide] * 3 + [row1, rates_of],
+        in_specs=[small, small] + [stat_spec] * 4 + [wide] * 3 + [row1, modes],
         out_specs=[wide, wide, stacked, states, modes],
         out_shape=[full16, full16, stack16, entries, ends_shape],
-        scratch_shapes=[pltpu.VMEM((R, LB), f32)] + [pltpu.VMEM((rows, W), f32)] * 2 + kept,
+        scratch_shapes=[pltpu.VMEM((rows, W), f32)] * 2 + kept,
         compiler_params=params, name="grad",
-    )(here_arr, doc_lengths, *stats, conv, query_gate, cotangent, gain, decay_rate)
+    )(here_arr, doc_lengths, *stats, conv, query_gate, cotangent, gain, rates)
     parts_b = gather(own_b, -1)
     left_b, gathered, near_b, far_b = pass_on(parts_b, left_b, begins, -1)
     ent_b, _ = lax.optimization_barrier((ent_b, gathered))

time: 103 us -> 94.2 us (0.915)
  Pallas kernels: 54.3 us -> 48.1 us
  local copies, waits for them, and re-layouts: 7.44 us -> 3.75 us
    pallas_call x2, Pallas kernels: 15 us -> 12.8 us  [within(): pl.pallas_call(functools.partial(local_kernel, way), grid=grid, in_specs=...]
    pallas_call x1, Pallas kernels: 11.4 us -> 9.72 us  [local(): pl.pallas_call(functools.partial(grad_kernel, total_width), grid=grid, in...]
    pallas_call x1, Pallas kernels: 9.3 us -> 7.75 us  [local(): pl.pallas_call(first_kernel, grid=grid, in_specs=[small, small, wide, wid...]
    another operation x5 -> x1, local copies, waits for them, and re-layouts: 1.53 us -> 0.08 us  [the longest x2 0.73 us: local(): jnp.tile(residues, (1, NG))]
    unnamed x30 -> x24, local copies, waits for them, and re-layouts: 3.99 us -> 2.7 us
  transfers between devices with their start and end apart: 13 -> 13, of which waited for: 2 -> 2; matrix products, arithmetic and copies ran while one was open for 7% -> 5% of each run, Pallas kernels for 20% -> 20%
where the time goes in v3:
time: 94.2 us; the launch traced here: 93.9 us
  Pallas kernels  48.1 us (51%)
  starting transfers between devices  20.8 us (22%)
  between operations  11.1 us (12%)
  other arithmetic  5.77 us (6%)
  waiting for transfers between devices  4.28 us (5%)
  local copies, waits for them, and re-layouts  3.75 us (4%)
    ppermute x13, starting transfers between devices, ring(): return lax.ppermute(x, axis, [(i, (i + by) % size) for i in range(size)])  20.8 us
    pallas_call x2, Pallas kernels, within(): pl.pallas_call(functools.partial(local_kernel, way), grid=grid, in_specs=...  12.8 us
    pallas_call x1, Pallas kernels, local(): pl.pallas_call(functools.partial(grad_kernel, total_width), grid=grid, in...  9.72 us
    pallas_call x1, Pallas kernels, local(): pl.pallas_call(first_kernel, grid=grid, in_specs=[small, small, wide, wid...  7.75 us
    pallas_call x1, Pallas kernels, local(): pl.pallas_call(gate_kernel, grid=grid, in_specs=[small] * 3 + [modes] * 3...  6.7 us
    pallas_call x1, Pallas kernels, local(): pl.pallas_call(last_kernel, grid=grid, in_specs=[small] * 3 + [modes] * 3...  5.63 us
    pallas_call x1, Pallas kernels, local(): pl.pallas_call(table_kernel, grid=grid, in_specs=[tapped] * 2 + [rates_of...  5.56 us
    ppermute x13, waiting for transfers between devices, ring(): return lax.ppermute(x, axis, [(i, (i + by) % size) for i in range(size)])  4.28 us
  transfers between devices with their start and end apart: 13, of which 2 were waited for; matrix products, arithmetic and copies ran while one was open for 5% of the time, Pallas kernels for 20%

profile of v3, /device:TPU:0, one launch (start us, length us, event | category | flops | bytes accessed | tf_op | source)
XLA Modules:
  0.0 93.9 jit_solution(7009492446187278814)
XLA Ops:
  0.6 0.0 copy-start.1
  0.6 0.0 copy-start.7
  0.7 0.0 copy-start.6
  0.7 7.7 %first.1 = (bf16[8192,128]{1,0:T(8,128)(2,1)}, f32[2048,128]{1,0:T(8,128)}, bf16[16,2048]{1,0:T(8,128)(2,1)}, f32[16,2048]{1,0:T(8,128)}) custom-call(s32[1,1]{1,0:T(1,128)} %bitcast.here_ref, s32[16]{0:T(128)} %len_ref.11, bf16[512,2048]{1,0:T(8,128)(2,1)} %k_ref.3, bf16[512,2048]{1,0:T(8,128)(2,1)} %v_ref.3, f32[16,128]{1,0:T(8,128)} %bitcast.21), custom_call_target="tpu_custom_call" | custom-call | tf_op jit(solution)/shard_map/first/pallas_call | solution.py:449
  8.4 1.5 %collective-permute-start.2 = (bf16[16,2048]{1,0:T(8,128)(2,1)}, bf16[16,2048]{1,0:T(8,128)(2,1)S(1)}, u32[]{:S(2)}, u32[]{:S(2)}) collective-permute-start(bf16[16,2048]{1,0:T(8,128)(2,1)} %get-tuple-element.33), channel_id=1, source_target_pairs={{0,12},{4,16},{8,20},{12,24},{16,28},{20,32},{24,36},{28,40},{32,4... | collective-permute-start | bytes 196616 | tf_op jit(solution)/shard_map/ppermute | solution.py:427
  9.9 1.9 %collective-permute-start.1 = (bf16[16,2048]{1,0:T(8,128)(2,1)}, bf16[16,2048]{1,0:T(8,128)(2,1)S(1)}, u32[]{:S(2)}, u32[]{:S(2)}) collective-permute-start(bf16[16,2048]{1,0:T(8,128)(2,1)} %get-tuple-element.33), channel_id=1, source_target_pairs={{0,8},{4,12},{8,16},{12,20},{16,24},{20,28},{24,32},{28,36},{32,40... | collective-permute-start | bytes 196616 | tf_op jit(solution)/shard_map/ppermute | solution.py:427
  11.8 1.5 %collective-permute-start = (bf16[16,2048]{1,0:T(8,128)(2,1)}, bf16[16,2048]{1,0:T(8,128)(2,1)S(1)}, u32[]{:S(2)}, u32[]{:S(2)}) collective-permute-start(bf16[16,2048]{1,0:T(8,128)(2,1)} %get-tuple-element.33), channel_id=1, source_target_pairs={{0,4},{4,8},{8,12},{12,16},{16,20},{20,24},{24,28},{28,32},{32,36}... | collective-permute-start | bytes 196616 | tf_op jit(solution)/shard_map/ppermute | solution.py:427
  13.4 0.0 copy-done.1
  13.4 0.1 copy.25
  13.5 0.0 copy-done.7
  13.5 0.1 copy.22
  13.6 0.1 reduce
  13.7 0.1 pad_add_fusion
  13.8 0.1 convert_reduce_fusion
  13.9 0.1 copy.24
  14.0 0.0 copy-done.6
  14.0 0.1 copy.23
  14.1 0.1 stack_reshape.7
  14.2 0.1 stack_reshape.6
  14.3 0.6 pad_maximum_fusion.flat_ref
  14.9 0.8 multiply_reduce_fusion
  15.8 0.7 broadcast_select_fusion
  16.4 0.7 fusion.12
  22.4 5.6 %tables.1 = (bf16[8192,128]{1,0:T(8,128)(2,1)}, bf16[8192,128]{1,0:T(8,128)(2,1)}) custom-call(f32[128,128]{1,0:T(8,128)} %get-tuple-element.73.tapf_ref, f32[128,128]{1,0:T(8,128)} %get-tuple-element.72.tapb_ref, f32[16,128]{1,0:T(8,128)} %bitcast.22, f32[16,128]{1,0:T(8,128)} %bitcast.25), custom_call_target="tpu_custom_call" | custom-call | flops 8388608 | bytes 12582912 | tf_op jit(solution)/shard_map/tables/pallas_call | solution.py:455
  28.0 0.0 collective-permute-done.2
  28.0 0.0 collective-permute-done.1
  28.0 0.0 collective-permute-done
  28.0 1.0 %fusion.3 = bf16[16,2048]{1,0:T(8,128)(2,1)S(1)} fusion(bf16[16,2048]{1,0:T(8,128)(2,1)S(1)} %collective-permute-done.2, bf16[16,2048]{1,0:T(8,128)(2,1)S(1)} %collective-permute-done.1, bf16[16,2048]{1,0:T(8,128)(2,1)S(1)} %collective-permute-done, bf16[16,2048]{1,0:T(8,128)(2,1)} %get-tuple-element.33, f32[16,2048]{1,0:T(8,128)} %get-tuple-element.34.rate_ref, ...), kind=kLoop, calls=%fused_computation.8 | loop fusion | flops 622592 | bytes 458768 | tf_op jit(solution)/shard_map/convert_element_type | solution.py:438
  29.1 2.1 %collective-permute-start.4 = (bf16[16,2048]{1,0:T(8,128)(2,1)S(1)}, bf16[16,2048]{1,0:T(8,128)(2,1)S(1)}, u32[]{:S(2)}, u32[]{:S(2)}) collective-permute-start(bf16[16,2048]{1,0:T(8,128)(2,1)S(1)} %fusion.3), channel_id=1, source_target_pairs={{0,20},{4,24},{8,28},{12,32},{16,36},{20,40},{24,44},{28,48},{32,5... | collective-permute-start | bytes 196616 | tf_op jit(solution)/shard_map/ppermute | solution.py:427
  31.2 1.3 %collective-permute-start.3 = (bf16[16,2048]{1,0:T(8,128)(2,1)S(1)}, bf16[16,2048]{1,0:T(8,128)(2,1)S(1)}, u32[]{:S(2)}, u32[]{:S(2)}) collective-permute-start(bf16[16,2048]{1,0:T(8,128)(2,1)S(1)} %fusion.3), channel_id=1, source_target_pairs={{0,4},{4,8},{8,12},{12,16},{16,20},{20,24},{24,28},{28,32},{32,36}... | collective-permute-start | bytes 196616 | tf_op jit(solution)/shard_map/ppermute | solution.py:427
  32.5 0.6 fusion.10.keep_ref
  33.1 6.4 %local.2.y_ref = bf16[512,2048]{1,0:T(8,128)(2,1)} custom-call(s32[1,1]{1,0:T(1,128)} %bitcast.here_ref, s32[16]{0:T(128)} %len_ref.11, bf16[8192,128]{1,0:T(8,128)(2,1)} %get-tuple-element.38.z_ref, f32[2048,128]{1,0:T(8,128)} %get-tuple-element.40.ent_ref, bf16[8192,128]{1,0:T(8,128)(2,1)} %get-tuple-element.41.left_ref), custom_call_target="tpu_custom_call" | custom-call | flops 16777216 | bytes 14680064 | tf_op jit(solution)/shard_map/local/pallas_call | solution.py:442
  39.5 0.0 collective-permute-done.4.far_ref
  39.5 0.0 collective-permute-done.3.near_ref
  39.5 0.0 copy-start.5
  39.5 0.6 copy-done.3
  40.1 0.0 copy-done.5
  40.2 6.7 %gate.1 = (bf16[512,2048]{1,0:T(8,128)(2,1)}, f32[8,512]{1,0:T(8,128)}) custom-call(s32[1,1]{1,0:T(1,128)} %bitcast.here_ref, s32[16]{0:T(128)} %len_ref.11, f32[1,2]{1,0:T(1,128)} %fusion.10.keep_ref, bf16[16,2048]{1,0:T(8,128)(2,1)} %copy-done.5, bf16[16,2048]{1,0:T(8,128)(2,1)} %copy-done.3, f32[16,2048]{1,0:T(8,128)} %get-tuple-element.34.rate_ref, ...), custom_call_target="tpu_custom_call" | custom-call | tf_op jit(solution)/shard_map/gate/pallas_call | solution.py:463
  46.9 2.8 %collective-permute-start.7 = (f32[8,512]{1,0:T(8,128)}, f32[8,512]{1,0:T(8,128)S(1)}, u32[]{:S(2)}, u32[]{:S(2)}) collective-permute-start(f32[8,512]{1,0:T(8,128)} %get-tuple-element.42.s0_ref), channel_id=1, source_target_pairs={{0,3},{1,0},{2,1},{3,2},{4,7},{5,4},{6,5},{7,6},{8,11},{9,8},{10,9... | collective-permute-start | bytes 49160 | tf_op jit(solution)/shard_map/ppermute | solution.py:427
  49.7 0.8 collective-permute-start.6
  50.5 0.9 collective-permute-start.5
  51.4 0.0 collective-permute-done.7.s3_ref
  51.4 3.8 %collective-permute-done.6.s2_ref = f32[8,512]{1,0:T(8,128)S(1)} collective-permute-done((f32[8,512]{1,0:T(8,128)}, f32[8,512]{1,0:T(8,128)S(1)}, u32[]{:S(2)}, u32[]{:S(2)}) %collective-permute-start.6) | collective-permute-done | bytes 16416 | tf_op jit(solution)/shard_map/ppermute | solution.py:427
  55.1 0.5 collective-permute-done.5.s1_ref
  55.6 0.0 copy-done.8
  55.6 0.1 copy-done.9
  55.7 0.5 copy-done.10
  56.2 9.7 %grad.1 = (bf16[512,2048]{1,0:T(8,128)(2,1)}, bf16[512,2048]{1,0:T(8,128)(2,1)}, bf16[8192,128]{1,0:T(8,128)(2,1)}, f32[2048,128]{1,0:T(8,128)}, bf16[16,2048]{1,0:T(8,128)(2,1)}) custom-call(s32[1,1]{1,0:T(1,128)} %bitcast.here_ref, s32[16]{0:T(128)} %len_ref.11, f32[8,512]{1,0:T(8,128)} %get-tuple-element.42.s0_ref, f32[8,512]{1,0:T(8,128)} %copy-done.10, ...), custom_call_target="tpu_custom_call" | custom-call | tf_op jit(solution)/shard_map/grad/pallas_call | solution.py:469
  65.9 1.9 %collective-permute-start.10 = (bf16[16,2048]{1,0:T(8,128)(2,1)}, bf16[16,2048]{1,0:T(8,128)(2,1)S(1)}, u32[]{:S(2)}, u32[]{:S(2)}) collective-permute-start(bf16[16,2048]{1,0:T(8,128)(2,1)} %get-tuple-element.48), channel_id=1, source_target_pairs={{0,116},{4,120},{8,124},{12,0},{16,4},{20,8},{24,12},{28,16},{32,2... | collective-permute-start | bytes 196616 | tf_op jit(solution)/shard_map/ppermute | solution.py:427
  67.9 1.3 %collective-permute-start.9 = (bf16[16,2048]{1,0:T(8,128)(2,1)}, bf16[16,2048]{1,0:T(8,128)(2,1)S(1)}, u32[]{:S(2)}, u32[]{:S(2)}) collective-permute-start(bf16[16,2048]{1,0:T(8,128)(2,1)} %get-tuple-element.48), channel_id=1, source_target_pairs={{0,120},{4,124},{8,0},{12,4},{16,8},{20,12},{24,16},{28,20},{32,24... | collective-permute-start | bytes 196616 | tf_op jit(solution)/shard_map/ppermute | solution.py:427
  69.2 0.4 collective-permute-start.8
  74.5 0.0 collective-permute-done.10
  74.5 0.0 collective-permute-done.9
  74.5 0.0 collective-permute-done.8
  74.5 0.9 fusion.7
  75.4 1.8 %collective-permute-start.12 = (bf16[16,2048]{1,0:T(8,128)(2,1)S(1)}, bf16[16,2048]{1,0:T(8,128)(2,1)S(1)}, u32[]{:S(2)}, u32[]{:S(2)}) collective-permute-start(bf16[16,2048]{1,0:T(8,128)(2,1)S(1)} %fusion.7), channel_id=1, source_target_pairs={{0,108},{4,112},{8,116},{12,120},{16,124},{20,0},{24,4},{28,8},{32... | collective-permute-start | bytes 196616 | tf_op jit(solution)/shard_map/ppermute | solution.py:427
  77.2 2.7 %collective-permute-start.11 = (bf16[16,2048]{1,0:T(8,128)(2,1)S(1)}, bf16[16,2048]{1,0:T(8,128)(2,1)S(1)}, u32[]{:S(2)}, u32[]{:S(2)}) collective-permute-start(bf16[16,2048]{1,0:T(8,128)(2,1)S(1)} %fusion.7), channel_id=1, source_target_pairs={{0,124},{4,0},{8,4},{12,8},{16,12},{20,16},{24,20},{28,24},{32,28}... | collective-permute-start | bytes 196616 | tf_op jit(solution)/shard_map/ppermute | solution.py:427
  79.9 0.7 fusion.9.keep_ref
  80.6 6.4 %local.3.y_ref = bf16[512,2048]{1,0:T(8,128)(2,1)} custom-call(s32[1,1]{1,0:T(1,128)} %bitcast.here_ref, s32[16]{0:T(128)} %len_ref.11, bf16[8192,128]{1,0:T(8,128)(2,1)} %get-tuple-element.52.z_ref, f32[2048,128]{1,0:T(8,128)} %get-tuple-element.54.ent_ref, bf16[8192,128]{1,0:T(8,128)(2,1)} %get-tuple-element.55.left_ref), custom_call_target="tpu_custom_call" | custom-call | flops 16777216 | bytes 14680064 | tf_op jit(solution)/shard_map/local/pallas_call | solution.py:442
  86.9 0.0 collective-permute-done.12.far_ref
  87.0 0.0 collective-permute-done.11.near_ref
  87.0 0.6 copy-done.2
  87.6 0.6 copy-done.4
  88.2 5.6 %last.1 = (bf16[512,2048]{1,0:T(8,128)(2,1)}, bf16[512,2048]{1,0:T(8,128)(2,1)}) custom-call(s32[1,1]{1,0:T(1,128)} %bitcast.here_ref, s32[16]{0:T(128)} %len_ref.11, f32[1,2]{1,0:T(1,128)} %fusion.9.keep_ref, bf16[16,2048]{1,0:T(8,128)(2,1)} %copy-done.4, bf16[16,2048]{1,0:T(8,128)(2,1)} %copy-done.2, f32[16,2048]{1,0:T(8,128)} %get-tuple-element.34.rate_ref, ...), custom_call_target="tpu_custom_call" | custom-call | tf_op jit(solution)/shard_map/last/pallas_call | solution.py:481
  (17 shorter events, 0.1 us)
Async XLA Ops:
  0.6 12.7 %copy-start.1 = (f32[128,16]{0,1:T(8,128)S(1)}, f32[128,16]{0,1:T(8,128)}, u32[]{:S(2)}) copy-start(f32[128,16]{0,1:T(8,128)} %param.13) | copy-start | bytes 24580
  0.6 12.8 %copy-start.7 = (s32[16]{0:T(128)S(1)}, s32[16]{0:T(128)}, u32[]{:S(2)}) copy-start(s32[16]{0:T(128)} %len_ref.11) | copy-start | bytes 196
  0.7 13.4 %copy-start.6 = (f32[128,16]{0,1:T(8,128)S(1)}, f32[128,16]{0,1:T(8,128)}, u32[]{:S(2)}) copy-start(f32[128,16]{0,1:T(8,128)} %param.12) | copy-start | bytes 24580
  8.4 19.6 %collective-permute-start.2 = (bf16[16,2048]{1,0:T(8,128)(2,1)}, bf16[16,2048]{1,0:T(8,128)(2,1)S(1)}, u32[]{:S(2)}, u32[]{:S(2)}) collective-permute-start(bf16[16,2048]{1,0:T(8,128)(2,1)} %get-tuple-element.33), channel_id=1, source_target_pairs={{0,12},{4,16},{8,20},{12,24},{16,28},{20,32},{24,36},{28,40},{32,4... | collective-permute-start | bytes 196616 | tf_op jit(solution)/shard_map/ppermute | solution.py:427
  9.9 18.1 %collective-permute-start.1 = (bf16[16,2048]{1,0:T(8,128)(2,1)}, bf16[16,2048]{1,0:T(8,128)(2,1)S(1)}, u32[]{:S(2)}, u32[]{:S(2)}) collective-permute-start(bf16[16,2048]{1,0:T(8,128)(2,1)} %get-tuple-element.33), channel_id=1, source_target_pairs={{0,8},{4,12},{8,16},{12,20},{16,24},{20,28},{24,32},{28,36},{32,40... | collective-permute-start | bytes 196616 | tf_op jit(solution)/shard_map/ppermute | solution.py:427
  11.8 16.2 %collective-permute-start = (bf16[16,2048]{1,0:T(8,128)(2,1)}, bf16[16,2048]{1,0:T(8,128)(2,1)S(1)}, u32[]{:S(2)}, u32[]{:S(2)}) collective-permute-start(bf16[16,2048]{1,0:T(8,128)(2,1)} %get-tuple-element.33), channel_id=1, source_target_pairs={{0,4},{4,8},{8,12},{12,16},{16,20},{20,24},{24,28},{28,32},{32,36}... | collective-permute-start | bytes 196616 | tf_op jit(solution)/shard_map/ppermute | solution.py:427
  29.1 10.4 %collective-permute-start.4 = (bf16[16,2048]{1,0:T(8,128)(2,1)S(1)}, bf16[16,2048]{1,0:T(8,128)(2,1)S(1)}, u32[]{:S(2)}, u32[]{:S(2)}) collective-permute-start(bf16[16,2048]{1,0:T(8,128)(2,1)S(1)} %fusion.3), channel_id=1, source_target_pairs={{0,20},{4,24},{8,28},{12,32},{16,36},{20,40},{24,44},{28,48},{32,5... | collective-permute-start | bytes 196616 | tf_op jit(solution)/shard_map/ppermute | solution.py:427
  31.2 8.3 %collective-permute-start.3 = (bf16[16,2048]{1,0:T(8,128)(2,1)S(1)}, bf16[16,2048]{1,0:T(8,128)(2,1)S(1)}, u32[]{:S(2)}, u32[]{:S(2)}) collective-permute-start(bf16[16,2048]{1,0:T(8,128)(2,1)S(1)} %fusion.3), channel_id=1, source_target_pairs={{0,4},{4,8},{8,12},{12,16},{16,20},{20,24},{24,28},{28,32},{32,36}... | collective-permute-start | bytes 196616 | tf_op jit(solution)/shard_map/ppermute | solution.py:427
  39.5 0.6 copy-start.3
  39.5 0.6 copy-start.5
  46.9 4.5 %collective-permute-start.7 = (f32[8,512]{1,0:T(8,128)}, f32[8,512]{1,0:T(8,128)S(1)}, u32[]{:S(2)}, u32[]{:S(2)}) collective-permute-start(f32[8,512]{1,0:T(8,128)} %get-tuple-element.42.s0_ref), channel_id=1, source_target_pairs={{0,3},{1,0},{2,1},{3,2},{4,7},{5,4},{6,5},{7,6},{8,11},{9,8},{10,9... | collective-permute-start | bytes 49160 | tf_op jit(solution)/shard_map/ppermute | solution.py:427
  49.7 5.5 %collective-permute-start.6 = (f32[8,512]{1,0:T(8,128)}, f32[8,512]{1,0:T(8,128)S(1)}, u32[]{:S(2)}, u32[]{:S(2)}) collective-permute-start(f32[8,512]{1,0:T(8,128)} %get-tuple-element.42.s0_ref), channel_id=1, source_target_pairs={{0,2},{1,3},{2,0},{3,1},{4,6},{5,7},{6,4},{7,5},{8,10},{9,11},{10,... | collective-permute-start | bytes 49160 | tf_op jit(solution)/shard_map/ppermute | solution.py:427
  50.5 5.2 %collective-permute-start.5 = (f32[8,512]{1,0:T(8,128)}, f32[8,512]{1,0:T(8,128)S(1)}, u32[]{:S(2)}, u32[]{:S(2)}) collective-permute-start(f32[8,512]{1,0:T(8,128)} %get-tuple-element.42.s0_ref), channel_id=1, source_target_pairs={{0,1},{1,2},{2,3},{3,0},{4,5},{5,6},{6,7},{7,4},{8,9},{9,10},{10,1... | collective-permute-start | bytes 49160 | tf_op jit(solution)/shard_map/ppermute | solution.py:427
  51.4 4.3 %copy-start.8 = (f32[8,512]{1,0:T(8,128)}, f32[8,512]{1,0:T(8,128)S(1)}, u32[]{:S(2)}) copy-start(f32[8,512]{1,0:T(8,128)S(1)} %collective-permute-done.7.s3_ref) | copy-start | bytes 49156
  55.1 0.6 copy-start.9
  55.6 0.6 copy-start.10
  56.2 18.3 %copy-start = (f32[16,2048]{1,0:T(8,128)S(1)}, f32[16,2048]{1,0:T(8,128)}, u32[]{:S(2)}) copy-start(f32[16,2048]{1,0:T(8,128)} %get-tuple-element.34.rate_ref) | copy-start | bytes 393220
  65.9 8.5 %collective-permute-start.10 = (bf16[16,2048]{1,0:T(8,128)(2,1)}, bf16[16,2048]{1,0:T(8,128)(2,1)S(1)}, u32[]{:S(2)}, u32[]{:S(2)}) collective-permute-start(bf16[16,2048]{1,0:T(8,128)(2,1)} %get-tuple-element.48), channel_id=1, source_target_pairs={{0,116},{4,120},{8,124},{12,0},{16,4},{20,8},{24,12},{28,16},{32,2... | collective-permute-start | bytes 196616 | tf_op jit(solution)/shard_map/ppermute | solution.py:427
  67.9 6.6 %collective-permute-start.9 = (bf16[16,2048]{1,0:T(8,128)(2,1)}, bf16[16,2048]{1,0:T(8,128)(2,1)S(1)}, u32[]{:S(2)}, u32[]{:S(2)}) collective-permute-start(bf16[16,2048]{1,0:T(8,128)(2,1)} %get-tuple-element.48), channel_id=1, source_target_pairs={{0,120},{4,124},{8,0},{12,4},{16,8},{20,12},{24,16},{28,20},{32,24... | collective-permute-start | bytes 196616 | tf_op jit(solution)/shard_map/ppermute | solution.py:427
  69.2 5.3 %collective-permute-start.8 = (bf16[16,2048]{1,0:T(8,128)(2,1)}, bf16[16,2048]{1,0:T(8,128)(2,1)S(1)}, u32[]{:S(2)}, u32[]{:S(2)}) collective-permute-start(bf16[16,2048]{1,0:T(8,128)(2,1)} %get-tuple-element.48), channel_id=1, source_target_pairs={{0,124},{4,0},{8,4},{12,8},{16,12},{20,16},{24,20},{28,24},{32,28}... | collective-permute-start | bytes 196616 | tf_op jit(solution)/shard_map/ppermute | solution.py:427
  75.4 11.5 %collective-permute-start.12 = (bf16[16,2048]{1,0:T(8,128)(2,1)S(1)}, bf16[16,2048]{1,0:T(8,128)(2,1)S(1)}, u32[]{:S(2)}, u32[]{:S(2)}) collective-permute-start(bf16[16,2048]{1,0:T(8,128)(2,1)S(1)} %fusion.7), channel_id=1, source_target_pairs={{0,108},{4,112},{8,116},{12,120},{16,124},{20,0},{24,4},{28,8},{32... | collective-permute-start | bytes 196616 | tf_op jit(solution)/shard_map/ppermute | solution.py:427
  77.2 9.7 %collective-permute-start.11 = (bf16[16,2048]{1,0:T(8,128)(2,1)S(1)}, bf16[16,2048]{1,0:T(8,128)(2,1)S(1)}, u32[]{:S(2)}, u32[]{:S(2)}) collective-permute-start(bf16[16,2048]{1,0:T(8,128)(2,1)S(1)} %fusion.7), channel_id=1, source_target_pairs={{0,124},{4,0},{8,4},{12,8},{16,12},{20,16},{24,20},{28,24},{32,28}... | collective-permute-start | bytes 196616 | tf_op jit(solution)/shard_map/ppermute | solution.py:427
  87.0 0.6 copy-start.2
  87.6 0.6 copy-start.4

commit v4 on v3

--- a/solution.py
+++ b/solution.py
@@ -267,10 +267,38 @@
     return jnp.concatenate(out, axis=0)
 
 
-def arrived(here_ref, len_ref, keep_ref, near_ref, far_ref, rates_ref, flat_ref, s, rows, way):
+def document(place, len_ref):
+    found, start = i32(-1), i32(0)
+    for n in range(DOCS):
+        found += jnp.where(place >= start, 1, 0)
+        start += len_ref[n]
+    return found
+
+
+def edge_keep(here_ref, len_ref, rows, devices, from_, to, way):
+    here = here_ref[0, 0]
+
+    def edge(n):
+        return document((here - n + 1) * rows - 1 if way > 0 else (here + n) * rows, len_ref)
+
+    inside = here >= to if way > 0 else here + to < devices
+    return jnp.where(inside & (edge(from_) == edge(to)), 1.0, 0.0).astype(f32)
+
+
+def pass_kernel(way, devices, rows, here_ref, len_ref, rate_ref, own_ref, *refs):
+    out_ref = refs[-1]
+    total, far = own_ref[...].astype(f32), jnp.exp(-rate_ref[...] * rows)
+    scale = far
+    for n, ref in enumerate(refs[:-1]):
+        total += edge_keep(here_ref, len_ref, rows, devices, 0, n + 1, way) * scale * ref[...].astype(f32)
+        scale *= far
+    out_ref[...] = total.astype(bf16)
+
+
+def arrived(here_ref, len_ref, keeps, near_ref, far_ref, rates_ref, flat_ref, s, rows, way):
     at = slice(s * W, (s + 1) * W)
     span = jnp.exp(-rates_ref[:, at] * (HOP * rows))
-    total = keep_ref[0, 0] * near_ref[:, at].astype(f32) + keep_ref[0, 1] * (span * far_ref[:, at].astype(f32))
+    total = keeps[0] * near_ref[:, at].astype(f32) + keeps[1] * (span * far_ref[:, at].astype(f32))
     diag = (iota(W, 0) // R) == (iota(W, 1) // G)
     square = jnp.where(diag, jnp.concatenate([total] * NG, axis=0), 0.0)
     hi = square.astype(bf16)
@@ -280,7 +308,7 @@
 
 
 def gate_kernel(
-    here_ref, len_ref, keep_ref, near_ref, far_ref, rate_ref, flat_ref, y_ref, q_ref, c_ref, gain_ref,
+    devices, here_ref, len_ref, near_ref, far_ref, rate_ref, flat_ref, y_ref, q_ref, c_ref, gain_ref,
     conv_ref, stat_ref, acc_ref,
 ):
     step = pl.program_id(0)
@@ -290,9 +318,10 @@
     def _():
         acc_ref[...] = jnp.zeros_like(acc_ref)
 
+    keeps = [edge_keep(here_ref, len_ref, rows, devices, 1, n, 1) for n in (1, 1 + HOP)]
     for s in range(LB // W):
         at = slice(s * W, (s + 1) * W)
-        carry = arrived(here_ref, len_ref, keep_ref, near_ref, far_ref, rate_ref, flat_ref, s, rows, 1)
+        carry = arrived(here_ref, len_ref, keeps, near_ref, far_ref, rate_ref, flat_ref, s, rows, 1)
         conv_ref[:, at] = (y_ref[:, at].astype(f32) + carry).astype(bf16)
     for m in range(rows // C):
         part = slice(m * C, (m + 1) * C)
@@ -356,20 +385,15 @@
     put_states(z_ref, ent_ref, own_ref, rate_ref[...], masks, -1)
 
 
-def last_kernel(here_ref, len_ref, keep_ref, near_ref, far_ref, rate_ref, flat_ref, y_ref, k_ref, v_ref, gk_ref, gv_ref):
+def last_kernel(devices, here_ref, len_ref, near_ref, far_ref, rate_ref, flat_ref, y_ref, k_ref, v_ref, gk_ref, gv_ref):
     rows = y_ref.shape[0]
+    keeps = [edge_keep(here_ref, len_ref, rows, devices, 1, n, -1) for n in (1, 1 + HOP)]
     for s in range(LB // W):
         at = slice(s * W, (s + 1) * W)
-        carry = arrived(here_ref, len_ref, keep_ref, near_ref, far_ref, rate_ref, flat_ref, s, rows, -1)
+        carry = arrived(here_ref, len_ref, keeps, near_ref, far_ref, rate_ref, flat_ref, s, rows, -1)
         grad = y_ref[:, at].astype(f32) + carry
         gk_ref[:, at] = (grad * v_ref[:, at].astype(f32)).astype(bf16)
         gv_ref[:, at] = (grad * k_ref[:, at].astype(f32)).astype(bf16)
-
-
-def doc_index(places, doc_lengths):
-    doc_ends = jnp.cumsum(doc_lengths)
-    doc_starts = doc_ends - doc_lengths
-    return jnp.sum((doc_starts[None, :] <= places[:, None]).astype(i32), axis=1) - 1
 
 
 def local(query_gate, key_branch, value_branch, norm_gain, residues, decay_rate, doc_lengths, cotangent):
@@ -379,17 +403,6 @@
     here = lax.axis_index("seq")
     total_width = width * lax.axis_size("ch")
     here_arr = here.astype(i32).reshape(1, 1)
-
-    offset = jnp.arange(REACH // rows + 1, dtype=i32)
-    docs = doc_index(jnp.concatenate([(here - offset + 1) * rows - 1, (here + offset) * rows]), doc_lengths)
-    ends, begins = docs[: len(offset)], docs[len(offset) :]
-
-    def keep(edge, from_, to, way):
-        inside = here >= to if way > 0 else here + to < devices
-        return ((edge[from_] == edge[to]) & inside).astype(f32)
-
-    keep_f = jnp.stack([keep(ends, 1, 1, 1), keep(ends, 1, 1 + HOP, 1)]).reshape(1, 2)
-    keep_b = jnp.stack([keep(begins, 1, 1, -1), keep(begins, 1, 1 + HOP, -1)]).reshape(1, 2)
 
     lane = jnp.arange(W)
 
@@ -429,13 +442,14 @@
     def gather(own, way):
         return [own] + [ring(own, "seq", way * n) for n in range(1, HOP)]
 
-    def pass_on(parts, beside, edge, way):
+    def pass_on(parts, beside, way):
         parts, beside = lax.optimization_barrier((parts, beside))
-        total, scale = 0.0, 1.0
-        for n, part in enumerate(parts):
-            total += keep(edge, 0, n, way) * scale * part.astype(f32)
-            scale *= jnp.exp(-rates * rows)
-        total = total.astype(bf16)
+        whole = pl.BlockSpec(memory_space=pltpu.VMEM)
+        total = pl.pallas_call(
+            functools.partial(pass_kernel, way, devices, rows), in_specs=[small] * 2 + [whole] * (1 + HOP),
+            out_specs=whole, out_shape=ends_shape, name="pass_on",
+            compiler_params=pltpu.CompilerParams(vmem_limit_bytes=8 * 1024 * 1024),
+        )(here_arr, doc_lengths, rates, *parts)
         return beside, total, ring(total, "seq", way), ring(total, "seq", way * (1 + HOP))
 
     def within(z, ent, left, way):
@@ -457,14 +471,14 @@
         out_shape=[stack16] * 2, scratch_shapes=[pltpu.VMEM((groups, W), f32)] * 2, compiler_params=params, name="tables",
         cost_estimate=pl.CostEstimate(flops=8 * rows * width, bytes_accessed=12 * rows * width, transcendentals=0),
     )(tap_f, tap_b, decay_rate.T, residues.T)
-    left_f, gathered, near_f, far_f = pass_on(parts_f, left_f, ends, 1)
+    left_f, gathered, near_f, far_f = pass_on(parts_f, left_f, 1)
     ent_f, _ = lax.optimization_barrier((ent_f, gathered))
     y_f = within(z_f, ent_f, left_f, 1)
     conv, stat = pl.pallas_call(
-        gate_kernel, grid=grid, in_specs=[small] * 3 + [modes] * 3 + [flat2] + [wide] * 3 + [row1],
+        functools.partial(gate_kernel, devices), grid=grid, in_specs=[small] * 2 + [modes] * 3 + [flat2] + [wide] * 3 + [row1],
         out_specs=[wide, stat_spec], out_shape=[full16, shaped(f32, 8, rows)],
         scratch_shapes=[pltpu.VMEM((rows, 2 * W), f32)], compiler_params=params, name="gate",
-    )(here_arr, doc_lengths, keep_f, near_f, far_f, rates, flat, y_f, query_gate, cotangent, gain)
+    )(here_arr, doc_lengths, near_f, far_f, rates, flat, y_f, query_gate, cotangent, gain)
     stats = [stat] + [ring(stat, "ch", n) for n in range(1, 4)]
     layer_out, grad_query, z_b, ent_b, own_b = pl.pallas_call(
         functools.partial(grad_kernel, total_width), grid=grid,
@@ -475,13 +489,13 @@
         compiler_params=params, name="grad",
     )(here_arr, doc_lengths, *stats, conv, query_gate, cotangent, gain, rates)
     parts_b = gather(own_b, -1)
-    left_b, gathered, near_b, far_b = pass_on(parts_b, left_b, begins, -1)
+    left_b, gathered, near_b, far_b = pass_on(parts_b, left_b, -1)
     ent_b, _ = lax.optimization_barrier((ent_b, gathered))
     y_b = within(z_b, ent_b, left_b, -1)
     grad_key, grad_value = pl.pallas_call(
-        last_kernel, grid=grid, in_specs=[small] * 3 + [modes] * 3 + [flat2] + [wide] * 3, out_specs=[wide, wide],
+        functools.partial(last_kernel, devices), grid=grid, in_specs=[small] * 2 + [modes] * 3 + [flat2] + [wide] * 3, out_specs=[wide, wide],
         out_shape=[full16, full16], compiler_params=params, name="last",
-    )(here_arr, doc_lengths, keep_b, near_b, far_b, rates, flat, y_b, key_branch, value_branch)
+    )(here_arr, doc_lengths, near_b, far_b, rates, flat, y_b, key_branch, value_branch)
     return layer_out, grad_query, grad_key, grad_value
 
 

time: 94.2 us -> 87.5 us (0.929)
  between operations: 11.1 us -> 0.82 us
  other arithmetic: 5.77 us -> 2.15 us
  waiting for transfers between devices: 4.28 us -> 7.35 us
  local copies, waits for them, and re-layouts: 3.75 us -> 5.53 us
  Pallas kernels: 48.1 us -> 49.6 us
    ppermute x13, waiting for transfers between devices: 4.28 us -> 7.35 us  [ring(): return lax.ppermute(x, axis, [(i, (i + by) % size) for i in range(size)])]
    unnamed x24 -> x32, local copies, waits for them, and re-layouts: 2.7 us -> 5.25 us
    convert_element_type x2 -> x0, other arithmetic: 1.98 us -> none  [pass_on(): total = total.astype(bf16)]
    pallas_call x2 -> x4, Pallas kernels: 12.3 us -> 13.9 us  [the longest x1 6.85 us: local(): pl.pallas_call(functools.partial(gate_kernel, devices), grid=grid, in_spe...]
    reshape x2 -> x0, other arithmetic: 1.29 us -> none  [the longest x1 0.66 us: local(): jnp.stack([keep(begins, 1, 1, -1), keep(begins, 1, 1 + HOP, -1)])]
  transfers between devices with their start and end apart: 13 -> 13, of which waited for: 2 -> 4; matrix products, arithmetic and copies ran while one was open for 5% -> 3% of each run, Pallas kernels for 20% -> 21%
where the time goes in v4:
time: 87.5 us; the launch traced here: 87.2 us
  Pallas kernels  49.6 us (57%)
  starting transfers between devices  21.7 us (25%)
  waiting for transfers between devices  7.35 us (8%)
  local copies, waits for them, and re-layouts  5.53 us (6%)
  other arithmetic  2.15 us (2%)
    ppermute x13, starting transfers between devices, ring(): return lax.ppermute(x, axis, [(i, (i + by) % size) for i in range(size)])  21.7 us
    pallas_call x2, Pallas kernels, within(): pl.pallas_call(functools.partial(local_kernel, way), grid=grid, in_specs=...  12.8 us
    pallas_call x1, Pallas kernels, local(): pl.pallas_call(functools.partial(grad_kernel, total_width), grid=grid, in...  9.7 us
    pallas_call x1, Pallas kernels, local(): pl.pallas_call(first_kernel, grid=grid, in_specs=[small, small, wide, wid...  7.75 us
    ppermute x13, waiting for transfers between devices, ring(): return lax.ppermute(x, axis, [(i, (i + by) % size) for i in range(size)])  7.35 us
    pallas_call x1, Pallas kernels, local(): pl.pallas_call(functools.partial(gate_kernel, devices), grid=grid, in_spe...  6.85 us
    pallas_call x1, Pallas kernels, local(): pl.pallas_call(functools.partial(last_kernel, devices), grid=grid, in_spe...  5.71 us
    pallas_call x1, Pallas kernels, local(): pl.pallas_call(table_kernel, grid=grid, in_specs=[tapped] * 2 + [rates_of...  5.52 us
  transfers between devices with their start and end apart: 13, of which 4 were waited for; matrix products, arithmetic and copies ran while one was open for 3% of the time, Pallas kernels for 21%

profile of v4, /device:TPU:0, one launch (start us, length us, event | category | flops | bytes accessed | tf_op | source)
XLA Modules:
  0.0 87.2 jit_solution(7257463496522232070)
XLA Ops:
  0.6 0.0 copy-start.6
  0.6 0.0 copy-start.11
  0.7 0.0 copy-start.4
  0.7 7.7 %first.1 = (bf16[8192,128]{1,0:T(8,128)(2,1)}, f32[2048,128]{1,0:T(8,128)}, bf16[16,2048]{1,0:T(8,128)(2,1)}, f32[16,2048]{1,0:T(8,128)}) custom-call(s32[1,1]{1,0:T(1,128)} %bitcast.here_ref, s32[16]{0:T(128)} %len_ref.15, bf16[512,2048]{1,0:T(8,128)(2,1)} %k_ref.3, bf16[512,2048]{1,0:T(8,128)(2,1)} %v_ref.3, f32[16,128]{1,0:T(8,128)} %bitcast.4), custom_call_target="tpu_custom_call" | custom-call | tf_op jit(solution)/shard_map/first/pallas_call | solution.py:463
  8.4 1.5 %collective-permute-start.2 = (bf16[16,2048]{1,0:T(8,128)(2,1)}, bf16[16,2048]{1,0:T(8,128)(2,1)S(1)}, u32[]{:S(2)}, u32[]{:S(2)}) collective-permute-start(bf16[16,2048]{1,0:T(8,128)(2,1)} %get-tuple-element.34.own_ref), channel_id=1, source_target_pairs={{0,12},{4,16},{8,20},{12,24},{16,28},{20,32},{24,36},{28,40},{32,4... | collective-permute-start | bytes 196616 | tf_op jit(solution)/shard_map/ppermute | solution.py:440
  9.9 1.9 %collective-permute-start.1 = (bf16[16,2048]{1,0:T(8,128)(2,1)}, bf16[16,2048]{1,0:T(8,128)(2,1)S(1)}, u32[]{:S(2)}, u32[]{:S(2)}) collective-permute-start(bf16[16,2048]{1,0:T(8,128)(2,1)} %get-tuple-element.34.own_ref), channel_id=1, source_target_pairs={{0,8},{4,12},{8,16},{12,20},{16,24},{20,28},{24,32},{28,36},{32,40... | collective-permute-start | bytes 196616 | tf_op jit(solution)/shard_map/ppermute | solution.py:440
  11.8 1.5 %collective-permute-start = (bf16[16,2048]{1,0:T(8,128)(2,1)}, bf16[16,2048]{1,0:T(8,128)(2,1)S(1)}, u32[]{:S(2)}, u32[]{:S(2)}) collective-permute-start(bf16[16,2048]{1,0:T(8,128)(2,1)} %get-tuple-element.34.own_ref), channel_id=1, source_target_pairs={{0,4},{4,8},{8,12},{12,16},{16,20},{20,24},{24,28},{28,32},{32,36}... | collective-permute-start | bytes 196616 | tf_op jit(solution)/shard_map/ppermute | solution.py:440
  13.3 0.0 copy-done.6
  13.4 0.1 copy.21
  13.5 0.0 copy-done.11
  13.5 0.1 copy.20
  13.6 0.8 multiply_reduce_fusion
  14.4 0.7 broadcast_select_fusion
  15.1 0.1 stack_reshape.7
  15.2 0.1 copy.22
  15.3 0.1 stack_reshape.6
  15.4 5.5 %tables.1 = (bf16[8192,128]{1,0:T(8,128)(2,1)}, bf16[8192,128]{1,0:T(8,128)(2,1)}) custom-call(f32[128,128]{1,0:T(8,128)} %get-tuple-element.61.tapf_ref, f32[128,128]{1,0:T(8,128)} %get-tuple-element.60.tapb_ref, f32[16,128]{1,0:T(8,128)} %bitcast.5, f32[16,128]{1,0:T(8,128)} %bitcast.8), custom_call_target="tpu_custom_call" | custom-call | flops 8388608 | bytes 12582912 | tf_op jit(solution)/shard_map/tables/pallas_call | solution.py:469
  20.9 0.0 collective-permute-done.2.refs_2_
  20.9 0.0 collective-permute-done.1.refs_1_
  20.9 0.0 collective-permute-done.refs_0_
  20.9 0.0 copy-done.4
  20.9 0.0 copy-start
  20.9 0.9 %copy-done = f32[16,2048]{1,0:T(8,128)S(1)} copy-done((f32[16,2048]{1,0:T(8,128)S(1)}, f32[16,2048]{1,0:T(8,128)}, u32[]{:S(2)}) %copy-start) | copy-done | bytes 131096
  21.8 0.8 copy-done.2
  22.7 0.7 pass_on.2
  23.3 2.1 %collective-permute-start.4 = (bf16[16,2048]{1,0:T(8,128)(2,1)S(1)}, bf16[16,2048]{1,0:T(8,128)(2,1)S(1)}, u32[]{:S(2)}, u32[]{:S(2)}) collective-permute-start(bf16[16,2048]{1,0:T(8,128)(2,1)S(1)} %pass_on.2), channel_id=1, source_target_pairs={{0,20},{4,24},{8,28},{12,32},{16,36},{20,40},{24,44},{28,48},{32,5... | collective-permute-start | bytes 196616 | tf_op jit(solution)/shard_map/ppermute | solution.py:440
  25.4 1.3 %collective-permute-start.3 = (bf16[16,2048]{1,0:T(8,128)(2,1)S(1)}, bf16[16,2048]{1,0:T(8,128)(2,1)S(1)}, u32[]{:S(2)}, u32[]{:S(2)}) collective-permute-start(bf16[16,2048]{1,0:T(8,128)(2,1)S(1)} %pass_on.2), channel_id=1, source_target_pairs={{0,4},{4,8},{8,12},{12,16},{16,20},{20,24},{24,28},{28,32},{32,36}... | collective-permute-start | bytes 196616 | tf_op jit(solution)/shard_map/ppermute | solution.py:440
  26.7 0.6 pad_maximum_fusion.flat_ref
  27.3 6.4 %local.2.y_ref = bf16[512,2048]{1,0:T(8,128)(2,1)} custom-call(s32[1,1]{1,0:T(1,128)} %bitcast.here_ref, s32[16]{0:T(128)} %len_ref.15, bf16[8192,128]{1,0:T(8,128)(2,1)} %get-tuple-element.38.z_ref, f32[2048,128]{1,0:T(8,128)} %get-tuple-element.40.ent_ref, bf16[8192,128]{1,0:T(8,128)(2,1)} %get-tuple-element.41.left_ref), custom_call_target="tpu_custom_call" | custom-call | flops 16777216 | bytes 14680064 | tf_op jit(solution)/shard_map/local/pallas_call | solution.py:456
  33.7 0.0 collective-permute-done.4.far_ref
  33.7 0.0 collective-permute-done.3.near_ref
  33.7 0.0 copy-start.9
  33.7 0.6 copy-done.7
  34.3 0.0 copy-done.9
  34.4 6.9 %gate.1 = (bf16[512,2048]{1,0:T(8,128)(2,1)}, f32[8,512]{1,0:T(8,128)}) custom-call(s32[1,1]{1,0:T(1,128)} %bitcast.here_ref, s32[16]{0:T(128)} %len_ref.15, bf16[16,2048]{1,0:T(8,128)(2,1)} %copy-done.9, bf16[16,2048]{1,0:T(8,128)(2,1)} %copy-done.7, f32[16,2048]{1,0:T(8,128)} %get-tuple-element.31.rate_ref, f32[2,2048]{1,0:T(2,128)} %pad_maximum_fusion.flat_ref, ...), custom_call_target="tpu_custom_call" | custom-call | tf_op jit(solution)/shard_map/gate/pallas_call | solution.py:477
  41.2 2.8 %collective-permute-start.7 = (f32[8,512]{1,0:T(8,128)}, f32[8,512]{1,0:T(8,128)S(1)}, u32[]{:S(2)}, u32[]{:S(2)}) collective-permute-start(f32[8,512]{1,0:T(8,128)} %get-tuple-element.42.s0_ref), channel_id=1, source_target_pairs={{0,3},{1,0},{2,1},{3,2},{4,7},{5,4},{6,5},{7,6},{8,11},{9,8},{10,9... | collective-permute-start | bytes 49160 | tf_op jit(solution)/shard_map/ppermute | solution.py:440
  44.1 0.8 collective-permute-start.6
  44.8 0.9 %collective-permute-start.5 = (f32[8,512]{1,0:T(8,128)}, f32[8,512]{1,0:T(8,128)S(1)}, u32[]{:S(2)}, u32[]{:S(2)}) collective-permute-start(f32[8,512]{1,0:T(8,128)} %get-tuple-element.42.s0_ref), channel_id=1, source_target_pairs={{0,1},{1,2},{2,3},{3,0},{4,5},{5,6},{6,7},{7,4},{8,9},{9,10},{10,1... | collective-permute-start | bytes 49160 | tf_op jit(solution)/shard_map/ppermute | solution.py:440
  45.7 0.0 collective-permute-done.7.s3_ref
  45.7 3.8 %collective-permute-done.6.s2_ref = f32[8,512]{1,0:T(8,128)S(1)} collective-permute-done((f32[8,512]{1,0:T(8,128)}, f32[8,512]{1,0:T(8,128)S(1)}, u32[]{:S(2)}, u32[]{:S(2)}) %collective-permute-start.6) | collective-permute-done | bytes 16416 | tf_op jit(solution)/shard_map/ppermute | solution.py:440
  49.5 0.5 collective-permute-done.5.s1_ref
  50.0 0.0 copy-done.12
  50.0 0.1 copy-done.13
  50.1 0.5 copy-done.14
  50.6 9.7 %grad.1 = (bf16[512,2048]{1,0:T(8,128)(2,1)}, bf16[512,2048]{1,0:T(8,128)(2,1)}, bf16[8192,128]{1,0:T(8,128)(2,1)}, f32[2048,128]{1,0:T(8,128)}, bf16[16,2048]{1,0:T(8,128)(2,1)}) custom-call(s32[1,1]{1,0:T(1,128)} %bitcast.here_ref, s32[16]{0:T(128)} %len_ref.15, f32[8,512]{1,0:T(8,128)} %get-tuple-element.42.s0_ref, f32[8,512]{1,0:T(8,128)} %copy-done.14, ...), custom_call_target="tpu_custom_call" | custom-call | tf_op jit(solution)/shard_map/grad/pallas_call | solution.py:483
  60.3 2.0 %collective-permute-start.10 = (bf16[16,2048]{1,0:T(8,128)(2,1)}, bf16[16,2048]{1,0:T(8,128)(2,1)S(1)}, u32[]{:S(2)}, u32[]{:S(2)}) collective-permute-start(bf16[16,2048]{1,0:T(8,128)(2,1)} %get-tuple-element.48.own_ref), channel_id=1, source_target_pairs={{0,116},{4,120},{8,124},{12,0},{16,4},{20,8},{24,12},{28,16},{32,2... | collective-permute-start | bytes 196616 | tf_op jit(solution)/shard_map/ppermute | solution.py:440
  62.3 1.2 %collective-permute-start.9 = (bf16[16,2048]{1,0:T(8,128)(2,1)}, bf16[16,2048]{1,0:T(8,128)(2,1)S(1)}, u32[]{:S(2)}, u32[]{:S(2)}) collective-permute-start(bf16[16,2048]{1,0:T(8,128)(2,1)} %get-tuple-element.48.own_ref), channel_id=1, source_target_pairs={{0,120},{4,124},{8,0},{12,4},{16,8},{20,12},{24,16},{28,20},{32,24... | collective-permute-start | bytes 196616 | tf_op jit(solution)/shard_map/ppermute | solution.py:440
  63.5 0.4 collective-permute-start.8
  63.9 1.1 %collective-permute-done.10.refs_2_ = bf16[16,2048]{1,0:T(8,128)(2,1)S(1)} collective-permute-done((bf16[16,2048]{1,0:T(8,128)(2,1)}, bf16[16,2048]{1,0:T(8,128)(2,1)S(1)}, u32[]{:S(2)}, u32[]{:S(2)}) %collective-permute-start.10) | collective-permute-done | bytes 65568 | tf_op jit(solution)/shard_map/ppermute | solution.py:440
  65.0 2.0 %collective-permute-done.9.refs_1_ = bf16[16,2048]{1,0:T(8,128)(2,1)S(1)} collective-permute-done((bf16[16,2048]{1,0:T(8,128)(2,1)}, bf16[16,2048]{1,0:T(8,128)(2,1)S(1)}, u32[]{:S(2)}, u32[]{:S(2)}) %collective-permute-start.9) | collective-permute-done | bytes 65568 | tf_op jit(solution)/shard_map/ppermute | solution.py:440
  67.0 0.0 collective-permute-done.8.refs_0_
  67.0 0.0 copy-done.1
  67.0 0.0 copy-done.5
  67.0 0.0 copy-start.3
  67.0 0.8 copy-done.3
  67.8 0.7 pass_on.3
  68.5 2.1 %collective-permute-start.12 = (bf16[16,2048]{1,0:T(8,128)(2,1)S(1)}, bf16[16,2048]{1,0:T(8,128)(2,1)S(1)}, u32[]{:S(2)}, u32[]{:S(2)}) collective-permute-start(bf16[16,2048]{1,0:T(8,128)(2,1)S(1)} %pass_on.3), channel_id=1, source_target_pairs={{0,108},{4,112},{8,116},{12,120},{16,124},{20,0},{24,4},{28,8},{32... | collective-permute-start | bytes 196616 | tf_op jit(solution)/shard_map/ppermute | solution.py:440
  70.5 3.2 %collective-permute-start.11 = (bf16[16,2048]{1,0:T(8,128)(2,1)S(1)}, bf16[16,2048]{1,0:T(8,128)(2,1)S(1)}, u32[]{:S(2)}, u32[]{:S(2)}) collective-permute-start(bf16[16,2048]{1,0:T(8,128)(2,1)S(1)} %pass_on.3), channel_id=1, source_target_pairs={{0,124},{4,0},{8,4},{12,8},{16,12},{20,16},{24,20},{28,24},{32,28}... | collective-permute-start | bytes 196616 | tf_op jit(solution)/shard_map/ppermute | solution.py:440
  73.8 6.4 %local.3.y_ref = bf16[512,2048]{1,0:T(8,128)(2,1)} custom-call(s32[1,1]{1,0:T(1,128)} %bitcast.here_ref, s32[16]{0:T(128)} %len_ref.15, bf16[8192,128]{1,0:T(8,128)(2,1)} %get-tuple-element.52.z_ref, f32[2048,128]{1,0:T(8,128)} %get-tuple-element.54.ent_ref, bf16[8192,128]{1,0:T(8,128)(2,1)} %get-tuple-element.55.left_ref), custom_call_target="tpu_custom_call" | custom-call | flops 16777216 | bytes 14680064 | tf_op jit(solution)/shard_map/local/pallas_call | solution.py:456
  80.2 0.0 collective-permute-done.12.far_ref
  80.2 0.0 collective-permute-done.11.near_ref
  80.2 0.6 copy-done.8
  80.8 0.6 copy-done.10
  81.5 5.7 %last.1 = (bf16[512,2048]{1,0:T(8,128)(2,1)}, bf16[512,2048]{1,0:T(8,128)(2,1)}) custom-call(s32[1,1]{1,0:T(1,128)} %bitcast.here_ref, s32[16]{0:T(128)} %len_ref.15, bf16[16,2048]{1,0:T(8,128)(2,1)} %copy-done.10, bf16[16,2048]{1,0:T(8,128)(2,1)} %copy-done.8, f32[16,2048]{1,0:T(8,128)} %get-tuple-element.31.rate_ref, f32[2,2048]{1,0:T(2,128)} %pad_maximum_fusion.flat_ref, ...), custom_call_target="tpu_custom_call" | custom-call | tf_op jit(solution)/shard_map/last/pallas_call | solution.py:495
  (14 shorter events, 0.1 us)
Async XLA Ops:
  0.6 12.7 %copy-start.6 = (f32[128,16]{0,1:T(8,128)S(1)}, f32[128,16]{0,1:T(8,128)}, u32[]{:S(2)}) copy-start(f32[128,16]{0,1:T(8,128)} %param.13) | copy-start | bytes 24580
  0.6 12.8 %copy-start.11 = (f32[128,16]{0,1:T(8,128)S(1)}, f32[128,16]{0,1:T(8,128)}, u32[]{:S(2)}) copy-start(f32[128,16]{0,1:T(8,128)} %param.12) | copy-start | bytes 24580
  0.7 20.2 %copy-start.4 = (s32[16]{0:T(128)S(1)}, s32[16]{0:T(128)}, u32[]{:S(2)}) copy-start(s32[16]{0:T(128)} %len_ref.15) | copy-start | bytes 196
  8.4 12.5 %collective-permute-start.2 = (bf16[16,2048]{1,0:T(8,128)(2,1)}, bf16[16,2048]{1,0:T(8,128)(2,1)S(1)}, u32[]{:S(2)}, u32[]{:S(2)}) collective-permute-start(bf16[16,2048]{1,0:T(8,128)(2,1)} %get-tuple-element.34.own_ref), channel_id=1, source_target_pairs={{0,12},{4,16},{8,20},{12,24},{16,28},{20,32},{24,36},{28,40},{32,4... | collective-permute-start | bytes 196616 | tf_op jit(solution)/shard_map/ppermute | solution.py:440
  9.9 11.0 %collective-permute-start.1 = (bf16[16,2048]{1,0:T(8,128)(2,1)}, bf16[16,2048]{1,0:T(8,128)(2,1)S(1)}, u32[]{:S(2)}, u32[]{:S(2)}) collective-permute-start(bf16[16,2048]{1,0:T(8,128)(2,1)} %get-tuple-element.34.own_ref), channel_id=1, source_target_pairs={{0,8},{4,12},{8,16},{12,20},{16,24},{20,28},{24,32},{28,36},{32,40... | collective-permute-start | bytes 196616 | tf_op jit(solution)/shard_map/ppermute | solution.py:440
  11.8 9.1 %collective-permute-start = (bf16[16,2048]{1,0:T(8,128)(2,1)}, bf16[16,2048]{1,0:T(8,128)(2,1)S(1)}, u32[]{:S(2)}, u32[]{:S(2)}) collective-permute-start(bf16[16,2048]{1,0:T(8,128)(2,1)} %get-tuple-element.34.own_ref), channel_id=1, source_target_pairs={{0,4},{4,8},{8,12},{12,16},{16,20},{20,24},{24,28},{28,32},{32,36}... | collective-permute-start | bytes 196616 | tf_op jit(solution)/shard_map/ppermute | solution.py:440
  20.9 0.9 %copy-start = (f32[16,2048]{1,0:T(8,128)S(1)}, f32[16,2048]{1,0:T(8,128)}, u32[]{:S(2)}) copy-start(f32[16,2048]{1,0:T(8,128)} %get-tuple-element.31.rate_ref) | copy-start | bytes 393220
  21.8 0.8 copy-start.2
  23.3 10.4 %collective-permute-start.4 = (bf16[16,2048]{1,0:T(8,128)(2,1)S(1)}, bf16[16,2048]{1,0:T(8,128)(2,1)S(1)}, u32[]{:S(2)}, u32[]{:S(2)}) collective-permute-start(bf16[16,2048]{1,0:T(8,128)(2,1)S(1)} %pass_on.2), channel_id=1, source_target_pairs={{0,20},{4,24},{8,28},{12,32},{16,36},{20,40},{24,44},{28,48},{32,5... | collective-permute-start | bytes 196616 | tf_op jit(solution)/shard_map/ppermute | solution.py:440
  25.4 8.3 %collective-permute-start.3 = (bf16[16,2048]{1,0:T(8,128)(2,1)S(1)}, bf16[16,2048]{1,0:T(8,128)(2,1)S(1)}, u32[]{:S(2)}, u32[]{:S(2)}) collective-permute-start(bf16[16,2048]{1,0:T(8,128)(2,1)S(1)} %pass_on.2), channel_id=1, source_target_pairs={{0,4},{4,8},{8,12},{12,16},{16,20},{20,24},{24,28},{28,32},{32,36}... | collective-permute-start | bytes 196616 | tf_op jit(solution)/shard_map/ppermute | solution.py:440
  33.7 0.6 copy-start.7
  33.7 0.6 copy-start.9
  41.2 4.5 %collective-permute-start.7 = (f32[8,512]{1,0:T(8,128)}, f32[8,512]{1,0:T(8,128)S(1)}, u32[]{:S(2)}, u32[]{:S(2)}) collective-permute-start(f32[8,512]{1,0:T(8,128)} %get-tuple-element.42.s0_ref), channel_id=1, source_target_pairs={{0,3},{1,0},{2,1},{3,2},{4,7},{5,4},{6,5},{7,6},{8,11},{9,8},{10,9... | collective-permute-start | bytes 49160 | tf_op jit(solution)/shard_map/ppermute | solution.py:440
  44.1 5.5 %collective-permute-start.6 = (f32[8,512]{1,0:T(8,128)}, f32[8,512]{1,0:T(8,128)S(1)}, u32[]{:S(2)}, u32[]{:S(2)}) collective-permute-start(f32[8,512]{1,0:T(8,128)} %get-tuple-element.42.s0_ref), channel_id=1, source_target_pairs={{0,2},{1,3},{2,0},{3,1},{4,6},{5,7},{6,4},{7,5},{8,10},{9,11},{10,... | collective-permute-start | bytes 49160 | tf_op jit(solution)/shard_map/ppermute | solution.py:440
  44.8 5.2 %collective-permute-start.5 = (f32[8,512]{1,0:T(8,128)}, f32[8,512]{1,0:T(8,128)S(1)}, u32[]{:S(2)}, u32[]{:S(2)}) collective-permute-start(f32[8,512]{1,0:T(8,128)} %get-tuple-element.42.s0_ref), channel_id=1, source_target_pairs={{0,1},{1,2},{2,3},{3,0},{4,5},{5,6},{6,7},{7,4},{8,9},{9,10},{10,1... | collective-permute-start | bytes 49160 | tf_op jit(solution)/shard_map/ppermute | solution.py:440
  45.7 4.3 %copy-start.12 = (f32[8,512]{1,0:T(8,128)}, f32[8,512]{1,0:T(8,128)S(1)}, u32[]{:S(2)}) copy-start(f32[8,512]{1,0:T(8,128)S(1)} %collective-permute-done.7.s3_ref) | copy-start | bytes 49156
  49.5 0.6 copy-start.13
  50.0 0.6 copy-start.14
  50.6 16.4 %copy-start.1 = (f32[16,2048]{1,0:T(8,128)S(1)}, f32[16,2048]{1,0:T(8,128)}, u32[]{:S(2)}) copy-start(f32[16,2048]{1,0:T(8,128)} %get-tuple-element.31.rate_ref) | copy-start | bytes 393220
  50.6 16.4 %copy-start.5 = (s32[16]{0:T(128)S(1)}, s32[16]{0:T(128)}, u32[]{:S(2)}) copy-start(s32[16]{0:T(128)} %len_ref.15) | copy-start | bytes 196
  60.3 4.7 %collective-permute-start.10 = (bf16[16,2048]{1,0:T(8,128)(2,1)}, bf16[16,2048]{1,0:T(8,128)(2,1)S(1)}, u32[]{:S(2)}, u32[]{:S(2)}) collective-permute-start(bf16[16,2048]{1,0:T(8,128)(2,1)} %get-tuple-element.48.own_ref), channel_id=1, source_target_pairs={{0,116},{4,120},{8,124},{12,0},{16,4},{20,8},{24,12},{28,16},{32,2... | collective-permute-start | bytes 196616 | tf_op jit(solution)/shard_map/ppermute | solution.py:440
  62.3 4.7 %collective-permute-start.9 = (bf16[16,2048]{1,0:T(8,128)(2,1)}, bf16[16,2048]{1,0:T(8,128)(2,1)S(1)}, u32[]{:S(2)}, u32[]{:S(2)}) collective-permute-start(bf16[16,2048]{1,0:T(8,128)(2,1)} %get-tuple-element.48.own_ref), channel_id=1, source_target_pairs={{0,120},{4,124},{8,0},{12,4},{16,8},{20,12},{24,16},{28,20},{32,24... | collective-permute-start | bytes 196616 | tf_op jit(solution)/shard_map/ppermute | solution.py:440
  63.5 3.5 %collective-permute-start.8 = (bf16[16,2048]{1,0:T(8,128)(2,1)}, bf16[16,2048]{1,0:T(8,128)(2,1)S(1)}, u32[]{:S(2)}, u32[]{:S(2)}) collective-permute-start(bf16[16,2048]{1,0:T(8,128)(2,1)} %get-tuple-element.48.own_ref), channel_id=1, source_target_pairs={{0,124},{4,0},{8,4},{12,8},{16,12},{20,16},{24,20},{28,24},{32,28}... | collective-permute-start | bytes 196616 | tf_op jit(solution)/shard_map/ppermute | solution.py:440
  67.0 0.8 copy-start.3
  68.5 11.7 %collective-permute-start.12 = (bf16[16,2048]{1,0:T(8,128)(2,1)S(1)}, bf16[16,2048]{1,0:T(8,128)(2,1)S(1)}, u32[]{:S(2)}, u32[]{:S(2)}) collective-permute-start(bf16[16,2048]{1,0:T(8,128)(2,1)S(1)} %pass_on.3), channel_id=1, source_target_pairs={{0,108},{4,112},{8,116},{12,120},{16,124},{20,0},{24,4},{28,8},{32... | collective-permute-start | bytes 196616 | tf_op jit(solution)/shard_map/ppermute | solution.py:440
  70.5 9.7 %collective-permute-start.11 = (bf16[16,2048]{1,0:T(8,128)(2,1)S(1)}, bf16[16,2048]{1,0:T(8,128)(2,1)S(1)}, u32[]{:S(2)}, u32[]{:S(2)}) collective-permute-start(bf16[16,2048]{1,0:T(8,128)(2,1)S(1)} %pass_on.3), channel_id=1, source_target_pairs={{0,124},{4,0},{8,4},{12,8},{16,12},{20,16},{24,20},{28,24},{32,28}... | collective-permute-start | bytes 196616 | tf_op jit(solution)/shard_map/ppermute | solution.py:440
  80.2 0.6 copy-start.8
  80.8 0.6 copy-start.10

commit v5 on v4

--- a/solution.py
+++ b/solution.py
@@ -19,7 +19,7 @@
 DEPTH = C + 3 * R
 EPS = 1e-6
 f32, bf16, i32 = jnp.float32, jnp.bfloat16, jnp.int32
-VLIM = 61 * 1024 * 1024
+VLIM = 56 * 1024 * 1024
 
 
 def dot(a, b):

time: 87.5 us -> 87.5 us (level)
  no operation moved by 1% of the time
where the time goes in v5:
time: 87.5 us; the launch traced here: 87.2 us
  Pallas kernels  49.6 us (57%)
  starting transfers between devices  21.7 us (25%)
  waiting for transfers between devices  7.35 us (8%)
  local copies, waits for them, and re-layouts  5.53 us (6%)
  other arithmetic  2.15 us (2%)
    ppermute x13, starting transfers between devices, ring(): return lax.ppermute(x, axis, [(i, (i + by) % size) for i in range(size)])  21.7 us
    pallas_call x2, Pallas kernels, within(): pl.pallas_call(functools.partial(local_kernel, way), grid=grid, in_specs=...  12.8 us
    pallas_call x1, Pallas kernels, local(): pl.pallas_call(functools.partial(grad_kernel, total_width), grid=grid, in...  9.7 us
    pallas_call x1, Pallas kernels, local(): pl.pallas_call(first_kernel, grid=grid, in_specs=[small, small, wide, wid...  7.75 us
    ppermute x13, waiting for transfers between devices, ring(): return lax.ppermute(x, axis, [(i, (i + by) % size) for i in range(size)])  7.35 us
    pallas_call x1, Pallas kernels, local(): pl.pallas_call(functools.partial(gate_kernel, devices), grid=grid, in_spe...  6.85 us
    pallas_call x1, Pallas kernels, local(): pl.pallas_call(functools.partial(last_kernel, devices), grid=grid, in_spe...  5.71 us
    pallas_call x1, Pallas kernels, local(): pl.pallas_call(table_kernel, grid=grid, in_specs=[tapped] * 2 + [rates_of...  5.52 us
  transfers between devices with their start and end apart: 13, of which 4 were waited for; matrix products, arithmetic and copies ran while one was open for 3% of the time, Pallas kernels for 21%

profile of v5, /device:TPU:0, one launch (start us, length us, event | category | flops | bytes accessed | tf_op | source)
XLA Modules:
  0.0 87.2 jit_solution(9806034290332451398)
XLA Ops:
  0.6 0.0 copy-start.6
  0.6 0.0 copy-start.11
  0.7 0.0 copy-start.4
  0.7 7.7 %first.1 = (bf16[8192,128]{1,0:T(8,128)(2,1)}, f32[2048,128]{1,0:T(8,128)}, bf16[16,2048]{1,0:T(8,128)(2,1)}, f32[16,2048]{1,0:T(8,128)}) custom-call(s32[1,1]{1,0:T(1,128)} %bitcast.here_ref, s32[16]{0:T(128)} %len_ref.15, bf16[512,2048]{1,0:T(8,128)(2,1)} %k_ref.3, bf16[512,2048]{1,0:T(8,128)(2,1)} %v_ref.3, f32[16,128]{1,0:T(8,128)} %bitcast.4), custom_call_target="tpu_custom_call" | custom-call | tf_op jit(solution)/shard_map/first/pallas_call | solution.py:463
  8.4 1.5 %collective-permute-start.2 = (bf16[16,2048]{1,0:T(8,128)(2,1)}, bf16[16,2048]{1,0:T(8,128)(2,1)S(1)}, u32[]{:S(2)}, u32[]{:S(2)}) collective-permute-start(bf16[16,2048]{1,0:T(8,128)(2,1)} %get-tuple-element.34.own_ref), channel_id=1, source_target_pairs={{0,12},{4,16},{8,20},{12,24},{16,28},{20,32},{24,36},{28,40},{32,4... | collective-permute-start | bytes 196616 | tf_op jit(solution)/shard_map/ppermute | solution.py:440
  9.9 1.9 %collective-permute-start.1 = (bf16[16,2048]{1,0:T(8,128)(2,1)}, bf16[16,2048]{1,0:T(8,128)(2,1)S(1)}, u32[]{:S(2)}, u32[]{:S(2)}) collective-permute-start(bf16[16,2048]{1,0:T(8,128)(2,1)} %get-tuple-element.34.own_ref), channel_id=1, source_target_pairs={{0,8},{4,12},{8,16},{12,20},{16,24},{20,28},{24,32},{28,36},{32,40... | collective-permute-start | bytes 196616 | tf_op jit(solution)/shard_map/ppermute | solution.py:440
  11.8 1.5 %collective-permute-start = (bf16[16,2048]{1,0:T(8,128)(2,1)}, bf16[16,2048]{1,0:T(8,128)(2,1)S(1)}, u32[]{:S(2)}, u32[]{:S(2)}) collective-permute-start(bf16[16,2048]{1,0:T(8,128)(2,1)} %get-tuple-element.34.own_ref), channel_id=1, source_target_pairs={{0,4},{4,8},{8,12},{12,16},{16,20},{20,24},{24,28},{28,32},{32,36}... | collective-permute-start | bytes 196616 | tf_op jit(solution)/shard_map/ppermute | solution.py:440
  13.3 0.0 copy-done.6
  13.4 0.1 copy.21
  13.5 0.0 copy-done.11
  13.5 0.1 copy.20
  13.6 0.8 multiply_reduce_fusion
  14.4 0.7 broadcast_select_fusion
  15.1 0.1 stack_reshape.7
  15.2 0.1 copy.22
  15.3 0.1 stack_reshape.6
  15.4 5.5 %tables.1 = (bf16[8192,128]{1,0:T(8,128)(2,1)}, bf16[8192,128]{1,0:T(8,128)(2,1)}) custom-call(f32[128,128]{1,0:T(8,128)} %get-tuple-element.61.tapf_ref, f32[128,128]{1,0:T(8,128)} %get-tuple-element.60.tapb_ref, f32[16,128]{1,0:T(8,128)} %bitcast.5, f32[16,128]{1,0:T(8,128)} %bitcast.8), custom_call_target="tpu_custom_call" | custom-call | flops 8388608 | bytes 12582912 | tf_op jit(solution)/shard_map/tables/pallas_call | solution.py:469
  20.9 0.0 collective-permute-done.2.refs_2_
  20.9 0.0 collective-permute-done.1.refs_1_
  20.9 0.0 collective-permute-done.refs_0_
  20.9 0.0 copy-done.4
  20.9 0.0 copy-start
  20.9 0.9 %copy-done = f32[16,2048]{1,0:T(8,128)S(1)} copy-done((f32[16,2048]{1,0:T(8,128)S(1)}, f32[16,2048]{1,0:T(8,128)}, u32[]{:S(2)}) %copy-start) | copy-done | bytes 131096
  21.8 0.8 copy-done.2
  22.7 0.7 pass_on.2
  23.3 2.1 %collective-permute-start.4 = (bf16[16,2048]{1,0:T(8,128)(2,1)S(1)}, bf16[16,2048]{1,0:T(8,128)(2,1)S(1)}, u32[]{:S(2)}, u32[]{:S(2)}) collective-permute-start(bf16[16,2048]{1,0:T(8,128)(2,1)S(1)} %pass_on.2), channel_id=1, source_target_pairs={{0,20},{4,24},{8,28},{12,32},{16,36},{20,40},{24,44},{28,48},{32,5... | collective-permute-start | bytes 196616 | tf_op jit(solution)/shard_map/ppermute | solution.py:440
  25.4 1.3 %collective-permute-start.3 = (bf16[16,2048]{1,0:T(8,128)(2,1)S(1)}, bf16[16,2048]{1,0:T(8,128)(2,1)S(1)}, u32[]{:S(2)}, u32[]{:S(2)}) collective-permute-start(bf16[16,2048]{1,0:T(8,128)(2,1)S(1)} %pass_on.2), channel_id=1, source_target_pairs={{0,4},{4,8},{8,12},{12,16},{16,20},{20,24},{24,28},{28,32},{32,36}... | collective-permute-start | bytes 196616 | tf_op jit(solution)/shard_map/ppermute | solution.py:440
  26.7 0.6 pad_maximum_fusion.flat_ref
  27.3 6.4 %local.2.y_ref = bf16[512,2048]{1,0:T(8,128)(2,1)} custom-call(s32[1,1]{1,0:T(1,128)} %bitcast.here_ref, s32[16]{0:T(128)} %len_ref.15, bf16[8192,128]{1,0:T(8,128)(2,1)} %get-tuple-element.38.z_ref, f32[2048,128]{1,0:T(8,128)} %get-tuple-element.40.ent_ref, bf16[8192,128]{1,0:T(8,128)(2,1)} %get-tuple-element.41.left_ref), custom_call_target="tpu_custom_call" | custom-call | flops 16777216 | bytes 14680064 | tf_op jit(solution)/shard_map/local/pallas_call | solution.py:456
  33.7 0.0 collective-permute-done.4.far_ref
  33.7 0.0 collective-permute-done.3.near_ref
  33.7 0.0 copy-start.9
  33.7 0.6 copy-done.7
  34.3 0.0 copy-done.9
  34.4 6.9 %gate.1 = (bf16[512,2048]{1,0:T(8,128)(2,1)}, f32[8,512]{1,0:T(8,128)}) custom-call(s32[1,1]{1,0:T(1,128)} %bitcast.here_ref, s32[16]{0:T(128)} %len_ref.15, bf16[16,2048]{1,0:T(8,128)(2,1)} %copy-done.9, bf16[16,2048]{1,0:T(8,128)(2,1)} %copy-done.7, f32[16,2048]{1,0:T(8,128)} %get-tuple-element.31.rate_ref, f32[2,2048]{1,0:T(2,128)} %pad_maximum_fusion.flat_ref, ...), custom_call_target="tpu_custom_call" | custom-call | tf_op jit(solution)/shard_map/gate/pallas_call | solution.py:477
  41.2 2.8 %collective-permute-start.7 = (f32[8,512]{1,0:T(8,128)}, f32[8,512]{1,0:T(8,128)S(1)}, u32[]{:S(2)}, u32[]{:S(2)}) collective-permute-start(f32[8,512]{1,0:T(8,128)} %get-tuple-element.42.s0_ref), channel_id=1, source_target_pairs={{0,3},{1,0},{2,1},{3,2},{4,7},{5,4},{6,5},{7,6},{8,11},{9,8},{10,9... | collective-permute-start | bytes 49160 | tf_op jit(solution)/shard_map/ppermute | solution.py:440
  44.1 0.8 collective-permute-start.6
  44.8 0.9 %collective-permute-start.5 = (f32[8,512]{1,0:T(8,128)}, f32[8,512]{1,0:T(8,128)S(1)}, u32[]{:S(2)}, u32[]{:S(2)}) collective-permute-start(f32[8,512]{1,0:T(8,128)} %get-tuple-element.42.s0_ref), channel_id=1, source_target_pairs={{0,1},{1,2},{2,3},{3,0},{4,5},{5,6},{6,7},{7,4},{8,9},{9,10},{10,1... | collective-permute-start | bytes 49160 | tf_op jit(solution)/shard_map/ppermute | solution.py:440
  45.7 0.0 collective-permute-done.7.s3_ref
  45.7 3.8 %collective-permute-done.6.s2_ref = f32[8,512]{1,0:T(8,128)S(1)} collective-permute-done((f32[8,512]{1,0:T(8,128)}, f32[8,512]{1,0:T(8,128)S(1)}, u32[]{:S(2)}, u32[]{:S(2)}) %collective-permute-start.6) | collective-permute-done | bytes 16416 | tf_op jit(solution)/shard_map/ppermute | solution.py:440
  49.5 0.5 collective-permute-done.5.s1_ref
  50.0 0.0 copy-done.12
  50.0 0.1 copy-done.13
  50.1 0.5 copy-done.14
  50.6 9.7 %grad.1 = (bf16[512,2048]{1,0:T(8,128)(2,1)}, bf16[512,2048]{1,0:T(8,128)(2,1)}, bf16[8192,128]{1,0:T(8,128)(2,1)}, f32[2048,128]{1,0:T(8,128)}, bf16[16,2048]{1,0:T(8,128)(2,1)}) custom-call(s32[1,1]{1,0:T(1,128)} %bitcast.here_ref, s32[16]{0:T(128)} %len_ref.15, f32[8,512]{1,0:T(8,128)} %get-tuple-element.42.s0_ref, f32[8,512]{1,0:T(8,128)} %copy-done.14, ...), custom_call_target="tpu_custom_call" | custom-call | tf_op jit(solution)/shard_map/grad/pallas_call | solution.py:483
  60.3 2.0 %collective-permute-start.10 = (bf16[16,2048]{1,0:T(8,128)(2,1)}, bf16[16,2048]{1,0:T(8,128)(2,1)S(1)}, u32[]{:S(2)}, u32[]{:S(2)}) collective-permute-start(bf16[16,2048]{1,0:T(8,128)(2,1)} %get-tuple-element.48.own_ref), channel_id=1, source_target_pairs={{0,116},{4,120},{8,124},{12,0},{16,4},{20,8},{24,12},{28,16},{32,2... | collective-permute-start | bytes 196616 | tf_op jit(solution)/shard_map/ppermute | solution.py:440
  62.3 1.2 %collective-permute-start.9 = (bf16[16,2048]{1,0:T(8,128)(2,1)}, bf16[16,2048]{1,0:T(8,128)(2,1)S(1)}, u32[]{:S(2)}, u32[]{:S(2)}) collective-permute-start(bf16[16,2048]{1,0:T(8,128)(2,1)} %get-tuple-element.48.own_ref), channel_id=1, source_target_pairs={{0,120},{4,124},{8,0},{12,4},{16,8},{20,12},{24,16},{28,20},{32,24... | collective-permute-start | bytes 196616 | tf_op jit(solution)/shard_map/ppermute | solution.py:440
  63.5 0.4 collective-permute-start.8
  63.9 1.1 %collective-permute-done.10.refs_2_ = bf16[16,2048]{1,0:T(8,128)(2,1)S(1)} collective-permute-done((bf16[16,2048]{1,0:T(8,128)(2,1)}, bf16[16,2048]{1,0:T(8,128)(2,1)S(1)}, u32[]{:S(2)}, u32[]{:S(2)}) %collective-permute-start.10) | collective-permute-done | bytes 65568 | tf_op jit(solution)/shard_map/ppermute | solution.py:440
  65.0 2.0 %collective-permute-done.9.refs_1_ = bf16[16,2048]{1,0:T(8,128)(2,1)S(1)} collective-permute-done((bf16[16,2048]{1,0:T(8,128)(2,1)}, bf16[16,2048]{1,0:T(8,128)(2,1)S(1)}, u32[]{:S(2)}, u32[]{:S(2)}) %collective-permute-start.9) | collective-permute-done | bytes 65568 | tf_op jit(solution)/shard_map/ppermute | solution.py:440
  67.0 0.0 collective-permute-done.8.refs_0_
  67.0 0.0 copy-done.1
  67.0 0.0 copy-done.5
  67.0 0.0 copy-start.3
  67.0 0.8 copy-done.3
  67.8 0.7 pass_on.3
  68.5 2.1 %collective-permute-start.12 = (bf16[16,2048]{1,0:T(8,128)(2,1)S(1)}, bf16[16,2048]{1,0:T(8,128)(2,1)S(1)}, u32[]{:S(2)}, u32[]{:S(2)}) collective-permute-start(bf16[16,2048]{1,0:T(8,128)(2,1)S(1)} %pass_on.3), channel_id=1, source_target_pairs={{0,108},{4,112},{8,116},{12,120},{16,124},{20,0},{24,4},{28,8},{32... | collective-permute-start | bytes 196616 | tf_op jit(solution)/shard_map/ppermute | solution.py:440
  70.5 3.2 %collective-permute-start.11 = (bf16[16,2048]{1,0:T(8,128)(2,1)S(1)}, bf16[16,2048]{1,0:T(8,128)(2,1)S(1)}, u32[]{:S(2)}, u32[]{:S(2)}) collective-permute-start(bf16[16,2048]{1,0:T(8,128)(2,1)S(1)} %pass_on.3), channel_id=1, source_target_pairs={{0,124},{4,0},{8,4},{12,8},{16,12},{20,16},{24,20},{28,24},{32,28}... | collective-permute-start | bytes 196616 | tf_op jit(solution)/shard_map/ppermute | solution.py:440
  73.8 6.4 %local.3.y_ref = bf16[512,2048]{1,0:T(8,128)(2,1)} custom-call(s32[1,1]{1,0:T(1,128)} %bitcast.here_ref, s32[16]{0:T(128)} %len_ref.15, bf16[8192,128]{1,0:T(8,128)(2,1)} %get-tuple-element.52.z_ref, f32[2048,128]{1,0:T(8,128)} %get-tuple-element.54.ent_ref, bf16[8192,128]{1,0:T(8,128)(2,1)} %get-tuple-element.55.left_ref), custom_call_target="tpu_custom_call" | custom-call | flops 16777216 | bytes 14680064 | tf_op jit(solution)/shard_map/local/pallas_call | solution.py:456
  80.2 0.0 collective-permute-done.12.far_ref
  80.2 0.0 collective-permute-done.11.near_ref
  80.2 0.6 copy-done.8
  80.8 0.6 copy-done.10
  81.5 5.7 %last.1 = (bf16[512,2048]{1,0:T(8,128)(2,1)}, bf16[512,2048]{1,0:T(8,128)(2,1)}) custom-call(s32[1,1]{1,0:T(1,128)} %bitcast.here_ref, s32[16]{0:T(128)} %len_ref.15, bf16[16,2048]{1,0:T(8,128)(2,1)} %copy-done.10, bf16[16,2048]{1,0:T(8,128)(2,1)} %copy-done.8, f32[16,2048]{1,0:T(8,128)} %get-tuple-element.31.rate_ref, f32[2,2048]{1,0:T(2,128)} %pad_maximum_fusion.flat_ref, ...), custom_call_target="tpu_custom_call" | custom-call | tf_op jit(solution)/shard_map/last/pallas_call | solution.py:495
  (14 shorter events, 0.1 us)
Async XLA Ops:
  0.6 12.7 %copy-start.6 = (f32[128,16]{0,1:T(8,128)S(1)}, f32[128,16]{0,1:T(8,128)}, u32[]{:S(2)}) copy-start(f32[128,16]{0,1:T(8,128)} %param.13) | copy-start | bytes 24580
  0.6 12.8 %copy-start.11 = (f32[128,16]{0,1:T(8,128)S(1)}, f32[128,16]{0,1:T(8,128)}, u32[]{:S(2)}) copy-start(f32[128,16]{0,1:T(8,128)} %param.12) | copy-start | bytes 24580
  0.7 20.2 %copy-start.4 = (s32[16]{0:T(128)S(1)}, s32[16]{0:T(128)}, u32[]{:S(2)}) copy-start(s32[16]{0:T(128)} %len_ref.15) | copy-start | bytes 196
  8.4 12.5 %collective-permute-start.2 = (bf16[16,2048]{1,0:T(8,128)(2,1)}, bf16[16,2048]{1,0:T(8,128)(2,1)S(1)}, u32[]{:S(2)}, u32[]{:S(2)}) collective-permute-start(bf16[16,2048]{1,0:T(8,128)(2,1)} %get-tuple-element.34.own_ref), channel_id=1, source_target_pairs={{0,12},{4,16},{8,20},{12,24},{16,28},{20,32},{24,36},{28,40},{32,4... | collective-permute-start | bytes 196616 | tf_op jit(solution)/shard_map/ppermute | solution.py:440
  9.9 11.0 %collective-permute-start.1 = (bf16[16,2048]{1,0:T(8,128)(2,1)}, bf16[16,2048]{1,0:T(8,128)(2,1)S(1)}, u32[]{:S(2)}, u32[]{:S(2)}) collective-permute-start(bf16[16,2048]{1,0:T(8,128)(2,1)} %get-tuple-element.34.own_ref), channel_id=1, source_target_pairs={{0,8},{4,12},{8,16},{12,20},{16,24},{20,28},{24,32},{28,36},{32,40... | collective-permute-start | bytes 196616 | tf_op jit(solution)/shard_map/ppermute | solution.py:440
  11.8 9.1 %collective-permute-start = (bf16[16,2048]{1,0:T(8,128)(2,1)}, bf16[16,2048]{1,0:T(8,128)(2,1)S(1)}, u32[]{:S(2)}, u32[]{:S(2)}) collective-permute-start(bf16[16,2048]{1,0:T(8,128)(2,1)} %get-tuple-element.34.own_ref), channel_id=1, source_target_pairs={{0,4},{4,8},{8,12},{12,16},{16,20},{20,24},{24,28},{28,32},{32,36}... | collective-permute-start | bytes 196616 | tf_op jit(solution)/shard_map/ppermute | solution.py:440
  20.9 0.9 %copy-start = (f32[16,2048]{1,0:T(8,128)S(1)}, f32[16,2048]{1,0:T(8,128)}, u32[]{:S(2)}) copy-start(f32[16,2048]{1,0:T(8,128)} %get-tuple-element.31.rate_ref) | copy-start | bytes 393220
  21.8 0.8 copy-start.2
  23.3 10.4 %collective-permute-start.4 = (bf16[16,2048]{1,0:T(8,128)(2,1)S(1)}, bf16[16,2048]{1,0:T(8,128)(2,1)S(1)}, u32[]{:S(2)}, u32[]{:S(2)}) collective-permute-start(bf16[16,2048]{1,0:T(8,128)(2,1)S(1)} %pass_on.2), channel_id=1, source_target_pairs={{0,20},{4,24},{8,28},{12,32},{16,36},{20,40},{24,44},{28,48},{32,5... | collective-permute-start | bytes 196616 | tf_op jit(solution)/shard_map/ppermute | solution.py:440
  25.4 8.3 %collective-permute-start.3 = (bf16[16,2048]{1,0:T(8,128)(2,1)S(1)}, bf16[16,2048]{1,0:T(8,128)(2,1)S(1)}, u32[]{:S(2)}, u32[]{:S(2)}) collective-permute-start(bf16[16,2048]{1,0:T(8,128)(2,1)S(1)} %pass_on.2), channel_id=1, source_target_pairs={{0,4},{4,8},{8,12},{12,16},{16,20},{20,24},{24,28},{28,32},{32,36}... | collective-permute-start | bytes 196616 | tf_op jit(solution)/shard_map/ppermute | solution.py:440
  33.7 0.6 copy-start.7
  33.7 0.6 copy-start.9
  41.2 4.5 %collective-permute-start.7 = (f32[8,512]{1,0:T(8,128)}, f32[8,512]{1,0:T(8,128)S(1)}, u32[]{:S(2)}, u32[]{:S(2)}) collective-permute-start(f32[8,512]{1,0:T(8,128)} %get-tuple-element.42.s0_ref), channel_id=1, source_target_pairs={{0,3},{1,0},{2,1},{3,2},{4,7},{5,4},{6,5},{7,6},{8,11},{9,8},{10,9... | collective-permute-start | bytes 49160 | tf_op jit(solution)/shard_map/ppermute | solution.py:440
  44.1 5.5 %collective-permute-start.6 = (f32[8,512]{1,0:T(8,128)}, f32[8,512]{1,0:T(8,128)S(1)}, u32[]{:S(2)}, u32[]{:S(2)}) collective-permute-start(f32[8,512]{1,0:T(8,128)} %get-tuple-element.42.s0_ref), channel_id=1, source_target_pairs={{0,2},{1,3},{2,0},{3,1},{4,6},{5,7},{6,4},{7,5},{8,10},{9,11},{10,... | collective-permute-start | bytes 49160 | tf_op jit(solution)/shard_map/ppermute | solution.py:440
  44.8 5.2 %collective-permute-start.5 = (f32[8,512]{1,0:T(8,128)}, f32[8,512]{1,0:T(8,128)S(1)}, u32[]{:S(2)}, u32[]{:S(2)}) collective-permute-start(f32[8,512]{1,0:T(8,128)} %get-tuple-element.42.s0_ref), channel_id=1, source_target_pairs={{0,1},{1,2},{2,3},{3,0},{4,5},{5,6},{6,7},{7,4},{8,9},{9,10},{10,1... | collective-permute-start | bytes 49160 | tf_op jit(solution)/shard_map/ppermute | solution.py:440
  45.7 4.3 %copy-start.12 = (f32[8,512]{1,0:T(8,128)}, f32[8,512]{1,0:T(8,128)S(1)}, u32[]{:S(2)}) copy-start(f32[8,512]{1,0:T(8,128)S(1)} %collective-permute-done.7.s3_ref) | copy-start | bytes 49156
  49.5 0.6 copy-start.13
  50.0 0.6 copy-start.14
  50.6 16.4 %copy-start.1 = (f32[16,2048]{1,0:T(8,128)S(1)}, f32[16,2048]{1,0:T(8,128)}, u32[]{:S(2)}) copy-start(f32[16,2048]{1,0:T(8,128)} %get-tuple-element.31.rate_ref) | copy-start | bytes 393220
  50.6 16.4 %copy-start.5 = (s32[16]{0:T(128)S(1)}, s32[16]{0:T(128)}, u32[]{:S(2)}) copy-start(s32[16]{0:T(128)} %len_ref.15) | copy-start | bytes 196
  60.3 4.7 %collective-permute-start.10 = (bf16[16,2048]{1,0:T(8,128)(2,1)}, bf16[16,2048]{1,0:T(8,128)(2,1)S(1)}, u32[]{:S(2)}, u32[]{:S(2)}) collective-permute-start(bf16[16,2048]{1,0:T(8,128)(2,1)} %get-tuple-element.48.own_ref), channel_id=1, source_target_pairs={{0,116},{4,120},{8,124},{12,0},{16,4},{20,8},{24,12},{28,16},{32,2... | collective-permute-start | bytes 196616 | tf_op jit(solution)/shard_map/ppermute | solution.py:440
  62.3 4.7 %collective-permute-start.9 = (bf16[16,2048]{1,0:T(8,128)(2,1)}, bf16[16,2048]{1,0:T(8,128)(2,1)S(1)}, u32[]{:S(2)}, u32[]{:S(2)}) collective-permute-start(bf16[16,2048]{1,0:T(8,128)(2,1)} %get-tuple-element.48.own_ref), channel_id=1, source_target_pairs={{0,120},{4,124},{8,0},{12,4},{16,8},{20,12},{24,16},{28,20},{32,24... | collective-permute-start | bytes 196616 | tf_op jit(solution)/shard_map/ppermute | solution.py:440
  63.5 3.5 %collective-permute-start.8 = (bf16[16,2048]{1,0:T(8,128)(2,1)}, bf16[16,2048]{1,0:T(8,128)(2,1)S(1)}, u32[]{:S(2)}, u32[]{:S(2)}) collective-permute-start(bf16[16,2048]{1,0:T(8,128)(2,1)} %get-tuple-element.48.own_ref), channel_id=1, source_target_pairs={{0,124},{4,0},{8,4},{12,8},{16,12},{20,16},{24,20},{28,24},{32,28}... | collective-permute-start | bytes 196616 | tf_op jit(solution)/shard_map/ppermute | solution.py:440
  67.0 0.8 copy-start.3
  68.5 11.7 %collective-permute-start.12 = (bf16[16,2048]{1,0:T(8,128)(2,1)S(1)}, bf16[16,2048]{1,0:T(8,128)(2,1)S(1)}, u32[]{:S(2)}, u32[]{:S(2)}) collective-permute-start(bf16[16,2048]{1,0:T(8,128)(2,1)S(1)} %pass_on.3), channel_id=1, source_target_pairs={{0,108},{4,112},{8,116},{12,120},{16,124},{20,0},{24,4},{28,8},{32... | collective-permute-start | bytes 196616 | tf_op jit(solution)/shard_map/ppermute | solution.py:440
  70.5 9.7 %collective-permute-start.11 = (bf16[16,2048]{1,0:T(8,128)(2,1)S(1)}, bf16[16,2048]{1,0:T(8,128)(2,1)S(1)}, u32[]{:S(2)}, u32[]{:S(2)}) collective-permute-start(bf16[16,2048]{1,0:T(8,128)(2,1)S(1)} %pass_on.3), channel_id=1, source_target_pairs={{0,124},{4,0},{8,4},{12,8},{16,12},{20,16},{24,20},{28,24},{32,28}... | collective-permute-start | bytes 196616 | tf_op jit(solution)/shard_map/ppermute | solution.py:440
  80.2 0.6 copy-start.8
  80.8 0.6 copy-start.10
